TPU v7x, 256 devices: a whole 4x4x8 slice. The times are simulated.
256 devices in a mesh: sub: 32 (over y, z), nar: 8 (over x, core).
Axes of the slice: x: 4, y: 4, z: 8, core: 2. Of those that a mesh axis runs over, the one named last changes fastest.
Arguments:
- residual: float32 [32, 32, 2048], P(None, 'sub', 'nar')
- iterate: float32 [32, 32, 2048], P(None, 'sub', 'nar'), may hold values from -6 to 6
- stiffness: float32 [32, 2048, 3072], P('sub', 'nar')
- local_inverse: float32 [32, 2048, 3072], P('sub', 'nar')
- eigvecs: float32 [32, 96, 2048], P('sub', None, 'nar'), may hold values from -0.125 to 0.125
- ev_count: int32 [32], P('sub'), may hold values from 16 to 96
- coarse_inverse: float32 [3072, 3072], P('sub', 'nar'), may hold values from -0.109375 to 0.109375
- send_rows: int32 [2, 32, 512], P(None, 'sub', 'nar'), may hold values from 0 to 255, as said below
Outputs:
- next_vector: float32 [32, 32, 2048], P(None, 'sub', 'nar')
- new_iterate: float32 [32, 32, 2048], P(None, 'sub', 'nar')
- hessenberg: float32 [3, 32], replicated
Inputs may be any that keep to these rules, and one draw needn't show every extreme that they name: `send_rows`: each device's list of 64 rows holds distinct rows of its own block of 256.
All inputs are finite; a program needn't handle non-finite values.
Results may differ from a plain program's by a relative error of at most 0.00015.
Values sent between devices are 32-bit elements; how exact they have to be, the bound alone decides.
No kernel may reach another device: no remote copies, remote signals or barrier semaphores. Data moves between devices by JAX's collectives and lax.ppermute only.
A program may use at most 64 MiB of HBM per device.

v0:
```python
import jax
import jax.numpy as jnp
from jax import lax
from jax.sharding import PartitionSpec as P

EPS = 1e-06


def from_behind(block, axis, distance):
    devices = range(lax.axis_size(axis))
    route = [(i - distance, i) for i in devices if i - distance in devices]
    return lax.ppermute(block, axis, route)


def extend(field, send_rows):
    toward_right = field[:, 0, send_rows[0, 0]][:, None, :]
    toward_left = field[:, 0, send_rows[1, 0]][:, None, :]
    from_left = from_behind(toward_right, "sub", 1)
    from_right = from_behind(toward_left, "sub", -1)
    own, lefts, rights = (
        lax.all_gather(field, "nar", axis=2, tiled=True),
        lax.all_gather(from_left, "nar", axis=2, tiled=True),
        lax.all_gather(from_right, "nar", axis=2, tiled=True),
    )
    return jnp.concatenate([own, lefts, rights], axis=2)


def precondition(field, local_inverse, eigvecs, ev_count, coarse_inverse, send_rows):
    local = jnp.einsum(
        "sre,kse->ksr", local_inverse, extend(field, send_rows), precision=lax.Precision.HIGHEST
    )
    maxev = eigvecs.shape[1]
    live = jnp.arange(maxev)[None, :] < ev_count[:, None]
    partial_res = jnp.einsum("sjr,ksr->ksj", eigvecs, field, precision=lax.Precision.HIGHEST)
    partial_res = jnp.where(live[None], partial_res, 0.0)
    count = field.shape[0]
    width = coarse_inverse.shape[1]
    summed = lax.psum(partial_res, "nar")
    whole = lax.all_gather(summed, "sub", axis=1, tiled=True)
    flat = whole.reshape(count, -1)
    piece = lax.dynamic_slice_in_dim(flat, lax.axis_index("nar") * width, width, 1)
    partial_sol = jnp.einsum("jc,kc->kj", coarse_inverse, piece, precision=lax.Precision.HIGHEST)
    coarse_sol = lax.psum(partial_sol, "nar")
    coarse_sol = jnp.where(live, coarse_sol, 0.0)
    correction = jnp.einsum("jr,kj->kr", eigvecs[0], coarse_sol, precision=lax.Precision.HIGHEST)
    return local + correction[:, None, :]


def local_inner(first, second, total):
    return jnp.sum(first * second, axis=(1, 2)) / total


def per_device(
    residual, iterate, stiffness, local_inverse, eigvecs, ev_count, coarse_inverse, send_rows
):
    total = lax.axis_size("sub") * lax.axis_size("nar") * residual.shape[2]
    beta = jnp.sqrt(lax.psum(local_inner(residual, residual, total), ("sub", "nar")) + EPS)
    start = residual / beta[:, None, None]
    precond = precondition(start, local_inverse, eigvecs, ev_count, coarse_inverse, send_rows)
    image = jnp.einsum(
        "sre,kse->ksr", stiffness, extend(precond, send_rows), precision=lax.Precision.HIGHEST
    )
    h00 = lax.psum(local_inner(start, image, total), ("sub", "nar"))
    remainder = image - h00[:, None, None] * start
    h10 = jnp.sqrt(lax.psum(local_inner(remainder, remainder, total), ("sub", "nar")) + EPS)
    next_vector = remainder / h10[:, None, None]
    factor = beta * h00 / (h00 * h00 + h10 * h10)
    new_iterate = iterate + factor[:, None, None] * precond
    return (next_vector, new_iterate, jnp.stack([beta, h00, h10]))


def solution(mesh):
    return jax.shard_map(
        per_device,
        mesh=mesh,
        in_specs=(
            P(None, "sub", "nar"),
            P(None, "sub", "nar"),
            P("sub", "nar", None),
            P("sub", "nar", None),
            P("sub", None, "nar"),
            P("sub"),
            P("sub", "nar"),
            P(None, "sub", "nar"),
        ),
        out_specs=(P(None, "sub", "nar"), P(None, "sub", "nar"), P()),
        check_vma=False,
    )
```

profile of v0, /device:TPU:1, one launch (start us, length us, event | category | flops | bytes accessed | tf_op | source)
XLA Modules:
  0.0 449.7 jit_solution(5919070150237011123)
XLA Ops:
  0.6 0.0 copy-start
  0.6 0.0 copy-start.2
  0.7 1.3 multiply_reduce_fusion.2
  1.9 81.4 %psum.35 = f32[32]{0:T(128)S(1)} all-reduce(f32[32]{0:T(128)S(1)} %broadcast_multiply_fusion.2), channel_id=1, replica_groups=mesh['sub'=32,'nar'=8] {'sub','nar'}, use_global_device_ids=true, to_apply=%region_1.0 | all-reduce | flops 32 | bytes 256 | tf_op jit(solution)/shard_map/psum | solution.py:57
  83.3 0.8 copy_divide_fusion
  84.2 0.1 copy.37
  84.3 0.7 fusion.30
  85.0 0.8 gather_fusion
  85.7 2.6 collective-permute-start
  88.3 1.4 gather_fusion.1
  89.7 1.3 collective-permute-start.1
  91.7 1.1 fusion.10
  92.8 21.1 %psum.36 = f32[32,1,96]{2,0,1:T(8,128)S(1)} all-reduce(f32[32,1,96]{2,0,1:T(8,128)S(1)} %fusion.10), channel_id=1, replica_groups=mesh['sub'=32,'nar'=8] {'nar'}, use_global_device_ids=true, to_apply=%region_2.3 | all-reduce | flops 3072 | bytes 24576 | tf_op jit(solution)/shard_map/psum | solution.py:38
  113.9 38.4 %all_gather.24 = f32[32,32,96]{2,0,1:T(8,128)S(1)} all-gather(f32[32,1,96]{2,0,1:T(8,128)S(1)} %psum.36), channel_id=1, replica_groups=mesh['sub'=32,'nar'=8] {'sub'}, dimensions={1}, use_global_device_ids=true | all-gather | bytes 405504 | tf_op jit(solution)/shard_map/all_gather | solution.py:39
  152.3 1.1 copy.43
  153.4 2.1 reshape.122
  155.5 1.2 fusion.22
  156.7 35.7 %psum.37 = f32[32,96]{1,0:T(8,128)S(1)} all-reduce(f32[32,96]{1,0:T(8,128)S(1)} %fusion.22), channel_id=1, replica_groups=mesh['sub'=32,'nar'=8] {'nar'}, use_global_device_ids=true, to_apply=%region_3.4 | all-reduce | flops 3072 | bytes 24576 | tf_op jit(solution)/shard_map/psum | solution.py:43
  192.4 0.0 copy-done.2
  192.4 0.8 fusion.19
  193.2 16.2 %all_gather.21 = f32[32,1,2048]{2,0,1:T(8,128)S(1)} all-gather(f32[32,1,256]{2,0,1:T(8,128)S(1)} %copy_divide_fusion), channel_id=1, replica_groups=mesh['sub'=32,'nar'=8] {'nar'}, dimensions={2}, use_global_device_ids=true | all-gather | bytes 294912 | tf_op jit(solution)/shard_map/all_gather | solution.py:21
  209.4 0.0 collective-permute-done
  209.4 13.9 %all_gather.22 = f32[32,1,512]{0,1,2:T(1,128)} all-gather(f32[32,1,64]{0,1,2:T(1,128)S(1)} %bitcast.71), channel_id=1, replica_groups=mesh['sub'=32,'nar'=8] {'nar'}, dimensions={2}, use_global_device_ids=true | all-gather | bytes 73728 | tf_op jit(solution)/shard_map/all_gather | solution.py:22
  223.3 1.0 copy.41
  224.4 0.0 collective-permute-done.1
  224.4 13.9 %all_gather.23 = f32[32,1,512]{0,1,2:T(1,128)} all-gather(f32[32,1,64]{0,1,2:T(1,128)S(1)} %bitcast.70), channel_id=1, replica_groups=mesh['sub'=32,'nar'=8] {'nar'}, dimensions={2}, use_global_device_ids=true | all-gather | bytes 73728 | tf_op jit(solution)/shard_map/all_gather | solution.py:23
  238.3 1.7 copy.42
  240.0 4.7 %fusion.4 = f32[32,256]{1,0:T(8,128)S(1)} fusion(f32[32,256]{1,0:T(8,128)} %fusion.19, f32[1,256,3072]{2,1,0:T(8,128)} %param.11, f32[32,1,512]{2,0,1:T(8,128)} %copy.42, f32[32,1,512]{2,0,1:T(8,128)S(1)} %copy.41, f32[32,1,2048]{2,0,1:T(8,128)S(1)} %all_gather.21), kind=kOutput, calls=%fused_computation.8 | convolution fusion | flops 302194688 | bytes 3604480 | tf_op jit(solution)/shard_map/sre,kse->ksr/dot_general | solution.py:29
  244.7 0.0 copy-start.1
  244.7 0.0 copy-start.3
  244.7 0.1 copy.44
  244.8 0.8 gather_fusion.2
  245.6 1.5 collective-permute-start.2
  247.2 14.3 %all-gather = f32[32,2048]{1,0:T(8,128)} all-gather(f32[32,256]{1,0:T(8,128)S(1)} %fusion.4), channel_id=2, replica_groups=mesh['sub'=32,'nar'=8] {'nar'}, dimensions={1}, use_global_device_ids=true | all-gather | bytes 294912 | tf_op jit(solution)/shard_map/all_gather | solution.py:21
  261.5 1.4 gather_fusion.3
  262.8 1.3 collective-permute-start.3
  264.1 0.0 collective-permute-done.2
  264.1 0.0 copy-start.4
  264.2 0.6 copy-done.4
  264.8 13.0 %all_gather.26 = f32[32,1,512]{0,1,2:T(1,128)S(1)} all-gather(f32[32,1,64]{0,1,2:T(1,128)} %bitcast.72), channel_id=1, replica_groups=mesh['sub'=32,'nar'=8] {'nar'}, dimensions={2}, use_global_device_ids=true | all-gather | bytes 73728 | tf_op jit(solution)/shard_map/all_gather | solution.py:22
  277.8 0.7 copy.48
  278.5 0.0 collective-permute-done.3
  278.5 13.2 %all_gather.27 = f32[32,1,512]{0,1,2:T(1,128)S(1)} all-gather(f32[32,1,64]{0,1,2:T(1,128)} %bitcast.23), channel_id=1, replica_groups=mesh['sub'=32,'nar'=8] {'nar'}, dimensions={2}, use_global_device_ids=true | all-gather | bytes 73728 | tf_op jit(solution)/shard_map/all_gather | solution.py:23
  291.7 0.7 copy.49
  292.5 0.0 copy-done
  292.5 4.0 multiply_reduce_fusion.1
  296.5 77.5 %psum.38 = f32[32]{0:T(128)S(1)} all-reduce(f32[32]{0:T(128)S(1)} %broadcast_multiply_fusion.1), channel_id=1, replica_groups=mesh['sub'=32,'nar'=8] {'sub','nar'}, use_global_device_ids=true, to_apply=%region_5.6 | all-reduce | flops 32 | bytes 256 | tf_op jit(solution)/shard_map/psum | solution.py:63
  374.0 0.0 copy-done.1
  374.0 0.2 multiply_reduce_fusion
  374.2 73.6 %psum.39 = f32[32]{0:T(128)S(1)} all-reduce(f32[32]{0:T(128)S(1)} %broadcast_multiply_fusion), channel_id=1, replica_groups=mesh['sub'=32,'nar'=8] {'sub','nar'}, use_global_device_ids=true, to_apply=%region_7.8 | all-reduce | flops 32 | bytes 256 | tf_op jit(solution)/shard_map/psum | solution.py:65
  447.8 0.0 copy-done.3
  447.8 0.1 bitcast_add_fusion
  447.9 0.6 copy.51
  448.5 0.6 copy.52
  449.2 0.6 pad_maximum_fusion
  (6 shorter events, 0.0 us)
Async XLA Ops:
  0.6 291.9 %copy-start = (f32[1,256,3072]{2,1,0:T(8,128)S(1)}, f32[1,256,3072]{2,1,0:T(8,128)}, u32[]{:S(2)}) copy-start(f32[1,256,3072]{2,1,0:T(8,128)} %param.10) | copy-start | bytes 9437188
  0.6 191.8 %copy-start.2 = (f32[1,96,256]{2,1,0:T(8,128)S(1)}, f32[1,96,256]{2,1,0:T(8,128)}, u32[]{:S(2)}) copy-start(f32[1,96,256]{2,1,0:T(8,128)} %param.12) | copy-start | bytes 294916
  85.7 123.7 %collective-permute-start = (f32[32,1,64]{0,2,1:T(8,128)S(1)}, f32[32,1,64]{0,2,1:T(8,128)S(1)}, u32[]{:S(2)}, u32[]{:S(2)}) collective-permute-start(f32[32,1,64]{0,2,1:T(8,128)S(1)} %bitcast.74), channel_id=1, source_target_pairs={{0,8},{8,16},{16,24},{24,32},{32,40},{40,48},{48,56},{56,64},{64,7... | collective-permute-start | bytes 24584 | tf_op jit(solution)/shard_map/ppermute | solution.py:12
  89.7 134.6 %collective-permute-start.1 = (f32[32,1,64]{0,2,1:T(8,128)}, f32[32,1,64]{0,2,1:T(8,128)S(1)}, u32[]{:S(2)}, u32[]{:S(2)}) collective-permute-start(f32[32,1,64]{0,2,1:T(8,128)} %bitcast.8), channel_id=1, source_target_pairs={{8,0},{16,8},{24,16},{32,24},{40,32},{48,40},{56,48},{64,56},{72,6... | collective-permute-start | bytes 24584 | tf_op jit(solution)/shard_map/ppermute | solution.py:12
  244.7 129.3 %copy-start.1 = (f32[32,1,256]{2,1,0:T(1,128)S(1)}, f32[32,1,256]{2,1,0:T(1,128)}, u32[]{:S(2)}) copy-start(f32[32,1,256]{2,1,0:T(1,128)} %param.8) | copy-start | bytes 98308
  244.7 203.0 %copy-start.3 = (f32[32,1,256]{2,1,0:T(1,128)S(1)}, f32[32,1,256]{2,1,0:T(1,128)}, u32[]{:S(2)}) copy-start(f32[32,1,256]{2,1,0:T(1,128)} %param.9) | copy-start | bytes 98308
  245.6 18.5 %collective-permute-start.2 = (f32[32,1,64]{0,2,1:T(8,128)S(1)}, f32[32,1,64]{0,2,1:T(8,128)S(1)}, u32[]{:S(2)}, u32[]{:S(2)}) collective-permute-start(f32[32,1,64]{0,2,1:T(8,128)S(1)} %bitcast.75), channel_id=1, source_target_pairs={{0,8},{8,16},{16,24},{24,32},{32,40},{40,48},{48,56},{56,64},{64,7... | collective-permute-start | bytes 24584 | tf_op jit(solution)/shard_map/ppermute | solution.py:12
  262.8 15.7 %collective-permute-start.3 = (f32[32,1,64]{0,2,1:T(8,128)}, f32[32,1,64]{0,2,1:T(8,128)}, u32[]{:S(2)}, u32[]{:S(2)}) collective-permute-start(f32[32,1,64]{0,2,1:T(8,128)} %bitcast.22), channel_id=1, source_target_pairs={{8,0},{16,8},{24,16},{32,24},{40,32},{48,40},{56,48},{64,56},{72,6... | collective-permute-start | bytes 24584 | tf_op jit(solution)/shard_map/ppermute | solution.py:12
  264.1 0.6 copy-start.4
where the time goes:
time: 451 us; the launch traced here: 450 us
  blocking collectives  412 us (91%)
  local copies, waits for them, and re-layouts  13.8 us (3%)
  matrix products  11.8 us (3%)
  starting transfers between devices  6.71 us (1%)
    psum x1, blocking collectives, per_device(): lax.psum(local_inner(residual, residual, total), ('sub', 'nar')) + EPS  81.4 us
    psum x1, blocking collectives, per_device(): h00 = lax.psum(local_inner(start, image, total), ('sub', 'nar'))  77.5 us
    psum x1, blocking collectives, per_device(): lax.psum(local_inner(remainder, remainder, total), ('sub', 'nar')) + EPS  73.6 us
    all_gather x1, blocking collectives, precondition(): whole = lax.all_gather(summed, 'sub', axis=1, tiled=True)  38.4 us
    psum x1, blocking collectives, precondition(): coarse_sol = lax.psum(partial_sol, 'nar')  35.7 us
    all_gather x2, blocking collectives, extend(): lax.all_gather(field, 'nar', axis=2, tiled=True)  30.5 us
    all_gather x2, blocking collectives, extend(): lax.all_gather(from_right, 'nar', axis=2, tiled=True)  27.1 us
    all_gather x2, blocking collectives, extend(): lax.all_gather(from_left, 'nar', axis=2, tiled=True)  26.9 us
  transfers between devices with their start and end apart: 4, of which 0 were waited for; matrix products, arithmetic and copies ran while one was open for 2% of the time, Pallas kernels for 0%

commit v1 on v0

v1 whole, which is shorter than its diff:
```python
import jax
import jax.numpy as jnp
from jax import lax
from jax.sharding import PartitionSpec as P

EPS = 1e-06
HIGH = lax.Precision.HIGH
HIGHEST = lax.Precision.HIGHEST


def spread(block, axes, count):
    copies = jnp.broadcast_to(block[None], (count,) + block.shape)
    return lax.all_to_all(copies, axes, 0, 0)


def pair_routes(nsub):
    odd = [(i, i ^ 1) for i in range(nsub)]
    even = [(i, (i + 1 if i % 2 else i - 1) % nsub) for i in range(nsub)]
    return odd, even


def beside(first, second, nsub):
    sub = lax.axis_index("sub")
    route_a, route_b = pair_routes(nsub)
    got_a = lax.ppermute(first, "sub", route_a)
    got_b = lax.ppermute(second, "sub", route_b)
    even = sub % 2 == 0
    lefts = jnp.where(sub == 0, 0.0, jnp.where(even, got_b, got_a))
    rights = jnp.where(sub == nsub - 1, 0.0, jnp.where(even, got_a, got_b))
    return jnp.concatenate([lefts, rights], axis=1)


def in_rows(blocks):
    return jnp.swapaxes(blocks, 0, 1).reshape(blocks.shape[1], -1)


def times(field, matrix, precision=HIGH):
    return lax.dot_general(field, matrix, (((1,), (1,)), ((), ())), precision=precision)


def per_device(
    residual, iterate, stiffness, local_inverse, eigvecs, ev_count, coarse_inverse, send_rows
):
    nsub, nnar = lax.axis_size("sub"), lax.axis_size("nar")
    count, _, rdev = residual.shape
    total = nsub * nnar * rdev
    over = send_rows.shape[2]
    maxev = eigvecs.shape[1]
    per_nar = nsub // nnar
    own = nnar * rdev
    sub, nar = lax.axis_index("sub"), lax.axis_index("nar")

    r = residual[:, 0, :]
    live = jnp.arange(maxev)[:, None] < ev_count[0]
    vecs = jnp.where(live, eigvecs[0], 0.0)
    even = sub % 2 == 0
    rights, lefts = send_rows[0, 0], send_rows[1, 0]
    picked = jnp.concatenate([jnp.where(even, rights, lefts), jnp.where(even, lefts, rights)])
    pick = (jnp.arange(rdev)[:, None] == picked[None, :]).astype(jnp.float32)

    def chosen(field):
        return jnp.dot(field, pick, precision=HIGHEST)

    partial_res = times(r, vecs)
    norm = jnp.sum(r * r, axis=1, keepdims=True)
    tail = jnp.zeros((count, 128 - maxev - 1), jnp.float32)
    block = jnp.concatenate([r, chosen(r), partial_res, norm, tail], axis=1)
    got = spread(block, "nar", nnar)
    res = jnp.sum(got[:, :, rdev + 2 * over :], axis=0)
    r_own = in_rows(got[:, :, :rdev])
    to_a = in_rows(got[:, :, rdev : rdev + over])
    to_b = in_rows(got[:, :, rdev + over : rdev + 2 * over])
    r_margin = beside(to_a, to_b, nsub)
    local = times(r_own, local_inverse[0, :, :own])

    whole = spread(res, "sub", nsub)
    norms = jnp.sum(whole[:, :, maxev], axis=0)
    beta = jnp.sqrt(norms / total + EPS)
    piece = lax.dynamic_slice_in_dim(whole, nar * per_nar, per_nar, 0)[:, :, :maxev]
    sol_part = times(in_rows(piece), coarse_inverse)
    sol = jnp.sum(spread(sol_part, "nar", nnar), axis=0)
    local = local + times(r_margin, local_inverse[0, :, own:])
    correction = jnp.dot(sol, vecs, precision=HIGH)
    precond = (local + correction) / beta[:, None]
    start = r / beta[:, None]

    block = jnp.concatenate([precond, chosen(precond)], axis=1)
    got = spread(block, "nar", nnar)
    p_own = in_rows(got[:, :, :rdev])
    to_a = in_rows(got[:, :, rdev : rdev + over])
    to_b = in_rows(got[:, :, rdev + over :])
    p_margin = beside(to_a, to_b, nsub)
    image = times(p_own, stiffness[0, :, :own]) + times(p_margin, stiffness[0, :, own:])

    n_d = jnp.sum(start * start, axis=1)
    a_d = jnp.sum(start * image, axis=1)

    def ratio(a, n):
        return jnp.where(n > 0, a / jnp.where(n > 0, n, 1.0), 0.0)

    h_d = ratio(a_d, n_d)
    off = image - h_d[:, None] * start
    s_d = jnp.sum(off * off, axis=1)
    stats = jnp.concatenate([n_d, a_d, s_d, jnp.zeros_like(n_d)])[None]
    stats = spread(stats, ("sub", "nar"), nsub * nnar)[:, 0]
    n_i, a_i, s_i = (stats[:, i * count : (i + 1) * count] for i in range(3))
    n, a = jnp.sum(n_i, axis=0), jnp.sum(a_i, axis=0)
    h = ratio(a, n)
    gap = ratio(a_i, n_i) - h[None]
    square = jnp.sum(s_i + (n_i * gap) * gap, axis=0)
    lost = EPS / (beta * beta)
    h00 = a / total
    square = square + a * h * (lost * lost)
    h10 = jnp.sqrt(square / total + EPS)
    remainder = image - h00[:, None] * start
    next_vector = remainder / h10[:, None]
    factor = beta * h00 / (h00 * h00 + h10 * h10)
    new_iterate = iterate[:, 0, :] + factor[:, None] * precond
    return (
        next_vector[:, None, :],
        new_iterate[:, None, :],
        jnp.stack([beta, h00, h10]),
    )


def solution(mesh):
    return jax.shard_map(
        per_device,
        mesh=mesh,
        in_specs=(
            P(None, "sub", "nar"),
            P(None, "sub", "nar"),
            P("sub", "nar", None),
            P("sub", "nar", None),
            P("sub", None, "nar"),
            P("sub"),
            P("sub", "nar"),
            P(None, "sub", "nar"),
        ),
        out_specs=(P(None, "sub", "nar"), P(None, "sub", "nar"), P()),
        check_vma=False,
    )
```

time: 451 us -> 117 us (0.26)
  blocking collectives: 412 us -> 33.1 us
  starting transfers between devices: 6.71 us -> 28.2 us
  waiting for transfers between devices: 0.01 us -> 18.3 us
  other arithmetic: 3.67 us -> 8.94 us
    psum x5 -> x0, blocking collectives: 289 us -> none  [the longest x1 81.4 us: per_device(): lax.psum(local_inner(residual, residual, total), ('sub', 'nar')) + EPS]
    all_gather x7 -> x0, blocking collectives: 123 us -> none  [the longest x1 38.4 us: precondition(): whole = lax.all_gather(summed, 'sub', axis=1, tiled=True)]
    all_to_all x0 -> x2, blocking collectives: none -> 33.1 us  [spread(): return lax.all_to_all(copies, axes, 0, 0)]
    all_to_all x0 -> x3, starting transfers between devices: none -> 22.5 us  [spread(): return lax.all_to_all(copies, axes, 0, 0)]
    all_to_all x0 -> x3, waiting for transfers between devices: none -> 13.5 us  [spread(): return lax.all_to_all(copies, axes, 0, 0)]
    transpose x0 -> x8, local copies, waits for them, and re-layouts: none -> 6.84 us  [in_rows(): return jnp.swapaxes(blocks, 0, 1).reshape(blocks.shape[1], -1)]
    all_gather x5 -> x0, local copies, waits for them, and re-layouts: 5.29 us -> none  [the longest x2 2.41 us: extend(): lax.all_gather(from_right, 'nar', axis=2, tiled=True)]
    ppermute x4, waiting for transfers between devices: 0.01 us -> 4.82 us  [the longest x2 4.82 us: beside(): got_b = lax.ppermute(second, 'sub', route_b)]
  transfers between devices with their start and end apart: 4 -> 7, of which waited for: 0 -> 4; matrix products, arithmetic and copies ran while one was open for 2% -> 14% of each run, Pallas kernels for 0% -> 0%
where the time goes in v1:
time: 117 us; the launch traced here: 116 us
  blocking collectives  33.1 us (28%)
  starting transfers between devices  28.2 us (24%)
  waiting for transfers between devices  18.3 us (16%)
  local copies, waits for them, and re-layouts  17.6 us (15%)
  other arithmetic  8.94 us (8%)
  matrix products  8.61 us (7%)
  between operations  1.68 us (1%)
    all_to_all x2, blocking collectives, spread(): return lax.all_to_all(copies, axes, 0, 0)  33.1 us
    all_to_all x3, starting transfers between devices, spread(): return lax.all_to_all(copies, axes, 0, 0)  22.5 us
    all_to_all x3, waiting for transfers between devices, spread(): return lax.all_to_all(copies, axes, 0, 0)  13.5 us
    transpose x8, local copies, waits for them, and re-layouts, in_rows(): return jnp.swapaxes(blocks, 0, 1).reshape(blocks.shape[1], -1)  6.84 us
    dot_general x6, matrix products, times(): lax.dot_general(field, matrix, (((1,), (1,)), ((), ())), precision=precis...  6.26 us
    ppermute x2, starting transfers between devices, beside(): got_b = lax.ppermute(second, 'sub', route_b)  5.67 us
    reshape x7, local copies, waits for them, and re-layouts, in_rows(): return jnp.swapaxes(blocks, 0, 1).reshape(blocks.shape[1], -1)  4.86 us
    ppermute x2, waiting for transfers between devices, beside(): got_b = lax.ppermute(second, 'sub', route_b)  4.82 us
  transfers between devices with their start and end apart: 7, of which 4 were waited for; matrix products, arithmetic and copies ran while one was open for 14% of the time, Pallas kernels for 0%

profile of v1, /device:TPU:1, one launch (start us, length us, event | category | flops | bytes accessed | tf_op | source)
XLA Modules:
  0.0 116.4 jit_solution(7303071364128099719)
XLA Ops:
  0.6 0.0 copy-start
  0.7 0.8 copy.90
  1.5 0.9 multiply_reduce_fusion.3
  2.3 0.7 fusion.35
  3.0 0.1 pad_add_fusion
  3.1 1.1 convolution_bitcast_fusion.1
  4.8 0.0 copy-start.9
  4.8 0.1 copy.59
  4.9 1.1 convolution_bitcast_fusion
  6.1 0.1 concatenate.19
  6.2 0.8 broadcast_in_dim.92
  7.0 7.3 %all-to-all-start = ((f32[8,32,512]{2,1,0:T(8,128)}), f32[8,32,512]{2,1,0:T(8,128)}, u32[]{:S(2)}, u32[]{:S(2)}) async-start(f32[8,32,512]{2,1,0:T(8,128)} %broadcast_in_dim.92), calls=%async_computation | async-start | bytes 1048576 | tf_op jit(solution)/shard_map/all_to_all | solution.py:13
  14.3 9.6 %all-to-all-done = f32[8,32,512]{2,1,0:T(8,128)} async-done(((f32[8,32,512]{2,1,0:T(8,128)}), f32[8,32,512]{2,1,0:T(8,128)}, u32[]{:S(2)}, u32[]{:S(2)}) %all-to-all-start) | async-done | bytes 524320 | tf_op jit(solution)/shard_map/all_to_all | solution.py:13
  23.9 0.9 slice_reduce_fusion.1
  24.8 0.8 broadcast_in_dim.94
  25.7 9.9 %all-to-all-start.1 = ((f32[32,32,128]{2,1,0:T(8,128)}), f32[32,32,128]{2,1,0:T(8,128)}, u32[]{:S(2)}, u32[]{:S(2)}) async-start(f32[32,32,128]{2,1,0:T(8,128)} %broadcast_in_dim.94), calls=%async_computation.1 | async-start | bytes 1048576 | tf_op jit(solution)/shard_map/all_to_all | solution.py:13
  35.5 1.0 slice_bitcast_fusion.1
  36.5 1.7 %slice_bitcast_fusion.5 = (f32[32,8,64]{2,0,1:T(8,128)S(1)}, f32[32,8,64]{2,0,1:T(8,128)}) fusion(f32[8,32,512]{2,1,0:T(8,128)} %all-to-all-done), kind=kLoop, calls=%fused_computation.23 | loop fusion | bytes 262144 | tf_op jit(solution)/shard_map/transpose | solution.py:34
  38.2 0.7 copy.61
  39.0 1.6 %reshape.187 = f32[32,512]{1,0:T(8,128)} reshape(f32[32,8,64]{2,1,0:T(8,128)} %copy.61) | data formatting | bytes 131072 | tf_op jit(solution)/shard_map/reshape | solution.py:34
  40.6 4.6 %collective-permute-start = (f32[32,512]{1,0:T(8,128)}, f32[32,512]{1,0:T(8,128)}, u32[]{:S(2)}, u32[]{:S(2)}) collective-permute-start(f32[32,512]{1,0:T(8,128)} %reshape.187), channel_id=1, source_target_pairs={{0,248},{8,16},{16,8},{24,32},{32,24},{40,48},{48,40},{56,64},{64,... | collective-permute-start | bytes 196616 | tf_op jit(solution)/shard_map/ppermute | solution.py:26
  45.1 1.6 %copy.62 = f32[32,8,64]{2,1,0:T(8,128)} copy(f32[32,8,64]{2,0,1:T(8,128)} %get-tuple-element.31) | data formatting | bytes 131072 | tf_op jit(solution)/shard_map/transpose | solution.py:34
  46.8 1.6 %reshape.188 = f32[32,512]{1,0:T(8,128)} reshape(f32[32,8,64]{2,1,0:T(8,128)} %copy.62) | data formatting | bytes 131072 | tf_op jit(solution)/shard_map/reshape | solution.py:34
  48.4 1.0 fusion.2
  49.4 0.0 copy-start.8
  49.4 3.0 %collective-permute-done = f32[32,512]{1,0:T(8,128)} collective-permute-done((f32[32,512]{1,0:T(8,128)}, f32[32,512]{1,0:T(8,128)}, u32[]{:S(2)}, u32[]{:S(2)}) %collective-permute-start) | collective-permute-done | bytes 65568 | tf_op jit(solution)/shard_map/ppermute | solution.py:26
  52.5 0.9 select_select_fusion.3
  53.3 0.6 convolution_add_fusion.2
  53.9 0.0 copy-start.2
  53.9 1.0 dynamic-slice_bitcast_fusion
  55.0 0.1 reshape.189
  55.1 0.2 fusion.46
  55.3 0.7 broadcast_in_dim.95
  55.9 5.4 %all-to-all-start.2 = ((f32[8,32,96]{2,1,0:T(8,128)}), f32[8,32,96]{2,1,0:T(8,128)S(1)}, u32[]{:S(2)}, u32[]{:S(2)}) async-start(f32[8,32,96]{2,1,0:T(8,128)} %broadcast_in_dim.95), calls=%async_computation.2 | async-start | bytes 262144 | tf_op jit(solution)/shard_map/all_to_all | solution.py:13
  61.3 1.3 %slice_reduce_fusion = f32[32]{0:T(128)S(1)} fusion(f32[32,32,128]{2,1,0:T(8,128)} %all-to-all-done.1), kind=kLoop, calls=%fused_computation.16 | loop fusion | flops 992 | bytes 4224 | tf_op jit(solution)/shard_map/reduce_sum | solution.py:77
  62.7 0.0 copy-start.4
  62.7 3.9 %all-to-all-done.2 = f32[8,32,96]{2,1,0:T(8,128)S(1)} async-done(((f32[8,32,96]{2,1,0:T(8,128)}), f32[8,32,96]{2,1,0:T(8,128)S(1)}, u32[]{:S(2)}, u32[]{:S(2)}) %all-to-all-start.2) | async-done | bytes 98336 | tf_op jit(solution)/shard_map/all_to_all | solution.py:13
  66.6 1.1 fusion.6
  67.8 0.2 fusion.17
  68.0 11.3 %all_to_all.25 = f32[8,32,384]{2,1,0:T(8,128)S(1)} all-to-all(f32[8,32,384]{2,1,0:T(8,128)S(1)} %broadcast_in_dim.98), channel_id=1, replica_groups=mesh['sub'=32,'nar'=8] {'nar'}, dimensions={0} | all-to-all | bytes 786432 | tf_op jit(solution)/shard_map/all_to_all | solution.py:13
  79.4 0.7 copy.73
  80.1 0.7 slice_bitcast_fusion.3
  80.8 0.1 copy.65
  80.9 0.1 reshape.191
  81.0 1.1 collective-permute-start.2
  82.1 1.0 copy.66
  83.0 0.7 reshape.192
  83.8 2.0 %fusion = f32[32,256]{1,0:T(8,128)S(1)} fusion(f32[32,2048]{1,0:T(8,128)} %bitcast.98, f32[1,256,3072]{2,1,0:T(8,128)S(1)} %copy-done.2), kind=kOutput, calls=%fused_computation | convolution fusion | flops 100663296 | bytes 2392064 | tf_op jit(solution)/shard_map/dot_general | solution.py:38
  85.8 1.8 %collective-permute-done.2 = f32[32,512]{1,0:T(8,128)} collective-permute-done((f32[32,512]{1,0:T(8,128)S(1)}, f32[32,512]{1,0:T(8,128)}, u32[]{:S(2)}, u32[]{:S(2)}) %collective-permute-start.2) | collective-permute-done | bytes 65568 | tf_op jit(solution)/shard_map/ppermute | solution.py:26
  87.6 0.9 select_select_fusion.1
  88.5 1.3 %multiply_reduce_fusion.1 = (f32[32]{0:T(128)S(1)}, f32[32]{0:T(128)S(1)}, f32[32,256]{1,0:T(8,128)S(1)}) fusion(f32[32]{0:T(128)} %copy-done.4, f32[32,1,256]{2,1,0:T(1,128)S(1)} %copy-done.3, f32[32,256]{1,0:T(8,128)S(1)} %fusion, f32[1,256,3072]{2,1,0:T(8,128)S(1)} %copy-done.2, f32[32,512]{1,0:T(8,128)S(1)} %get-tuple-element.35, ...), kind=kOutput, calls=%fused_computation.58 | convolution fusion | flops 50413504 | bytes 1278336 | tf_op jit(solution)/shard_map/dot_general | solution.py:38
  89.8 0.2 multiply_reduce_fusion
  90.0 0.1 pad_maximum_fusion.2
  90.1 0.1 broadcast_in_dim.100
  90.2 21.7 %all_to_all.26 = f32[256,1,128]{2,1,0:T(1,128)S(1)} all-to-all(f32[256,1,128]{2,1,0:T(1,128)S(1)} %broadcast_in_dim.100), channel_id=1, replica_groups=mesh['sub'=32,'nar'=8] {'sub','nar'}, dimensions={0} | all-to-all | bytes 262144 | tf_op jit(solution)/shard_map/all_to_all | solution.py:13
  111.9 0.1 copy.67
  112.0 0.1 slice_reduce_fusion.3
  112.2 0.2 fusion.30
  112.3 0.7 add_divide_fusion
  113.0 0.7 bitcast_multiply_fusion
  113.7 0.9 fusion.29
  114.5 0.6 copy.68
  115.2 0.6 copy.69
  115.8 0.6 pad_maximum_fusion.1
  (34 shorter events, 0.2 us)
Async XLA Ops:
  0.6 54.4 %copy-start = (f32[96,384]{1,0:T(8,128)S(1)}, f32[96,384]{1,0:T(8,128)}, u32[]{:S(2)}) copy-start(f32[96,384]{1,0:T(8,128)} %param.14) | copy-start | bytes 442372
  3.1 3.0 %copy-start.7 = (s32[128]{0:T(128)}, s32[128]{0:T(128)S(1)}, u32[]{:S(2)}) copy-start(s32[128]{0:T(128)S(1)} %pad_add_fusion) | copy-start | bytes 1540
  3.1 45.3 %copy-start.1 = (f32[1,256,3072]{2,1,0:T(8,128)S(1)}, f32[1,256,3072]{2,1,0:T(8,128)}, u32[]{:S(2)}) copy-start(f32[1,256,3072]{2,1,0:T(8,128)} %param.11) | copy-start | bytes 9437188
  4.8 1.3 %copy-start.9 = (pred[96]{0:T(512)(128)(4,1)}, pred[96]{0:T(512)(128)(4,1)S(1)}, u32[]{:S(2)}) copy-start(pred[96]{0:T(512)(128)(4,1)S(1)} %iota_compare_fusion.3) | copy-start | bytes 292
  7.0 16.9 %all-to-all-start = ((f32[8,32,512]{2,1,0:T(8,128)}), f32[8,32,512]{2,1,0:T(8,128)}, u32[]{:S(2)}, u32[]{:S(2)}) async-start(f32[8,32,512]{2,1,0:T(8,128)} %broadcast_in_dim.92), calls=%async_computation | async-start | bytes 1048576 | tf_op jit(solution)/shard_map/all_to_all | solution.py:13
  25.7 28.2 %all-to-all-start.1 = ((f32[32,32,128]{2,1,0:T(8,128)}), f32[32,32,128]{2,1,0:T(8,128)}, u32[]{:S(2)}, u32[]{:S(2)}) async-start(f32[32,32,128]{2,1,0:T(8,128)} %broadcast_in_dim.94), calls=%async_computation.1 | async-start | bytes 1048576 | tf_op jit(solution)/shard_map/all_to_all | solution.py:13
  40.6 11.9 %collective-permute-start = (f32[32,512]{1,0:T(8,128)}, f32[32,512]{1,0:T(8,128)}, u32[]{:S(2)}, u32[]{:S(2)}) collective-permute-start(f32[32,512]{1,0:T(8,128)} %reshape.187), channel_id=1, source_target_pairs={{0,248},{8,16},{16,8},{24,32},{32,24},{40,48},{48,40},{56,64},{64,... | collective-permute-start | bytes 196616 | tf_op jit(solution)/shard_map/ppermute | solution.py:26
  48.4 4.1 %collective-permute-start.1 = (f32[32,512]{1,0:T(8,128)}, f32[32,512]{1,0:T(8,128)S(1)}, u32[]{:S(2)}, u32[]{:S(2)}) collective-permute-start(f32[32,512]{1,0:T(8,128)} %reshape.188), channel_id=1, source_target_pairs={{0,8},{8,0},{16,24},{24,16},{32,40},{40,32},{48,56},{56,48},{64,72... | collective-permute-start | bytes 196616 | tf_op jit(solution)/shard_map/ppermute | solution.py:25
  49.4 17.2 %copy-start.10 = (pred[96]{0:T(512)(128)(4,1)S(1)}, pred[96]{0:T(512)(128)(4,1)}, u32[]{:S(2)}) copy-start(pred[96]{0:T(512)(128)(4,1)} %copy-done.9) | copy-start | bytes 292
  49.4 18.3 %copy-start.8 = (s32[128]{0:T(128)S(1)}, s32[128]{0:T(128)}, u32[]{:S(2)}) copy-start(s32[128]{0:T(128)} %copy-done.7) | copy-start | bytes 1540
  53.9 29.9 %copy-start.2 = (f32[1,256,3072]{2,1,0:T(8,128)S(1)}, f32[1,256,3072]{2,1,0:T(8,128)}, u32[]{:S(2)}) copy-start(f32[1,256,3072]{2,1,0:T(8,128)} %param.10) | copy-start | bytes 9437188
  55.9 10.7 %all-to-all-start.2 = ((f32[8,32,96]{2,1,0:T(8,128)}), f32[8,32,96]{2,1,0:T(8,128)S(1)}, u32[]{:S(2)}, u32[]{:S(2)}) async-start(f32[8,32,96]{2,1,0:T(8,128)} %broadcast_in_dim.95), calls=%async_computation.2 | async-start | bytes 262144 | tf_op jit(solution)/shard_map/all_to_all | solution.py:13
  62.7 5.3 %copy-start.6 = (f32[32]{0:T(128)}, f32[32]{0:T(128)S(1)}, u32[]{:S(2)}) copy-start(f32[32]{0:T(128)S(1)} %slice_reduce_fusion) | copy-start | bytes 388
  62.7 5.3 %copy-start.4 = (f32[32]{0:T(128)}, f32[32]{0:T(128)S(1)}, u32[]{:S(2)}) copy-start(f32[32]{0:T(128)S(1)} %add_sqrt_fusion.2) | copy-start | bytes 388
  68.0 20.5 %copy-start.3 = (f32[32,1,256]{2,1,0:T(1,128)S(1)}, f32[32,1,256]{2,1,0:T(1,128)}, u32[]{:S(2)}) copy-start(f32[32,1,256]{2,1,0:T(1,128)} %param.8) | copy-start | bytes 98308
  81.0 6.6 %collective-permute-start.2 = (f32[32,512]{1,0:T(8,128)S(1)}, f32[32,512]{1,0:T(8,128)}, u32[]{:S(2)}, u32[]{:S(2)}) collective-permute-start(f32[32,512]{1,0:T(8,128)S(1)} %reshape.191), channel_id=1, source_target_pairs={{0,248},{8,16},{16,8},{24,32},{32,24},{40,48},{48,40},{56,64},{64,... | collective-permute-start | bytes 196616 | tf_op jit(solution)/shard_map/ppermute | solution.py:26
  83.8 6.0 %copy-start.5 = (f32[32]{0:T(128)S(1)}, f32[32]{0:T(128)}, u32[]{:S(2)}) copy-start(f32[32]{0:T(128)} %copy-done.4) | copy-start | bytes 388
  83.8 3.8 %collective-permute-start.3 = (f32[32,512]{1,0:T(8,128)}, f32[32,512]{1,0:T(8,128)S(1)}, u32[]{:S(2)}, u32[]{:S(2)}) collective-permute-start(f32[32,512]{1,0:T(8,128)} %reshape.192), channel_id=1, source_target_pairs={{0,8},{8,0},{16,24},{24,16},{32,40},{40,32},{48,56},{56,48},{64,72... | collective-permute-start | bytes 196616 | tf_op jit(solution)/shard_map/ppermute | solution.py:25

commit v2 on v0

v2 whole, which is shorter than its diff:
```python
import functools

import jax
import jax.numpy as jnp
from jax import lax
from jax.experimental import pallas as pl
from jax.experimental.pallas import tpu as pltpu
from jax.sharding import PartitionSpec as P

EPS = 1e-06
HIGH = lax.Precision.HIGH
F32, BF16 = jnp.float32, jnp.bfloat16
LANES = 128
NT = (((1,), (1,)), ((), ()))
NN = (((1,), (0,)), ((), ()))


def shape(*dims):
    return jax.ShapeDtypeStruct(dims, F32)


VMEM = pl.BlockSpec(memory_space=pltpu.VMEM)
SMEM = pl.BlockSpec(memory_space=pltpu.SMEM)


def local_call(body, outs, in_specs, *args, scratch=(), **options):
    many = isinstance(outs, tuple)
    return pl.pallas_call(
        body,
        out_shape=outs,
        in_specs=in_specs,
        out_specs=tuple(VMEM for _ in outs) if many else VMEM,
        scratch_shapes=scratch,
        compiler_params=pltpu.CompilerParams(vmem_limit_bytes=32 * 2**20),
        **options,
    )(*args)


def halves(x):
    high = x.astype(BF16)
    return high, (x - high.astype(F32)).astype(BF16)


def dot3(a, b, dims):
    dot = functools.partial(lax.dot_general, dimension_numbers=dims, preferred_element_type=F32)
    (ah, al), (bh, bl) = halves(a), halves(b)
    return dot(ah, bh) + (dot(al, bh) + dot(ah, bl))


def exactly(pick, x, dims, first):
    high = x.astype(BF16)
    rest = x - high.astype(F32)
    mid = rest.astype(BF16)
    low = (rest - mid.astype(F32)).astype(BF16)
    total = None
    for part in (low, mid, high):
        pair = (pick, part) if first else (part, pick)
        term = lax.dot_general(*pair, dimension_numbers=dims, preferred_element_type=F32)
        total = term if total is None else total + term
    return total


def iota(dims, axis):
    return lax.broadcasted_iota(jnp.int32, dims, axis)


def as_row(col):
    k = col.shape[0]
    return jnp.sum(jnp.where(iota((k, LANES), 0) == iota((k, LANES), 1), col, 0.0), axis=0, keepdims=True)


def as_col(row, k):
    return jnp.sum(jnp.where(iota((k, LANES), 0) == iota((k, LANES), 1), row, 0.0), axis=1, keepdims=True)


def picker(rows_ref, rdev):
    even = lax.axis_index("sub") % 2 == 0
    rights, lefts = rows_ref[0], rows_ref[1]
    picked = jnp.concatenate([jnp.where(even, rights, lefts), jnp.where(even, lefts, rights)], axis=1)
    return (iota((rdev, LANES), 0) == picked).astype(F32).astype(BF16)


def masked(vecs_ref, count_ref):
    vecs = vecs_ref[0]
    return jnp.where(iota(vecs.shape, 0) < count_ref[0], vecs, 0.0)


def begin_kernel(res_ref, vecs_ref, count_ref, part_ref, wide_ref):
    k, _, rdev = res_ref.shape
    r = res_ref[:, 0, :]
    vecs = masked(vecs_ref, count_ref)
    ncol = LANES // k
    rows = vecs.shape[0] // ncol
    wide_ref[...] = jnp.zeros_like(wide_ref)
    for b in range(ncol):
        wide_ref[b * k : (b + 1) * k, b * rdev : (b + 1) * rdev] = r
    left = jnp.concatenate([vecs[b * rows : (b + 1) * rows] for b in range(ncol)], axis=1)
    part = dot3(left, wide_ref[...], NT)
    norm = as_row(jnp.sum(r * r, axis=1, keepdims=True))
    each = part_ref.shape[1] - 1
    for c in range(part_ref.shape[0]):
        part_ref[c, :each, :] = part[c * each : (c + 1) * each]
        part_ref[c, each:, :] = norm


def rows_kernel(res_ref, rows_ref, out_ref):
    rdev = res_ref.shape[2]
    r = res_ref[:, 0, :]
    both = jnp.concatenate([r, exactly(picker(rows_ref, rdev), r, NN, False)], axis=1)
    for c in range(out_ref.shape[0]):
        out_ref[c] = both


def vecs_kernel(vecs_ref, count_ref, rows_ref, out_ref):
    vecs = masked(vecs_ref, count_ref)
    rdev = vecs.shape[1]
    both = jnp.concatenate([vecs, exactly(picker(rows_ref, rdev), vecs, NN, False)], axis=1)
    for c in range(out_ref.shape[0]):
        out_ref[c] = both


def coarse_kernel(inv_ref, out_ref, *, nnar, maxev, ncol, each):
    nrow, ncols = inv_ref.shape
    per = ncols // maxev
    pad = each + 1
    total = nnar * ncol * per * pad
    p = iota((total, ncols), 0)
    a = p % pad
    q = (p // pad) % per
    b = (p // (pad * per)) % ncol
    c = p // (pad * per * ncol)
    want = jnp.where(a < each, q * maxev + b * (maxev // ncol) + c * each + a, -1)
    pick = (want == iota((total, ncols), 1)).astype(F32).astype(BF16)
    moved = exactly(pick, inv_ref[...], NT, True)
    out_ref[...] = jnp.zeros_like(out_ref)
    span = ncol * per * pad
    for d in range(nnar):
        out_ref[d, :, :nrow] = moved[d * span : (d + 1) * span]


def sum_kernel(got_ref, out_ref):
    total = jnp.sum(got_ref[...], axis=0)
    out_ref[...] = jnp.broadcast_to(total[None], out_ref.shape)


def weave(blocks, a_ref, b_ref):
    half = LANES // 2
    for i in range(0, len(blocks), 2):
        one, two = blocks[i], blocks[i + 1]
        low = iota(one.shape, 1) < half
        at = slice(i * half, i * half + LANES)
        a_ref[:, at] = jnp.where(low, one, pltpu.roll(two, half, 1))
        b_ref[:, at] = jnp.where(low, pltpu.roll(one, half, 1), two)


def spread_rows_kernel(got_ref, own_ref, a_ref, b_ref):
    n, _, width = got_ref.shape
    rdev = width - LANES
    for c in range(n):
        own_ref[:, c * rdev : (c + 1) * rdev] = got_ref[c, :, :rdev]
    weave([got_ref[c, :, rdev:] for c in range(n)], a_ref, b_ref)


def margins(a_ref, b_ref):
    sub, nsub = lax.axis_index("sub"), lax.axis_size("sub")
    even = sub % 2 == 0
    a, b = a_ref[...], b_ref[...]
    lefts = jnp.where(sub == 0, 0.0, jnp.where(even, b, a))
    rights = jnp.where(sub == nsub - 1, 0.0, jnp.where(even, a, b))
    return lefts, rights


def margin_product(a_ref, b_ref, mat_ref):
    lefts, rights = margins(a_ref, b_ref)
    half = lefts.shape[1]
    return dot3(lefts, mat_ref[0, :, :half], NT) + dot3(rights, mat_ref[0, :, half:], NT)


def local_kernel(a_ref, b_ref, mat_ref, own_ref, rows_ref, out_ref):
    local = own_ref[...] + margin_product(a_ref, b_ref, mat_ref)
    pick = picker(rows_ref, local.shape[1])
    out_ref[...] = jnp.concatenate([local, exactly(pick, local, NN, False)], axis=1)


def solve_kernel(got_ref, inv_ref, local_ref, out_ref, beta_ref, wide_ref, *, total, maxev):
    nsub, pad, _ = got_ref.shape
    k = local_ref.shape[0]
    width = local_ref.shape[1]
    nnar, span, _ = inv_ref.shape
    ncol = LANES // k
    chunk = span // ncol
    norms = jnp.sum(got_ref[:, pad - 1, :], axis=0, keepdims=True)
    beta = jnp.sqrt(as_col(norms, k) / total + EPS)
    res = got_ref[...].reshape(nsub * pad, LANES)
    for c in range(nnar):
        for b in range(ncol):
            wide_ref[c * chunk : (c + 1) * chunk, b * LANES : (b + 1) * LANES] = inv_ref[
                c, b * chunk : (b + 1) * chunk, :
            ]
    sol = dot3(res.T, wide_ref[...], NN)
    part = sum(sol[b * k : (b + 1) * k, b * LANES : (b + 1) * LANES] for b in range(ncol))
    both = jnp.concatenate([local_ref[...], part], axis=1) / beta
    for c in range(nnar):
        out_ref[c] = both
    beta_ref[...] = jnp.broadcast_to(beta, beta_ref.shape)


def precond_kernel(got_ref, vecs_ref, own_ref, a_ref, b_ref, mine_ref):
    n, k, width = got_ref.shape
    wide = width - LANES
    rdev = wide - LANES
    maxev = vecs_ref.shape[1]
    sol = jnp.sum(got_ref[:, :, wide:], axis=0)[:, :maxev]
    ends = []
    for c in range(n):
        field = got_ref[c, :, :wide] + dot3(sol, vecs_ref[c], NN)
        own_ref[:, c * rdev : (c + 1) * rdev] = field[:, :rdev]
        ends.append(field[:, rdev:])
    weave(ends, a_ref, b_ref)
    nar = lax.axis_index("nar")
    mine_ref[...] = own_ref[:, pl.ds(pl.multiple_of(nar * rdev, rdev), rdev)]


def ratio(a, n):
    return jnp.where(n > 0, a / jnp.where(n > 0, n, 1.0), 0.0)


def image_kernel(a_ref, b_ref, mat_ref, own_ref, res_ref, beta_ref, image_ref, out_ref):
    k = own_ref.shape[0]
    image = own_ref[...] + margin_product(a_ref, b_ref, mat_ref)
    start = res_ref[:, 0, :] / beta_ref[:, :1]
    n = jnp.sum(start * start, axis=1, keepdims=True)
    a = jnp.sum(start * image, axis=1, keepdims=True)
    off = image - ratio(a, n) * start
    s = jnp.sum(off * off, axis=1, keepdims=True)
    image_ref[...] = image
    row = as_row(n) + pltpu.roll(as_row(a), k, 1) + pltpu.roll(as_row(s), 2 * k, 1)
    out_ref[...] = jnp.broadcast_to(row[None], out_ref.shape)


def end_kernel(got_ref, image_ref, res_ref, iter_ref, pre_ref, beta_ref, next_ref, new_ref, hess_ref, *, total):
    k = image_ref.shape[0]
    stats = got_ref[:, 0, :]
    n_i = stats
    a_i = pltpu.roll(stats, LANES - k, 1)
    s_i = pltpu.roll(stats, LANES - 2 * k, 1)
    n = jnp.sum(n_i, axis=0, keepdims=True)
    a = jnp.sum(a_i, axis=0, keepdims=True)
    h = ratio(a, n)
    gap = ratio(a_i, n_i) - h
    square = jnp.sum(s_i + (n_i * gap) * gap, axis=0, keepdims=True)
    beta = beta_ref[:, :1]
    lost = EPS / (beta * beta)
    a_col = as_col(a, k)
    h00 = a_col / total
    square = as_col(square, k) + a_col * as_col(h, k) * (lost * lost)
    h10 = jnp.sqrt(square / total + EPS)
    start = res_ref[:, 0, :] / beta
    next_ref[:, 0, :] = (image_ref[...] - h00 * start) / h10
    factor = beta * h00 / (h00 * h00 + h10 * h10)
    new_ref[:, 0, :] = iter_ref[:, 0, :] + factor * pre_ref[...]
    hess_ref[...] = jnp.concatenate([as_row(beta)[:, :k], as_row(h00)[:, :k], as_row(h10)[:, :k]], axis=0)


def exchange(blocks, axes):
    return lax.all_to_all(blocks, axes, 0, 0)


def beside(first, second, nsub):
    route_a = [(i, i ^ 1) for i in range(nsub)]
    route_b = [(i, (i + 1 if i % 2 else i - 1) % nsub) for i in range(nsub)]
    return lax.ppermute(first, "sub", route_a), lax.ppermute(second, "sub", route_b)


def times(field, matrix):
    return lax.dot_general(field, matrix, NT, precision=HIGH)


def with_margins(kernel, outs, a, b, matrix, *rest):
    rdev, ext = matrix.shape[1:]
    width = 2 * a.shape[1]
    block = (ext - width) // width

    def whole(x):
        zeros = (0,) * x.ndim
        return pl.BlockSpec(x.shape, lambda i: zeros)

    many = isinstance(outs, tuple)
    return pl.pallas_call(
        kernel,
        grid=(1,),
        out_shape=outs,
        in_specs=[whole(a), whole(b), pl.BlockSpec((1, rdev, width), lambda i: (0, 0, block))]
        + [whole(x) for x in rest],
        out_specs=tuple(whole(x) for x in outs) if many else whole(outs),
        compiler_params=pltpu.CompilerParams(vmem_limit_bytes=32 * 2**20),
    )(a, b, matrix, *rest)


def per_device(
    residual, iterate, stiffness, local_inverse, eigvecs, ev_count, coarse_inverse, send_rows
):
    nsub, nnar = lax.axis_size("sub"), lax.axis_size("nar")
    k, _, rdev = residual.shape
    total = nsub * nnar * rdev
    over = send_rows.shape[2]
    maxev = eigvecs.shape[1]
    own = nnar * rdev
    ncol = LANES // k
    each = maxev // ncol // nnar
    pad = each + 1
    span = coarse_inverse.shape[1] // maxev * ncol * pad

    part = local_call(
        begin_kernel, shape(nnar, pad, LANES), [VMEM, VMEM, SMEM], residual, eigvecs, ev_count,
        scratch=[pltpu.VMEM((LANES, ncol * rdev), F32)],
    )
    part = exchange(part, "nar")
    rows = local_call(rows_kernel, shape(nnar, k, rdev + 2 * over), [VMEM, VMEM], residual, send_rows)
    rows = exchange(rows, "nar")
    inverse = local_call(
        functools.partial(coarse_kernel, nnar=nnar, maxev=maxev, ncol=ncol, each=each),
        shape(nnar, span, LANES), [VMEM], coarse_inverse,
    )
    inverse = exchange(inverse, "nar")
    vecs = local_call(
        vecs_kernel, shape(nnar, maxev, rdev + 2 * over), [VMEM, SMEM, VMEM], eigvecs, ev_count, send_rows
    )
    vecs = exchange(vecs, "nar")
    res = local_call(sum_kernel, shape(nsub, pad, LANES), [VMEM], part)
    res = exchange(res, "sub")

    pieces = (shape(k, own), shape(k, nnar * over), shape(k, nnar * over))
    r_own, to_a, to_b = local_call(spread_rows_kernel, pieces, [VMEM], rows)
    got_a, got_b = beside(to_a, to_b, nsub)
    local = times(r_own, local_inverse[0, :, :own])
    local = with_margins(
        local_kernel, shape(k, rdev + 2 * over), got_a, got_b, local_inverse, local, send_rows
    )

    block, beta = local_call(
        functools.partial(solve_kernel, total=total, maxev=maxev),
        (shape(nnar, k, rdev + 2 * over + LANES), shape(k, LANES)),
        [VMEM, VMEM, VMEM], res, inverse, local,
        scratch=[pltpu.VMEM((nsub * pad, ncol * LANES), F32)],
    )
    block = exchange(block, "nar")
    p_own, to_a, to_b, precond = local_call(
        precond_kernel, pieces + (shape(k, rdev),), [VMEM, VMEM], block, vecs
    )

    got_a, got_b = beside(to_a, to_b, nsub)
    image = times(p_own, stiffness[0, :, :own])
    image, stats = with_margins(
        image_kernel, (shape(k, rdev), shape(nsub * nnar, 1, LANES)),
        got_a, got_b, stiffness, image, residual, beta,
    )
    stats = exchange(stats, ("sub", "nar"))
    return local_call(
        functools.partial(end_kernel, total=total),
        (shape(k, 1, rdev), shape(k, 1, rdev), shape(3, k)),
        [VMEM] * 6, stats, image, residual, iterate, precond, beta,
    )


def solution(mesh):
    return jax.shard_map(
        per_device,
        mesh=mesh,
        in_specs=(
            P(None, "sub", "nar"),
            P(None, "sub", "nar"),
            P("sub", "nar", None),
            P("sub", "nar", None),
            P("sub", None, "nar"),
            P("sub"),
            P("sub", "nar"),
            P(None, "sub", "nar"),
        ),
        out_specs=(P(None, "sub", "nar"), P(None, "sub", "nar"), P()),
        check_vma=False,
    )
```

time: 451 us -> 129 us (0.29)
  blocking collectives: 412 us -> 40.9 us
  starting transfers between devices: 6.71 us -> 40 us
  waiting for transfers between devices: 0.01 us -> 22.1 us
  Pallas kernels: 0 us -> 9.16 us
  matrix products: 11.8 us -> 3.77 us
    psum x5 -> x0, blocking collectives: 289 us -> none  [the longest x1 81.4 us: per_device(): lax.psum(local_inner(residual, residual, total), ('sub', 'nar')) + EPS]
    all_gather x7 -> x0, blocking collectives: 123 us -> none  [the longest x1 38.4 us: precondition(): whole = lax.all_gather(summed, 'sub', axis=1, tiled=True)]
    all_to_all x0 -> x2, blocking collectives: none -> 40.9 us  [exchange(): return lax.all_to_all(blocks, axes, 0, 0)]
    all_to_all x0 -> x5, starting transfers between devices: none -> 31.8 us  [exchange(): return lax.all_to_all(blocks, axes, 0, 0)]
    all_to_all x0 -> x5, waiting for transfers between devices: none -> 18.7 us  [exchange(): return lax.all_to_all(blocks, axes, 0, 0)]
    pallas_call x0 -> x11, Pallas kernels: none -> 9.16 us  [the longest x9 6.72 us: local_call(): pl.pallas_call(body, out_shape=outs, in_specs=in_specs, out_specs=tuple((...]
    unnamed x12 -> x40, local copies, waits for them, and re-layouts: 1.94 us -> 10.7 us
    dot_general x5 -> x2, matrix products: 11.8 us -> 3.77 us  [times(): return lax.dot_general(field, matrix, NT, precision=HIGH)]
  transfers between devices with their start and end apart: 4 -> 9, of which waited for: 0 -> 5; matrix products, arithmetic and copies ran while one was open for 2% -> 3% of each run, Pallas kernels for 0% -> 3%
where the time goes in v2:
time: 129 us; the launch traced here: 128 us
  blocking collectives  40.9 us (32%)
  starting transfers between devices  40 us (31%)
  waiting for transfers between devices  22.1 us (17%)
  local copies, waits for them, and re-layouts  10.7 us (8%)
  Pallas kernels  9.16 us (7%)
  matrix products  3.77 us (3%)
  between operations  1.62 us (1%)
    all_to_all x2, blocking collectives, exchange(): return lax.all_to_all(blocks, axes, 0, 0)  40.9 us
    all_to_all x5, starting transfers between devices, exchange(): return lax.all_to_all(blocks, axes, 0, 0)  31.8 us
    all_to_all x5, waiting for transfers between devices, exchange(): return lax.all_to_all(blocks, axes, 0, 0)  18.7 us
    unnamed x40, local copies, waits for them, and re-layouts  10.7 us
    pallas_call x9, Pallas kernels, local_call(): pl.pallas_call(body, out_shape=outs, in_specs=in_specs, out_specs=tuple((...  6.72 us
    ppermute x2, starting transfers between devices, beside(): lax.ppermute(second, 'sub', route_b)  6.56 us
    dot_general x2, matrix products, times(): return lax.dot_general(field, matrix, NT, precision=HIGH)  3.77 us
    ppermute x2, waiting for transfers between devices, beside(): lax.ppermute(second, 'sub', route_b)  3.41 us
  transfers between devices with their start and end apart: 9, of which 5 were waited for; matrix products, arithmetic and copies ran while one was open for 3% of the time, Pallas kernels for 3%

profile of v2, /device:TPU:1, one launch (start us, length us, event | category | flops | bytes accessed | tf_op | source)
XLA Modules:
  0.0 128.2 jit_solution(16115627572651579204)
XLA Ops:
  0.6 0.0 copy-start
  1.4 0.0 copy-start.5
  1.4 0.9 copy-done.5
  2.4 0.0 copy-start.9
  2.4 0.9 copy-done.9
  3.2 0.9 shard_map.103
  4.2 6.5 %all-to-all-start = ((f32[8,4,128]{2,1,0:T(4,128)}), f32[8,4,128]{2,1,0:T(4,128)S(1)}, u32[]{:S(2)}, u32[]{:S(2)}) async-start(f32[8,4,128]{2,1,0:T(4,128)} %shard_map.103), calls=%async_computation | async-start | bytes 32768 | tf_op jit(solution)/shard_map/all_to_all | solution.py:266
  10.6 0.0 copy-start.6
  10.6 0.8 copy-done.6
  11.4 0.7 copy-done.17
  12.1 0.3 shard_map.106
  12.4 0.0 copy-start.3
  12.4 0.7 copy-done.3
  13.2 2.1 %all-to-all-done.got_ref = f32[8,4,128]{2,1,0:T(4,128)S(1)} async-done(((f32[8,4,128]{2,1,0:T(4,128)}), f32[8,4,128]{2,1,0:T(4,128)S(1)}, u32[]{:S(2)}, u32[]{:S(2)}) %all-to-all-start) | async-done | bytes 16416 | tf_op jit(solution)/shard_map/all_to_all | solution.py:266
  15.3 4.1 %all-to-all-start.3 = ((f32[8,32,384]{2,1,0:T(8,128)}), f32[8,32,384]{2,1,0:T(8,128)S(1)}, u32[]{:S(2)}, u32[]{:S(2)}) async-start(f32[8,32,384]{2,1,0:T(8,128)} %copy-done.3), calls=%async_computation.3 | async-start | bytes 786432 | tf_op jit(solution)/shard_map/all_to_all | solution.py:266
  19.4 0.0 copy-start.12
  19.4 0.6 copy-done.12
  20.0 7.5 %all-to-all-done.3.got_ref = f32[8,32,384]{2,1,0:T(8,128)S(1)} async-done(((f32[8,32,384]{2,1,0:T(8,128)}), f32[8,32,384]{2,1,0:T(8,128)S(1)}, u32[]{:S(2)}, u32[]{:S(2)}) %all-to-all-start.3) | async-done | bytes 393248 | tf_op jit(solution)/shard_map/all_to_all | solution.py:266
  27.5 10.6 %all-to-all-start.1 = ((f32[32,4,128]{2,1,0:T(4,128)}), f32[32,4,128]{2,1,0:T(4,128)}, u32[]{:S(2)}, u32[]{:S(2)}) async-start(f32[32,4,128]{2,1,0:T(4,128)} %copy-done.12), calls=%async_computation.1 | async-start | bytes 131072 | tf_op jit(solution)/shard_map/all_to_all | solution.py:266
  38.1 0.0 copy-start.13
  38.1 0.9 copy-done.13
  39.0 0.6 shard_map.105
  39.6 0.0 copy-start.4
  39.6 0.7 copy-done.4
  40.3 0.7 shard_map.107
  41.0 0.0 copy-start.11
  41.0 0.7 copy-done.11
  41.7 1.2 collective-permute-start
  42.9 4.6 %collective-permute-start.1 = (f32[32,512]{1,0:T(8,128)}, f32[32,512]{1,0:T(8,128)}, u32[]{:S(2)}, u32[]{:S(2)}) collective-permute-start(f32[32,512]{1,0:T(8,128)} %get-tuple-element.15), channel_id=1, source_target_pairs={{0,248},{8,16},{16,8},{24,32},{32,24},{40,48},{48,40},{56,64},{64,... | collective-permute-start | bytes 196616 | tf_op jit(solution)/shard_map/ppermute | solution.py:272
  47.5 0.0 all-to-all-done.1.got_ref
  47.5 5.3 %all-to-all-start.2 = ((f32[8,64,128]{2,1,0:T(8,128)}), f32[8,64,128]{2,1,0:T(8,128)S(1)}, u32[]{:S(2)}, u32[]{:S(2)}) async-start(f32[8,64,128]{2,1,0:T(8,128)} %copy-done.4), calls=%async_computation.2 | async-start | bytes 524288 | tf_op jit(solution)/shard_map/all_to_all | solution.py:266
  52.8 2.7 %fusion.2.own_ref = f32[32,256]{1,0:T(8,128)S(1)} fusion(f32[32,2048]{1,0:T(8,128)} %copy-done.11, f32[1,256,3072]{2,1,0:T(8,128)} %mat_ref.2), kind=kOutput, calls=%fused_computation.2 | convolution fusion | flops 100663296 | bytes 2392064 | tf_op jit(solution)/shard_map/dot_general | solution.py:276
  55.5 0.0 collective-permute-done.a_ref
  55.5 0.0 collective-permute-done.1.b_ref
  55.5 0.0 copy-done
  55.6 0.0 copy-start.18
  55.6 0.7 copy-done.18
  56.2 1.6 %shard_map.108.local_ref = f32[32,384]{1,0:T(8,128)S(1)} custom-call(f32[32,512]{1,0:T(8,128)} %collective-permute-done.a_ref, f32[32,512]{1,0:T(8,128)} %collective-permute-done.1.b_ref, f32[1,256,3072]{2,1,0:T(8,128)S(1)} %copy-done, f32[32,256]{1,0:T(8,128)S(1)} %fusion.2.own_ref, s32[2,1,64]{2,1,0:T(1,128)S(1)} %copy-done.18), custom_call_target="tpu_custom_call" | custom-call | tf_op jit(solution)/shard_map/pallas_call | solution.py:289
  57.8 1.5 %all-to-all-done.2.inv_ref = f32[8,64,128]{2,1,0:T(8,128)S(1)} async-done(((f32[8,64,128]{2,1,0:T(8,128)}), f32[8,64,128]{2,1,0:T(8,128)S(1)}, u32[]{:S(2)}, u32[]{:S(2)}) %all-to-all-start.2) | async-done | bytes 262176 | tf_op jit(solution)/shard_map/all_to_all | solution.py:266
  59.3 1.1 shard_map.109
  60.5 0.0 copy-start.8
  60.5 0.8 copy-done.8
  61.3 0.6 copy-done.14
  61.9 5.3 %all-to-all-start.4 = ((f32[8,32,512]{2,1,0:T(8,128)}), f32[8,32,512]{2,1,0:T(8,128)}, u32[]{:S(2)}, u32[]{:S(2)}) async-start(f32[8,32,512]{2,1,0:T(8,128)} %copy-done.8), calls=%async_computation.4 | async-start | bytes 1048576 | tf_op jit(solution)/shard_map/all_to_all | solution.py:266
  67.2 0.0 copy-done.10
  67.2 0.7 copy-done.19
  67.9 0.3 shard_map.110
  68.2 0.0 copy-start.2
  68.2 1.0 copy-done.2
  69.2 7.6 %all-to-all-done.4.got_ref = f32[8,32,512]{2,1,0:T(8,128)} async-done(((f32[8,32,512]{2,1,0:T(8,128)}), f32[8,32,512]{2,1,0:T(8,128)}, u32[]{:S(2)}, u32[]{:S(2)}) %all-to-all-start.4) | async-done | bytes 524320 | tf_op jit(solution)/shard_map/all_to_all | solution.py:266
  76.8 21.0 %all_to_all.35.vecs_ref = f32[8,96,384]{2,1,0:T(8,128)S(1)} all-to-all(f32[8,96,384]{2,1,0:T(8,128)} %copy-done.2), channel_id=1, replica_groups=mesh['sub'=32,'nar'=8] {'nar'}, dimensions={0} | all-to-all | bytes 2359296 | tf_op jit(solution)/shard_map/all_to_all | solution.py:266
  97.8 1.6 %shard_map.111 = (f32[32,2048]{1,0:T(8,128)S(1)}, f32[32,512]{1,0:T(8,128)S(1)}, f32[32,512]{1,0:T(8,128)S(1)}, f32[32,256]{1,0:T(8,128)S(1)}) custom-call(f32[8,32,512]{2,1,0:T(8,128)} %all-to-all-done.4.got_ref, f32[8,96,384]{2,1,0:T(8,128)S(1)} %all_to_all.35.vecs_ref), custom_call_target="tpu_custom_call" | custom-call | tf_op jit(solution)/shard_map/pallas_call | solution.py:28
  99.3 0.5 collective-permute-start.2
  99.8 2.0 %collective-permute-start.3 = (f32[32,512]{1,0:T(8,128)S(1)}, f32[32,512]{1,0:T(8,128)S(1)}, u32[]{:S(2)}, u32[]{:S(2)}) collective-permute-start(f32[32,512]{1,0:T(8,128)S(1)} %get-tuple-element.19), channel_id=1, source_target_pairs={{0,248},{8,16},{16,8},{24,32},{32,24},{40,48},{48,40},{56,64},{64,... | collective-permute-start | bytes 196616 | tf_op jit(solution)/shard_map/ppermute | solution.py:272
  101.8 0.0 copy-done.1
  101.8 1.0 fusion.own_ref
  102.8 0.0 collective-permute-done.2.a_ref
  102.8 3.4 %collective-permute-done.3.b_ref = f32[32,512]{1,0:T(8,128)S(1)} collective-permute-done((f32[32,512]{1,0:T(8,128)S(1)}, f32[32,512]{1,0:T(8,128)S(1)}, u32[]{:S(2)}, u32[]{:S(2)}) %collective-permute-start.3) | collective-permute-done | bytes 65568 | tf_op jit(solution)/shard_map/ppermute | solution.py:272
  106.2 0.0 copy-done.7
  106.2 0.0 copy-done.15
  106.2 0.9 shard_map.112
  107.1 19.9 %all_to_all.36.got_ref = f32[256,1,128]{2,1,0:T(1,128)S(1)} all-to-all(f32[256,1,128]{2,1,0:T(1,128)S(1)} %get-tuple-element.22), channel_id=1, replica_groups=mesh['sub'=32,'nar'=8] {'sub','nar'}, dimensions={0} | all-to-all | bytes 262144 | tf_op jit(solution)/shard_map/all_to_all | solution.py:266
  127.1 0.0 copy-done.16
  127.1 1.2 shard_map.113
  (9 shorter events, 0.0 us)
Async XLA Ops:
  0.6 54.9 %copy-start = (f32[1,256,3072]{2,1,0:T(8,128)S(1)}, f32[1,256,3072]{2,1,0:T(8,128)}, u32[]{:S(2)}) copy-start(f32[1,256,3072]{2,1,0:T(8,128)} %mat_ref.2) | copy-start | bytes 9437188
  1.4 0.9 copy-start.5
  2.4 0.9 copy-start.9
  4.2 11.2 %all-to-all-start = ((f32[8,4,128]{2,1,0:T(4,128)}), f32[8,4,128]{2,1,0:T(4,128)S(1)}, u32[]{:S(2)}, u32[]{:S(2)}) async-start(f32[8,4,128]{2,1,0:T(4,128)} %shard_map.103), calls=%async_computation | async-start | bytes 32768 | tf_op jit(solution)/shard_map/all_to_all | solution.py:266
  10.6 0.8 copy-start.6
  11.4 0.7 copy-start.17
  12.4 0.7 copy-start.3
  15.3 12.2 %all-to-all-start.3 = ((f32[8,32,384]{2,1,0:T(8,128)}), f32[8,32,384]{2,1,0:T(8,128)S(1)}, u32[]{:S(2)}, u32[]{:S(2)}) async-start(f32[8,32,384]{2,1,0:T(8,128)} %copy-done.3), calls=%async_computation.3 | async-start | bytes 786432 | tf_op jit(solution)/shard_map/all_to_all | solution.py:266
  19.4 0.6 copy-start.12
  27.5 20.0 %all-to-all-start.1 = ((f32[32,4,128]{2,1,0:T(4,128)}), f32[32,4,128]{2,1,0:T(4,128)}, u32[]{:S(2)}, u32[]{:S(2)}) async-start(f32[32,4,128]{2,1,0:T(4,128)} %copy-done.12), calls=%async_computation.1 | async-start | bytes 131072 | tf_op jit(solution)/shard_map/all_to_all | solution.py:266
  38.1 0.9 copy-start.13
  39.6 0.7 copy-start.4
  41.0 0.7 copy-start.11
  41.7 13.8 %collective-permute-start = (f32[32,512]{1,0:T(8,128)}, f32[32,512]{1,0:T(8,128)}, u32[]{:S(2)}, u32[]{:S(2)}) collective-permute-start(f32[32,512]{1,0:T(8,128)} %get-tuple-element.14), channel_id=1, source_target_pairs={{0,8},{8,0},{16,24},{24,16},{32,40},{40,32},{48,56},{56,48},{64,72... | collective-permute-start | bytes 196616 | tf_op jit(solution)/shard_map/ppermute | solution.py:272
  42.9 12.7 %collective-permute-start.1 = (f32[32,512]{1,0:T(8,128)}, f32[32,512]{1,0:T(8,128)}, u32[]{:S(2)}, u32[]{:S(2)}) collective-permute-start(f32[32,512]{1,0:T(8,128)} %get-tuple-element.15), channel_id=1, source_target_pairs={{0,248},{8,16},{16,8},{24,32},{32,24},{40,48},{48,40},{56,64},{64,... | collective-permute-start | bytes 196616 | tf_op jit(solution)/shard_map/ppermute | solution.py:272
  47.5 11.8 %all-to-all-start.2 = ((f32[8,64,128]{2,1,0:T(8,128)}), f32[8,64,128]{2,1,0:T(8,128)S(1)}, u32[]{:S(2)}, u32[]{:S(2)}) async-start(f32[8,64,128]{2,1,0:T(8,128)} %copy-done.4), calls=%async_computation.2 | async-start | bytes 524288 | tf_op jit(solution)/shard_map/all_to_all | solution.py:266
  52.8 14.4 %copy-start.10 = (f32[1,96,256]{2,1,0:T(8,128)S(1)}, f32[1,96,256]{2,1,0:T(8,128)}, u32[]{:S(2)}) copy-start(f32[1,96,256]{2,1,0:T(8,128)} %vecs_ref.3) | copy-start | bytes 294916
  55.6 0.7 copy-start.18
  60.5 0.8 copy-start.8
  61.3 0.6 copy-start.14
  61.9 39.9 %copy-start.1 = (f32[1,256,3072]{2,1,0:T(8,128)S(1)}, f32[1,256,3072]{2,1,0:T(8,128)}, u32[]{:S(2)}) copy-start(f32[1,256,3072]{2,1,0:T(8,128)} %mat_ref.3) | copy-start | bytes 9437188
  61.9 14.9 %all-to-all-start.4 = ((f32[8,32,512]{2,1,0:T(8,128)}), f32[8,32,512]{2,1,0:T(8,128)}, u32[]{:S(2)}, u32[]{:S(2)}) async-start(f32[8,32,512]{2,1,0:T(8,128)} %copy-done.8), calls=%async_computation.4 | async-start | bytes 1048576 | tf_op jit(solution)/shard_map/all_to_all | solution.py:266
  67.2 0.7 copy-start.19
  68.2 1.0 copy-start.2
  69.2 37.0 %copy-start.7 = (f32[32,1,256]{2,1,0:T(1,128)S(1)}, f32[32,1,256]{2,1,0:T(1,128)}, u32[]{:S(2)}) copy-start(f32[32,1,256]{2,1,0:T(1,128)} %res_ref.7) | copy-start | bytes 98308
  69.2 37.0 %copy-start.15 = (f32[32,128]{1,0:T(8,128)S(1)}, f32[32,128]{1,0:T(8,128)}, u32[]{:S(2)}) copy-start(f32[32,128]{1,0:T(8,128)} %copy-done.14) | copy-start | bytes 49156
  99.3 27.7 %copy-start.16 = (f32[32,1,256]{2,1,0:T(1,128)S(1)}, f32[32,1,256]{2,1,0:T(1,128)}, u32[]{:S(2)}) copy-start(f32[32,1,256]{2,1,0:T(1,128)} %iter_ref.1) | copy-start | bytes 98308
  99.3 3.5 %collective-permute-start.2 = (f32[32,512]{1,0:T(8,128)S(1)}, f32[32,512]{1,0:T(8,128)S(1)}, u32[]{:S(2)}, u32[]{:S(2)}) collective-permute-start(f32[32,512]{1,0:T(8,128)S(1)} %get-tuple-element.18), channel_id=1, source_target_pairs={{0,8},{8,0},{16,24},{24,16},{32,40},{40,32},{48,56},{56,48},{64,72... | collective-permute-start | bytes 196616 | tf_op jit(solution)/shard_map/ppermute | solution.py:272
  99.8 6.4 %collective-permute-start.3 = (f32[32,512]{1,0:T(8,128)S(1)}, f32[32,512]{1,0:T(8,128)S(1)}, u32[]{:S(2)}, u32[]{:S(2)}) collective-permute-start(f32[32,512]{1,0:T(8,128)S(1)} %get-tuple-element.19), channel_id=1, source_target_pairs={{0,248},{8,16},{16,8},{24,32},{32,24},{40,48},{48,40},{56,64},{64,... | collective-permute-start | bytes 196616 | tf_op jit(solution)/shard_map/ppermute | solution.py:272

commit v3 on v2

v3 whole, which is shorter than its diff:
```python
import functools

import jax
import jax.numpy as jnp
from jax import lax
from jax.experimental import pallas as pl
from jax.experimental.pallas import tpu as pltpu
from jax.sharding import PartitionSpec as P

EPS = 1e-06
F32, BF16 = jnp.float32, jnp.bfloat16
LANES = 128
NT = (((1,), (1,)), ((), ()))
NN = (((1,), (0,)), ((), ()))


def shape(*dims):
    return jax.ShapeDtypeStruct(dims, F32)


def whole(x):
    zeros = (0,) * len(x.shape)
    return pl.BlockSpec(x.shape, lambda i: zeros)


def local_call(body, outs, *args, specs=None, scratch=(), limit=4, cost=1):
    many = isinstance(outs, tuple)
    specs = specs or {}
    return pl.pallas_call(
        body,
        grid=(1,),
        out_shape=outs,
        in_specs=[specs.get(i) or whole(x) for i, x in enumerate(args)],
        out_specs=tuple(whole(x) for x in outs) if many else whole(outs),
        scratch_shapes=scratch,
        compiler_params=pltpu.CompilerParams(vmem_limit_bytes=limit * 2**20),
        cost_estimate=pl.CostEstimate(flops=int(cost * 1e9), bytes_accessed=1024, transcendentals=0),
    )(*args)


def halves(x):
    high = x.astype(BF16)
    return high, (x - high.astype(F32)).astype(BF16)


def dot3(a, b, dims):
    dot = functools.partial(lax.dot_general, dimension_numbers=dims, preferred_element_type=F32)
    (ah, al), (bh, bl) = halves(a), halves(b)
    return dot(ah, bh) + (dot(al, bh) + dot(ah, bl))


def exactly(pick, x, dims, first):
    high = x.astype(BF16)
    rest = x - high.astype(F32)
    mid = rest.astype(BF16)
    low = (rest - mid.astype(F32)).astype(BF16)
    total = None
    for part in (low, mid, high):
        pair = (pick, part) if first else (part, pick)
        term = lax.dot_general(*pair, dimension_numbers=dims, preferred_element_type=F32)
        total = term if total is None else total + term
    return total


def iota(dims, axis):
    return lax.broadcasted_iota(jnp.int32, dims, axis)


def as_row(col):
    k = col.shape[0]
    return jnp.sum(jnp.where(iota((k, LANES), 0) == iota((k, LANES), 1), col, 0.0), axis=0, keepdims=True)


def as_col(row, k):
    return jnp.sum(jnp.where(iota((k, LANES), 0) == iota((k, LANES), 1), row, 0.0), axis=1, keepdims=True)


def own_list(rows_ref):
    even = lax.axis_index("sub") % 2 == 0
    rights, lefts = rows_ref[0], rows_ref[1]
    return jnp.concatenate([jnp.where(even, rights, lefts), jnp.where(even, lefts, rights)], axis=1)


def pick_of(listed, rdev):
    return (iota((rdev, LANES), 0).astype(F32) == listed).astype(F32).astype(BF16)


def masked(vecs_ref, count_ref):
    vecs = vecs_ref[0]
    return jnp.where(iota(vecs.shape, 0) < count_ref[0], vecs, 0.0)


def begin_kernel(
    res_hbm, vecs_hbm, inv_hbm, rows_hbm, count_ref, out_ref,
    wide_ref, res_ref, vecs_ref, inv_ref, rows_ref, sems, *, each
):
    pairs = ((res_hbm, res_ref), (vecs_hbm, vecs_ref), (inv_hbm, inv_ref), (rows_hbm, rows_ref))
    copies = [pltpu.make_async_copy(one, two, sems.at[i]) for i, (one, two) in enumerate(pairs)]
    for copy in copies:
        copy.start()
    wide_ref[...] = jnp.zeros_like(wide_ref)
    out_ref[...] = jnp.zeros_like(out_ref)
    for copy in copies:
        copy.wait()
    k, _, rdev = res_ref.shape
    r = res_ref[:, 0, :]
    vecs = masked(vecs_ref, count_ref)
    maxev = vecs.shape[0]
    ncol = LANES // k
    rows = maxev // ncol
    for b in range(ncol):
        wide_ref[b * k : (b + 1) * k, b * rdev : (b + 1) * rdev] = r
    left = jnp.concatenate([vecs[b * rows : (b + 1) * rows] for b in range(ncol)], axis=1)
    part = dot3(left, wide_ref[...], NT)
    norm = as_row(jnp.sum(r * r, axis=1, keepdims=True))
    listed = own_list(rows_ref).astype(F32)
    nnar = out_ref.shape[0]
    moved = coarse_columns(inv_ref[...], nnar=nnar, maxev=maxev, ncol=ncol, each=each)
    span = moved.shape[0] // nnar
    at = rdev // LANES * k
    for c in range(nnar):
        for i in range(rdev // LANES):
            out_ref[c, i * k : (i + 1) * k, :] = r[:, i * LANES : (i + 1) * LANES]
        out_ref[c, at : at + each, :] = part[c * each : (c + 1) * each]
        out_ref[c, at + each : at + each + 1, :] = norm
        out_ref[c, at + each + 1 : at + each + 2, :] = listed
        out_ref[c, at + 8 :, :maxev] = moved[c * span : (c + 1) * span]


def coarse_columns(inverse, *, nnar, maxev, ncol, each):
    ncols = inverse.shape[1]
    per = ncols // maxev
    p = iota((1, ncols), 1)
    a = p % each
    q = (p // each) % per
    b = (p // (each * per)) % ncol
    c = p // (each * per * ncol)
    want = q * maxev + b * (maxev // ncol) + c * each + a
    pick = (want == iota((ncols, ncols), 0)).astype(F32).astype(BF16)
    return exactly(pick, inverse, NN, False).T


def weave(ends, a_ref, b_ref):
    half = LANES // 2
    for i in range(0, len(ends), 2):
        one, two = ends[i], ends[i + 1]
        low = iota(one.shape, 1) < half
        at = slice(i * half, i * half + LANES)
        a_ref[:, at] = jnp.where(low, one, pltpu.roll(two, half, 1))
        b_ref[:, at] = jnp.where(low, pltpu.roll(one, half, 1), two)


def sum_kernel(got_ref, after_ref, out_ref):
    del after_ref
    total = jnp.sum(got_ref[...], axis=0)[: out_ref.shape[1]]
    out_ref[...] = jnp.broadcast_to(total[None], out_ref.shape)


def middle_kernel(got_ref, own_ref, a_ref, b_ref):
    n, _, lanes = got_ref.shape
    k = own_ref.shape[0]
    rdev = own_ref.shape[1] // n
    halves_of = rdev // lanes
    at = halves_of * k
    ends = []
    for c in range(n):
        field = jnp.concatenate([got_ref[c, i * k : (i + 1) * k, :] for i in range(halves_of)], axis=1)
        own_ref[:, c * rdev : (c + 1) * rdev] = field
        listed = got_ref[c, at + 4 : at + 5, :]
        ends.append(exactly(pick_of(listed, rdev), field, NN, False))
    weave(ends, a_ref, b_ref)


def margins(a_ref, b_ref):
    sub, nsub = lax.axis_index("sub"), lax.axis_size("sub")
    even = sub % 2 == 0
    a, b = a_ref[...], b_ref[...]
    lefts = jnp.where(sub == 0, 0.0, jnp.where(even, b, a))
    rights = jnp.where(sub == nsub - 1, 0.0, jnp.where(even, a, b))
    return lefts, rights


def product_kernel(field_ref, mat_ref, out_ref, high_ref, low_ref):
    own = field_ref.shape[1]
    out_ref[...] = dot3(field_ref[...], mat_ref[0, :, :own], NT)
    high_ref[...], low_ref[...] = halves(mat_ref[0, :, own:])


def margin_product(a_ref, b_ref, high_ref, low_ref):
    dot = functools.partial(lax.dot_general, dimension_numbers=NT, preferred_element_type=F32)
    high, low = halves(jnp.concatenate(margins(a_ref, b_ref), axis=1))
    return dot(high, high_ref[...]) + (dot(low, high_ref[...]) + dot(high, low_ref[...]))


def local_kernel(a_ref, b_ref, own_ref, high_ref, low_ref, *refs):
    vecs, (out_ref, vecs_ref) = refs[:-2], refs[-2:]
    out_ref[...] = own_ref[...] + margin_product(a_ref, b_ref, high_ref, low_ref)
    for i, ref in enumerate(vecs):
        vecs_ref[i] = ref[0]


def solve_kernel(got_ref, one_ref, two_ref, local_ref, out_ref, beta_ref, wide_ref, *, total, maxev):
    nsub, pad, _ = got_ref.shape
    k = local_ref.shape[0]
    each = pad - 1
    nnar = one_ref.shape[0]
    ncol = LANES // k
    per = nsub // nnar
    chunk = per * each
    norms = jnp.sum(got_ref[:, pad - 1, :], axis=0, keepdims=True)
    beta = jnp.sqrt(as_col(norms, k) / total + EPS)
    res = got_ref[...].reshape(nsub * pad, LANES)
    wide_ref[...] = jnp.zeros_like(wide_ref)
    for c in range(nnar):
        for b in range(ncol):
            ref, at = (one_ref, b * chunk) if b < ncol // 2 else (two_ref, (b - ncol // 2) * chunk)
            piece = ref[c, at : at + chunk, :]
            for q in range(per):
                to = (c * per + q) * pad
                wide_ref[to : to + each, b * LANES : (b + 1) * LANES] = piece[q * each : (q + 1) * each]
    sol = dot3(res.T, wide_ref[...], NN)
    part = sum(sol[b * k : (b + 1) * k, b * LANES : (b + 1) * LANES] for b in range(ncol))
    both = jnp.concatenate([local_ref[...], part], axis=1) / beta
    for c in range(nnar):
        out_ref[c] = both
    beta_ref[...] = jnp.broadcast_to(beta, beta_ref.shape)


def precond_kernel(got_ref, lists_ref, count_ref, even_ref, odd_ref, own_ref, a_ref, b_ref, mine_ref):
    n, k, width = got_ref.shape
    rdev = width - LANES
    maxev = even_ref.shape[1]
    nar = lax.axis_index("nar")
    sol = jnp.sum(got_ref[:, :, rdev:], axis=0)
    sol = jnp.where(iota(sol.shape, 1) < count_ref[0], sol, 0.0)[:, :maxev]
    for i in range(n):
        field = got_ref[nar ^ i, :, :rdev] + dot3(sol, (odd_ref if i % 2 else even_ref)[i // 2], NN)
        own_ref[:, pl.ds(pl.multiple_of((nar ^ i) * rdev, rdev), rdev)] = field
        if i == 0:
            mine_ref[...] = field
    ends = [
        exactly(pick_of(lists_ref[c, 4:5, :], rdev), own_ref[:, c * rdev : (c + 1) * rdev], NN, False)
        for c in range(n)
    ]
    weave(ends, a_ref, b_ref)


def ratio(a, n):
    return jnp.where(n > 0, a / jnp.where(n > 0, n, 1.0), 0.0)


def image_kernel(a_ref, b_ref, own_ref, high_ref, low_ref, res_ref, beta_ref, image_ref, out_ref):
    k = own_ref.shape[0]
    image = own_ref[...] + margin_product(a_ref, b_ref, high_ref, low_ref)
    start = res_ref[:, 0, :] / beta_ref[:, :1]
    n = jnp.sum(start * start, axis=1, keepdims=True)
    a = jnp.sum(start * image, axis=1, keepdims=True)
    off = image - ratio(a, n) * start
    s = jnp.sum(off * off, axis=1, keepdims=True)
    image_ref[...] = image
    row = as_row(n) + pltpu.roll(as_row(a), k, 1) + pltpu.roll(as_row(s), 2 * k, 1)
    out_ref[...] = jnp.broadcast_to(row[None], out_ref.shape)


def end_kernel(got_ref, image_ref, res_ref, iter_ref, pre_ref, beta_ref, next_ref, new_ref, hess_ref, *, total):
    k = image_ref.shape[0]
    stats = got_ref[:, 0, :]
    n_i = stats
    a_i = pltpu.roll(stats, LANES - k, 1)
    s_i = pltpu.roll(stats, LANES - 2 * k, 1)
    n = jnp.sum(n_i, axis=0, keepdims=True)
    a = jnp.sum(a_i, axis=0, keepdims=True)
    h = ratio(a, n)
    gap = ratio(a_i, n_i) - h
    square = jnp.sum(s_i + (n_i * gap) * gap, axis=0, keepdims=True)
    beta = beta_ref[:, :1]
    lost = EPS / (beta * beta)
    a_col = as_col(a, k)
    h00 = a_col / total
    square = as_col(square, k) + a_col * as_col(h, k) * (lost * lost)
    h10 = jnp.sqrt(square / total + EPS)
    start = res_ref[:, 0, :] / beta
    next_ref[:, 0, :] = (image_ref[...] - h00 * start) / h10
    factor = beta * h00 / (h00 * h00 + h10 * h10)
    new_ref[:, 0, :] = iter_ref[:, 0, :] + factor * pre_ref[...]
    hess_ref[...] = jnp.concatenate([as_row(beta)[:, :k], as_row(h00)[:, :k], as_row(h10)[:, :k]], axis=0)


def exchange(blocks, axes):
    return lax.all_to_all(blocks, axes, 0, 0)


def beside(first, second, nsub):
    route_a = [(i, i ^ 1) for i in range(nsub)]
    route_b = [(i, (i + 1 if i % 2 else i - 1) % nsub) for i in range(nsub)]
    return lax.ppermute(first, "sub", route_a), lax.ppermute(second, "sub", route_b)


def across(block, n, mask):
    return lax.ppermute(block, "nar", [(i, i ^ mask) for i in range(n)])


def product(field, matrix):
    rdev, ext = matrix.shape[1:]
    split = jax.ShapeDtypeStruct((rdev, ext - field.shape[1]), BF16)
    return local_call(product_kernel, (shape(field.shape[0], rdev), split, split), field, matrix, limit=10)


def per_device(
    residual, iterate, stiffness, local_inverse, eigvecs, ev_count, coarse_inverse, send_rows
):
    nsub, nnar = lax.axis_size("sub"), lax.axis_size("nar")
    k, _, rdev = residual.shape
    total = nsub * nnar * rdev
    over = send_rows.shape[2]
    maxev = eigvecs.shape[1]
    own = nnar * rdev
    ncol = LANES // k
    each = maxev // ncol // nnar
    pad = each + 1
    span = coarse_inverse.shape[1] // nnar
    head = rdev // LANES * k
    smem = pl.BlockSpec(memory_space=pltpu.SMEM)
    hbm = pl.BlockSpec(memory_space=pltpu.HBM)

    vecs = [eigvecs] + [across(eigvecs, nnar, m) for m in range(2, nnar, 2)]

    part = local_call(
        functools.partial(begin_kernel, each=each),
        shape(nnar, head + 8 + span, LANES), residual, eigvecs, coarse_inverse, send_rows, ev_count,
        specs={0: hbm, 1: hbm, 2: hbm, 3: hbm, 4: smem},
        scratch=[
            pltpu.VMEM((LANES, ncol * rdev), F32),
            pltpu.VMEM(residual.shape, F32),
            pltpu.VMEM(eigvecs.shape, F32),
            pltpu.VMEM(coarse_inverse.shape, F32),
            pltpu.VMEM(send_rows.shape, jnp.int32),
            pltpu.SemaphoreType.DMA((4,)),
        ],
        limit=60,
    )
    part = exchange(part, "nar")
    lists = pl.BlockSpec((nnar, 8, LANES), lambda i: (0, head // 8, 0))
    pieces = (shape(k, own), shape(k, nnar * over), shape(k, nnar * over))
    r_own, to_a, to_b = local_call(
        middle_kernel, pieces, part,
        specs={0: pl.BlockSpec((nnar, head + 8, LANES), lambda i: (0, 0, 0))},
    )
    res = local_call(
        sum_kernel, shape(nsub, pad, LANES), part, to_b, specs={0: lists, 1: hbm}, cost=10
    )
    res = exchange(res, "sub")

    got_a, got_b = beside(to_a, to_b, nsub)
    local, vecs = local_call(
        local_kernel, (shape(k, rdev), shape(nnar // 2, maxev, rdev)),
        got_a, got_b, *product(r_own, local_inverse), *vecs,
    )
    vecs = (vecs, across(vecs, nnar, 1))

    first = (head + 8) // (span // 2)
    block, beta = local_call(
        functools.partial(solve_kernel, total=total, maxev=maxev),
        (shape(nnar, k, rdev + LANES), shape(k, LANES)), res, part, part, local,
        specs={
            j + 1: pl.BlockSpec((nnar, span // 2, LANES), lambda i, j=j: (0, first + j, 0))
            for j in range(2)
        },
        scratch=[pltpu.VMEM((nsub * pad, ncol * LANES), F32)],
    )
    block = exchange(block, "nar")
    p_own, to_a, to_b, precond = local_call(
        precond_kernel, pieces + (shape(k, rdev),), block, part, ev_count, *vecs,
        specs={1: lists, 2: smem},
    )

    got_a, got_b = beside(to_a, to_b, nsub)
    image, stats = local_call(
        image_kernel, (shape(k, rdev), shape(nsub * nnar, 1, LANES)),
        got_a, got_b, *product(p_own, stiffness), residual, beta,
    )
    stats = exchange(stats, ("sub", "nar"))
    return local_call(
        functools.partial(end_kernel, total=total),
        (shape(k, 1, rdev), shape(k, 1, rdev), shape(3, k)),
        stats, image, residual, iterate, precond, beta,
    )


def solution(mesh):
    return jax.shard_map(
        per_device,
        mesh=mesh,
        in_specs=(
            P(None, "sub", "nar"),
            P(None, "sub", "nar"),
            P("sub", "nar", None),
            P("sub", "nar", None),
            P("sub", None, "nar"),
            P("sub"),
            P("sub", "nar"),
            P(None, "sub", "nar"),
        ),
        out_specs=(P(None, "sub", "nar"), P(None, "sub", "nar"), P()),
        check_vma=False,
    )
```

time: 129 us -> 86.3 us (0.67)
  blocking collectives: 40.9 us -> 20 us
  local copies, waits for them, and re-layouts: 10.7 us -> 1.9 us
  starting transfers between devices: 40 us -> 32.8 us
  matrix products: 3.77 us -> 0 us
  waiting for transfers between devices: 22.1 us -> 19.6 us
    all_to_all x2 -> x1, blocking collectives: 40.9 us -> 20 us  [exchange(): return lax.all_to_all(blocks, axes, 0, 0)]
    all_to_all x5 -> x3, starting transfers between devices: 31.8 us -> 16.7 us  [exchange(): return lax.all_to_all(blocks, axes, 0, 0)]
    unnamed x40 -> x10, local copies, waits for them, and re-layouts: 10.7 us -> 1.9 us
    ppermute x0 -> x4, starting transfers between devices: none -> 6.1 us  [across(): return lax.ppermute(block, 'nar', [(i, i ^ mask) for i in range(n)])]
    dot_general x2 -> x0, matrix products: 3.77 us -> none  [times(): return lax.dot_general(field, matrix, NT, precision=HIGH)]
    all_to_all x5 -> x3, waiting for transfers between devices: 18.7 us -> 15.2 us  [exchange(): return lax.all_to_all(blocks, axes, 0, 0)]
    ppermute x2, starting transfers between devices: 6.56 us -> 8.14 us  [beside(): lax.ppermute(second, 'sub', route_b)]
    pallas_call x11 -> x10, Pallas kernels: 9.16 us -> 10.2 us  [local_call(): pl.pallas_call(body, grid=(1,), out_shape=outs, in_specs=[specs.get(i) or...]
  transfers between devices with their start and end apart: 9 -> 11, of which waited for: 5 -> 5; matrix products, arithmetic and copies ran while one was open for 3% -> 0% of each run, Pallas kernels for 3% -> 6%
where the time goes in v3:
time: 86.3 us; the launch traced here: 85.8 us
  starting transfers between devices  32.8 us (38%)
  blocking collectives  20 us (23%)
  waiting for transfers between devices  19.6 us (23%)
  Pallas kernels  10.2 us (12%)
  local copies, waits for them, and re-layouts  1.9 us (2%)
  between operations  1.42 us (2%)
    all_to_all x1, blocking collectives, exchange(): return lax.all_to_all(blocks, axes, 0, 0)  20 us
    all_to_all x3, starting transfers between devices, exchange(): return lax.all_to_all(blocks, axes, 0, 0)  16.7 us
    all_to_all x3, waiting for transfers between devices, exchange(): return lax.all_to_all(blocks, axes, 0, 0)  15.2 us
    pallas_call x10, Pallas kernels, local_call(): pl.pallas_call(body, grid=(1,), out_shape=outs, in_specs=[specs.get(i) or...  10.2 us
    ppermute x2, starting transfers between devices, beside(): lax.ppermute(second, 'sub', route_b)  8.14 us
    ppermute x4, starting transfers between devices, across(): return lax.ppermute(block, 'nar', [(i, i ^ mask) for i in range(n)])  6.1 us
    ppermute x2, waiting for transfers between devices, beside(): lax.ppermute(second, 'sub', route_b)  3.84 us
    unnamed x10, local copies, waits for them, and re-layouts  1.9 us
  transfers between devices with their start and end apart: 11, of which 5 were waited for; matrix products, arithmetic and copies ran while one was open for 0% of the time, Pallas kernels for 6%

profile of v3, /device:TPU:1, one launch (start us, length us, event | category | flops | bytes accessed | tf_op | source)
XLA Modules:
  0.0 85.8 jit_solution(2341370778108118244)
XLA Ops:
  0.6 0.0 copy-start.2
  1.3 2.4 %shard_map.103 = f32[8,120,128]{2,1,0:T(8,128)} custom-call(f32[32,1,256]{2,1,0:T(1,128)} %res_ref.3, f32[1,96,256]{2,1,0:T(8,128)} %refs_0_.1, f32[96,384]{1,0:T(8,128)} %inv_hbm.1, s32[2,1,64]{2,1,0:T(1,128)} %rows_hbm.1, s32[1]{0:T(128)S(6)} %copy.11.count_ref), custom_call_target="tpu_custom_call" | custom-call | flops 1000000000 | bytes 1024 | tf_op jit(solution)/shard_map/pallas_call | solution.py:29
  3.8 6.6 %all-to-all-start = ((f32[8,120,128]{2,1,0:T(8,128)}), f32[8,120,128]{2,1,0:T(8,128)S(1)}, u32[]{:S(2)}, u32[]{:S(2)}) async-start(f32[8,120,128]{2,1,0:T(8,128)} %shard_map.103), calls=%async_computation | async-start | bytes 983040 | tf_op jit(solution)/shard_map/all_to_all | solution.py:290
  10.4 0.0 copy-done.2
  10.4 2.9 %collective-permute-start.3 = (f32[1,96,256]{2,1,0:T(8,128)S(1)}, f32[1,96,256]{2,1,0:T(8,128)S(1)}, u32[]{:S(2)}, u32[]{:S(2)}) collective-permute-start(f32[1,96,256]{2,1,0:T(8,128)S(1)} %copy-done.2), channel_id=1, source_target_pairs={{0,4},{1,5},{2,6},{3,7},{4,0},{5,1},{6,2},{7,3},{8,12},{9,13},{10,... | collective-permute-start | bytes 294920 | tf_op jit(solution)/shard_map/ppermute | solution.py:300
  13.3 0.3 collective-permute-start.2
  13.6 0.6 collective-permute-start.4
  14.2 5.4 %all-to-all-done.got_ref.one_ref.two_ref.lists_ref = f32[8,120,128]{2,1,0:T(8,128)S(1)} async-done(((f32[8,120,128]{2,1,0:T(8,128)}), f32[8,120,128]{2,1,0:T(8,128)S(1)}, u32[]{:S(2)}, u32[]{:S(2)}) %all-to-all-start) | async-done | bytes 491552 | tf_op jit(solution)/shard_map/all_to_all | solution.py:290
  19.6 0.4 shard_map.104
  20.0 7.3 %collective-permute-start.1 = (f32[32,512]{1,0:T(8,128)S(1)}, f32[32,512]{1,0:T(8,128)S(1)}, u32[]{:S(2)}, u32[]{:S(2)}) collective-permute-start(f32[32,512]{1,0:T(8,128)S(1)} %get-tuple-element.22.after_ref), channel_id=1, source_target_pairs={{0,248},{8,16},{16,8},{24,32},{32,24},{40,48},{48,40},{56,64},{64,... | collective-permute-start | bytes 196616 | tf_op jit(solution)/shard_map/ppermute | solution.py:296
  27.3 0.6 shard_map.105
  27.9 3.9 %all-to-all-start.1 = ((f32[32,4,128]{2,1,0:T(4,128)}), f32[32,4,128]{2,1,0:T(4,128)S(1)}, u32[]{:S(2)}, u32[]{:S(2)}) async-start(f32[32,4,128]{2,1,0:T(4,128)} %shard_map.105), calls=%async_computation.1 | async-start | bytes 131072 | tf_op jit(solution)/shard_map/all_to_all | solution.py:290
  31.8 1.2 %collective-permute-start = (f32[32,512]{1,0:T(8,128)S(1)}, f32[32,512]{1,0:T(8,128)S(1)}, u32[]{:S(2)}, u32[]{:S(2)}) collective-permute-start(f32[32,512]{1,0:T(8,128)S(1)} %get-tuple-element.23), channel_id=1, source_target_pairs={{0,8},{8,0},{16,24},{24,16},{32,40},{40,32},{48,56},{56,48},{64,72... | collective-permute-start | bytes 196616 | tf_op jit(solution)/shard_map/ppermute | solution.py:296
  33.0 0.0 copy-start
  33.0 1.9 %copy-done = f32[1,256,3072]{2,1,0:T(8,128)S(1)} copy-done((f32[1,256,3072]{2,1,0:T(8,128)S(1)}, f32[1,256,3072]{2,1,0:T(8,128)}, u32[]{:S(2)}) %copy-start) | copy-done | bytes 3145752
  34.9 1.2 %shard_map.106 = (f32[32,256]{1,0:T(8,128)S(1)}, bf16[256,1024]{1,0:T(8,128)(2,1)S(1)}, bf16[256,1024]{1,0:T(8,128)(2,1)S(1)}) custom-call(f32[32,2048]{1,0:T(8,128)S(1)} %get-tuple-element.24.field_ref, f32[1,256,3072]{2,1,0:T(8,128)S(1)} %copy-done), custom_call_target="tpu_custom_call" | custom-call | flops 1000000000 | bytes 1024 | tf_op jit(solution)/shard_map/pallas_call | solution.py:29
  36.0 0.0 collective-permute-done.3.refs_2_
  36.0 0.0 collective-permute-done.2.refs_1_
  36.1 0.0 collective-permute-done.4.refs_3_
  36.1 0.0 collective-permute-done.a_ref
  36.1 0.0 collective-permute-done.1.b_ref
  36.1 0.6 shard_map.107
  36.7 2.3 %collective-permute-start.5 = (f32[4,96,256]{2,1,0:T(8,128)S(1)}, f32[4,96,256]{2,1,0:T(8,128)S(1)}, u32[]{:S(2)}, u32[]{:S(2)}) collective-permute-start(f32[4,96,256]{2,1,0:T(8,128)S(1)} %get-tuple-element.30.even_ref), channel_id=1, source_target_pairs={{0,1},{1,0},{2,3},{3,2},{4,5},{5,4},{6,7},{7,6},{8,9},{9,8},{10,11... | collective-permute-start | bytes 1179656 | tf_op jit(solution)/shard_map/ppermute | solution.py:300
  39.0 1.7 %all-to-all-done.1.got_ref = f32[32,4,128]{2,1,0:T(4,128)S(1)} async-done(((f32[32,4,128]{2,1,0:T(4,128)}), f32[32,4,128]{2,1,0:T(4,128)S(1)}, u32[]{:S(2)}, u32[]{:S(2)}) %all-to-all-start.1) | async-done | bytes 65568 | tf_op jit(solution)/shard_map/all_to_all | solution.py:290
  40.6 1.1 %shard_map.108 = (f32[8,32,384]{2,1,0:T(8,128)}, f32[32,128]{1,0:T(8,128)S(1)}) custom-call(f32[32,4,128]{2,1,0:T(4,128)S(1)} %all-to-all-done.1.got_ref, f32[8,120,128]{2,1,0:T(8,128)S(1)} %all-to-all-done.got_ref.one_ref.two_ref.lists_ref, f32[8,120,128]{2,1,0:T(8,128)S(1)} %all-to-all-done.got_ref.one_ref.two_ref.lists_ref, ...), custom_call_target="tpu_custom_call" | custom-call | flops 1000000000 | bytes 1024 | tf_op jit(solution)/shard_map/pallas_call | solution.py:29
  41.7 6.3 %all-to-all-start.2 = ((f32[8,32,384]{2,1,0:T(8,128)}), f32[8,32,384]{2,1,0:T(8,128)S(1)}, u32[]{:S(2)}, u32[]{:S(2)}) async-start(f32[8,32,384]{2,1,0:T(8,128)} %get-tuple-element.29), calls=%async_computation.2 | async-start | bytes 786432 | tf_op jit(solution)/shard_map/all_to_all | solution.py:290
  48.0 0.0 copy-start.3
  48.0 0.0 collective-permute-done.5.odd_ref
  48.0 8.1 %all-to-all-done.2.got_ref = f32[8,32,384]{2,1,0:T(8,128)S(1)} async-done(((f32[8,32,384]{2,1,0:T(8,128)}), f32[8,32,384]{2,1,0:T(8,128)S(1)}, u32[]{:S(2)}, u32[]{:S(2)}) %all-to-all-start.2) | async-done | bytes 393248 | tf_op jit(solution)/shard_map/all_to_all | solution.py:290
  56.1 0.0 copy-start.1
  56.1 0.7 shard_map.109
  56.8 0.6 collective-permute-start.6
  57.4 0.9 %collective-permute-start.7 = (f32[32,512]{1,0:T(8,128)S(1)}, f32[32,512]{1,0:T(8,128)S(1)}, u32[]{:S(2)}, u32[]{:S(2)}) collective-permute-start(f32[32,512]{1,0:T(8,128)S(1)} %get-tuple-element.32), channel_id=1, source_target_pairs={{0,248},{8,16},{16,8},{24,32},{32,24},{40,48},{48,40},{56,64},{64,... | collective-permute-start | bytes 196616 | tf_op jit(solution)/shard_map/ppermute | solution.py:296
  58.3 0.0 copy-done.1
  58.3 0.0 copy-start.4
  58.3 1.2 %shard_map.110 = (f32[32,256]{1,0:T(8,128)S(1)}, bf16[256,1024]{1,0:T(8,128)(2,1)S(1)}, bf16[256,1024]{1,0:T(8,128)(2,1)S(1)}) custom-call(f32[32,2048]{1,0:T(8,128)S(1)} %get-tuple-element.33.field_ref, f32[1,256,3072]{2,1,0:T(8,128)S(1)} %copy-done.1), custom_call_target="tpu_custom_call" | custom-call | flops 1000000000 | bytes 1024 | tf_op jit(solution)/shard_map/pallas_call | solution.py:29
  59.4 0.5 collective-permute-done.6.a_ref
  60.0 3.8 %collective-permute-done.7.b_ref = f32[32,512]{1,0:T(8,128)S(1)} collective-permute-done((f32[32,512]{1,0:T(8,128)S(1)}, f32[32,512]{1,0:T(8,128)S(1)}, u32[]{:S(2)}, u32[]{:S(2)}) %collective-permute-start.7) | collective-permute-done | bytes 65568 | tf_op jit(solution)/shard_map/ppermute | solution.py:296
  63.8 0.0 copy-done.3
  63.8 0.9 %shard_map.111 = (f32[32,256]{1,0:T(8,128)S(1)}, f32[256,1,128]{2,1,0:T(1,128)S(1)}) custom-call(f32[32,512]{1,0:T(8,128)S(1)} %collective-permute-done.6.a_ref, f32[32,512]{1,0:T(8,128)S(1)} %collective-permute-done.7.b_ref, f32[32,256]{1,0:T(8,128)S(1)} %get-tuple-element.34.own_ref, bf16[256,1024]{1,0:T(8,128)(2,1)S(1)} %get-tuple-element.35.high_ref, ...), custom_call_target="tpu_custom_call" | custom-call | flops 1000000000 | bytes 1024 | tf_op jit(solution)/shard_map/pallas_call | solution.py:29
  64.7 20.0 %all_to_all.20.got_ref = f32[256,1,128]{2,1,0:T(1,128)S(1)} all-to-all(f32[256,1,128]{2,1,0:T(1,128)S(1)} %get-tuple-element.38), channel_id=1, replica_groups=mesh['sub'=32,'nar'=8] {'sub','nar'}, dimensions={0} | all-to-all | bytes 262144 | tf_op jit(solution)/shard_map/all_to_all | solution.py:290
  84.6 0.0 copy-done.4
  84.7 1.2 %shard_map.112 = (f32[32,1,256]{2,1,0:T(1,128)}, f32[32,1,256]{2,1,0:T(1,128)}, f32[3,32]{1,0:T(4,128)}) custom-call(f32[256,1,128]{2,1,0:T(1,128)S(1)} %all_to_all.20.got_ref, f32[32,256]{1,0:T(8,128)S(1)} %get-tuple-element.39.image_ref, f32[32,1,256]{2,1,0:T(1,128)S(1)} %copy-done.3, f32[32,1,256]{2,1,0:T(1,128)S(1)} %copy-done.4, ...), custom_call_target="tpu_custom_call" | custom-call | flops 1000000000 | bytes 1024 | tf_op jit(solution)/shard_map/pallas_call | solution.py:29
Async XLA Ops:
  0.6 9.8 %copy-start.2 = (f32[1,96,256]{2,1,0:T(8,128)S(1)}, f32[1,96,256]{2,1,0:T(8,128)}, u32[]{:S(2)}) copy-start(f32[1,96,256]{2,1,0:T(8,128)} %refs_0_.1) | copy-start | bytes 294916
  3.8 15.8 %all-to-all-start = ((f32[8,120,128]{2,1,0:T(8,128)}), f32[8,120,128]{2,1,0:T(8,128)S(1)}, u32[]{:S(2)}, u32[]{:S(2)}) async-start(f32[8,120,128]{2,1,0:T(8,128)} %shard_map.103), calls=%async_computation | async-start | bytes 983040 | tf_op jit(solution)/shard_map/all_to_all | solution.py:290
  10.4 25.6 %collective-permute-start.3 = (f32[1,96,256]{2,1,0:T(8,128)S(1)}, f32[1,96,256]{2,1,0:T(8,128)S(1)}, u32[]{:S(2)}, u32[]{:S(2)}) collective-permute-start(f32[1,96,256]{2,1,0:T(8,128)S(1)} %copy-done.2), channel_id=1, source_target_pairs={{0,4},{1,5},{2,6},{3,7},{4,0},{5,1},{6,2},{7,3},{8,12},{9,13},{10,... | collective-permute-start | bytes 294920 | tf_op jit(solution)/shard_map/ppermute | solution.py:300
  13.3 22.7 %collective-permute-start.2 = (f32[1,96,256]{2,1,0:T(8,128)S(1)}, f32[1,96,256]{2,1,0:T(8,128)S(1)}, u32[]{:S(2)}, u32[]{:S(2)}) collective-permute-start(f32[1,96,256]{2,1,0:T(8,128)S(1)} %copy-done.2), channel_id=1, source_target_pairs={{0,2},{1,3},{2,0},{3,1},{4,6},{5,7},{6,4},{7,5},{8,10},{9,11},{10,... | collective-permute-start | bytes 294920 | tf_op jit(solution)/shard_map/ppermute | solution.py:300
  13.6 22.5 %collective-permute-start.4 = (f32[1,96,256]{2,1,0:T(8,128)S(1)}, f32[1,96,256]{2,1,0:T(8,128)S(1)}, u32[]{:S(2)}, u32[]{:S(2)}) collective-permute-start(f32[1,96,256]{2,1,0:T(8,128)S(1)} %copy-done.2), channel_id=1, source_target_pairs={{0,6},{1,7},{2,4},{3,5},{4,2},{5,3},{6,0},{7,1},{8,14},{9,15},{10,... | collective-permute-start | bytes 294920 | tf_op jit(solution)/shard_map/ppermute | solution.py:300
  20.0 16.1 %collective-permute-start.1 = (f32[32,512]{1,0:T(8,128)S(1)}, f32[32,512]{1,0:T(8,128)S(1)}, u32[]{:S(2)}, u32[]{:S(2)}) collective-permute-start(f32[32,512]{1,0:T(8,128)S(1)} %get-tuple-element.22.after_ref), channel_id=1, source_target_pairs={{0,248},{8,16},{16,8},{24,32},{32,24},{40,48},{48,40},{56,64},{64,... | collective-permute-start | bytes 196616 | tf_op jit(solution)/shard_map/ppermute | solution.py:296
  27.9 12.7 %all-to-all-start.1 = ((f32[32,4,128]{2,1,0:T(4,128)}), f32[32,4,128]{2,1,0:T(4,128)S(1)}, u32[]{:S(2)}, u32[]{:S(2)}) async-start(f32[32,4,128]{2,1,0:T(4,128)} %shard_map.105), calls=%async_computation.1 | async-start | bytes 131072 | tf_op jit(solution)/shard_map/all_to_all | solution.py:290
  31.8 4.3 %collective-permute-start = (f32[32,512]{1,0:T(8,128)S(1)}, f32[32,512]{1,0:T(8,128)S(1)}, u32[]{:S(2)}, u32[]{:S(2)}) collective-permute-start(f32[32,512]{1,0:T(8,128)S(1)} %get-tuple-element.23), channel_id=1, source_target_pairs={{0,8},{8,0},{16,24},{24,16},{32,40},{40,32},{48,56},{56,48},{64,72... | collective-permute-start | bytes 196616 | tf_op jit(solution)/shard_map/ppermute | solution.py:296
  33.0 1.9 %copy-start = (f32[1,256,3072]{2,1,0:T(8,128)S(1)}, f32[1,256,3072]{2,1,0:T(8,128)}, u32[]{:S(2)}) copy-start(f32[1,256,3072]{2,1,0:T(8,128)} %mat_ref.2) | copy-start | bytes 9437188
  36.7 11.3 %collective-permute-start.5 = (f32[4,96,256]{2,1,0:T(8,128)S(1)}, f32[4,96,256]{2,1,0:T(8,128)S(1)}, u32[]{:S(2)}, u32[]{:S(2)}) collective-permute-start(f32[4,96,256]{2,1,0:T(8,128)S(1)} %get-tuple-element.30.even_ref), channel_id=1, source_target_pairs={{0,1},{1,0},{2,3},{3,2},{4,5},{5,4},{6,7},{7,6},{8,9},{9,8},{10,11... | collective-permute-start | bytes 1179656 | tf_op jit(solution)/shard_map/ppermute | solution.py:300
  41.7 14.4 %all-to-all-start.2 = ((f32[8,32,384]{2,1,0:T(8,128)}), f32[8,32,384]{2,1,0:T(8,128)S(1)}, u32[]{:S(2)}, u32[]{:S(2)}) async-start(f32[8,32,384]{2,1,0:T(8,128)} %get-tuple-element.29), calls=%async_computation.2 | async-start | bytes 786432 | tf_op jit(solution)/shard_map/all_to_all | solution.py:290
  48.0 15.8 %copy-start.3 = (f32[32,1,256]{2,1,0:T(1,128)S(1)}, f32[32,1,256]{2,1,0:T(1,128)}, u32[]{:S(2)}) copy-start(f32[32,1,256]{2,1,0:T(1,128)} %res_ref.3) | copy-start | bytes 98308
  56.1 2.2 %copy-start.1 = (f32[1,256,3072]{2,1,0:T(8,128)S(1)}, f32[1,256,3072]{2,1,0:T(8,128)}, u32[]{:S(2)}) copy-start(f32[1,256,3072]{2,1,0:T(8,128)} %mat_ref.3) | copy-start | bytes 9437188
  56.8 3.2 %collective-permute-start.6 = (f32[32,512]{1,0:T(8,128)S(1)}, f32[32,512]{1,0:T(8,128)S(1)}, u32[]{:S(2)}, u32[]{:S(2)}) collective-permute-start(f32[32,512]{1,0:T(8,128)S(1)} %get-tuple-element.31), channel_id=1, source_target_pairs={{0,8},{8,0},{16,24},{24,16},{32,40},{40,32},{48,56},{56,48},{64,72... | collective-permute-start | bytes 196616 | tf_op jit(solution)/shard_map/ppermute | solution.py:296
  57.4 6.4 %collective-permute-start.7 = (f32[32,512]{1,0:T(8,128)S(1)}, f32[32,512]{1,0:T(8,128)S(1)}, u32[]{:S(2)}, u32[]{:S(2)}) collective-permute-start(f32[32,512]{1,0:T(8,128)S(1)} %get-tuple-element.32), channel_id=1, source_target_pairs={{0,248},{8,16},{16,8},{24,32},{32,24},{40,48},{48,40},{56,64},{64,... | collective-permute-start | bytes 196616 | tf_op jit(solution)/shard_map/ppermute | solution.py:296
  58.3 26.4 %copy-start.4 = (f32[32,1,256]{2,1,0:T(1,128)S(1)}, f32[32,1,256]{2,1,0:T(1,128)}, u32[]{:S(2)}) copy-start(f32[32,1,256]{2,1,0:T(1,128)} %iter_ref.1) | copy-start | bytes 98308

commit v4 on v3

--- a/solution.py
+++ b/solution.py
@@ -140,14 +140,15 @@
     return exactly(pick, inverse, NN, False).T
 
 
-def weave(ends, a_ref, b_ref):
+def weave(ends, out_ref):
     half = LANES // 2
+    core = lax.axis_index("nar") % 2
+    low = iota(ends[0].shape, 1) < half
     for i in range(0, len(ends), 2):
         one, two = ends[i], ends[i + 1]
-        low = iota(one.shape, 1) < half
-        at = slice(i * half, i * half + LANES)
-        a_ref[:, at] = jnp.where(low, one, pltpu.roll(two, half, 1))
-        b_ref[:, at] = jnp.where(low, pltpu.roll(one, half, 1), two)
+        first = jnp.where(low, one, pltpu.roll(two, half, 1))
+        second = jnp.where(low, pltpu.roll(one, half, 1), two)
+        out_ref[:, i * half : i * half + LANES] = jnp.where(core == 0, first, second)
 
 
 def sum_kernel(got_ref, after_ref, out_ref):
@@ -156,7 +157,7 @@
     out_ref[...] = jnp.broadcast_to(total[None], out_ref.shape)
 
 
-def middle_kernel(got_ref, own_ref, a_ref, b_ref):
+def middle_kernel(got_ref, own_ref, send_ref):
     n, _, lanes = got_ref.shape
     k = own_ref.shape[0]
     rdev = own_ref.shape[1] // n
@@ -168,15 +169,16 @@
         own_ref[:, c * rdev : (c + 1) * rdev] = field
         listed = got_ref[c, at + 4 : at + 5, :]
         ends.append(exactly(pick_of(listed, rdev), field, NN, False))
-    weave(ends, a_ref, b_ref)
-
-
-def margins(a_ref, b_ref):
+    weave(ends, send_ref)
+
+
+def margins(got_ref, other_ref):
     sub, nsub = lax.axis_index("sub"), lax.axis_size("sub")
-    even = sub % 2 == 0
-    a, b = a_ref[...], b_ref[...]
-    lefts = jnp.where(sub == 0, 0.0, jnp.where(even, b, a))
-    rights = jnp.where(sub == nsub - 1, 0.0, jnp.where(even, a, b))
+    core = lax.axis_index("nar") % 2
+    right = sub % 2 == core
+    got, other = got_ref[...], other_ref[...]
+    lefts = jnp.where(sub == 0, 0.0, jnp.where(right, other, got))
+    rights = jnp.where(sub == nsub - 1, 0.0, jnp.where(right, got, other))
     return lefts, rights
 
 
@@ -226,7 +228,7 @@
     beta_ref[...] = jnp.broadcast_to(beta, beta_ref.shape)
 
 
-def precond_kernel(got_ref, lists_ref, count_ref, even_ref, odd_ref, own_ref, a_ref, b_ref, mine_ref):
+def precond_kernel(got_ref, lists_ref, count_ref, even_ref, odd_ref, own_ref, send_ref, mine_ref):
     n, k, width = got_ref.shape
     rdev = width - LANES
     maxev = even_ref.shape[1]
@@ -242,7 +244,7 @@
         exactly(pick_of(lists_ref[c, 4:5, :], rdev), own_ref[:, c * rdev : (c + 1) * rdev], NN, False)
         for c in range(n)
     ]
-    weave(ends, a_ref, b_ref)
+    weave(ends, send_ref)
 
 
 def ratio(a, n):
@@ -290,10 +292,17 @@
     return lax.all_to_all(blocks, axes, 0, 0)
 
 
-def beside(first, second, nsub):
-    route_a = [(i, i ^ 1) for i in range(nsub)]
-    route_b = [(i, (i + 1 if i % 2 else i - 1) % nsub) for i in range(nsub)]
-    return lax.ppermute(first, "sub", route_a), lax.ppermute(second, "sub", route_b)
+def beside(block, nsub, nnar):
+    def partner(sub, nar):
+        if nar % 2 == 0:
+            return sub ^ 1
+        return (sub + 1 if sub % 2 else sub - 1) % nsub
+
+    route = [
+        (sub * nnar + nar, partner(sub, nar) * nnar + nar) for sub in range(nsub) for nar in range(nnar)
+    ]
+    got = lax.ppermute(block, ("sub", "nar"), route)
+    return got, across(got, nnar, 1)
 
 
 def across(block, n, mask):
@@ -341,20 +350,20 @@
     )
     part = exchange(part, "nar")
     lists = pl.BlockSpec((nnar, 8, LANES), lambda i: (0, head // 8, 0))
-    pieces = (shape(k, own), shape(k, nnar * over), shape(k, nnar * over))
-    r_own, to_a, to_b = local_call(
+    pieces = (shape(k, own), shape(k, nnar * over))
+    r_own, send = local_call(
         middle_kernel, pieces, part,
         specs={0: pl.BlockSpec((nnar, head + 8, LANES), lambda i: (0, 0, 0))},
     )
     res = local_call(
-        sum_kernel, shape(nsub, pad, LANES), part, to_b, specs={0: lists, 1: hbm}, cost=10
+        sum_kernel, shape(nsub, pad, LANES), part, send, specs={0: lists, 1: hbm}, cost=10
     )
     res = exchange(res, "sub")
 
-    got_a, got_b = beside(to_a, to_b, nsub)
+    got = beside(send, nsub, nnar)
     local, vecs = local_call(
         local_kernel, (shape(k, rdev), shape(nnar // 2, maxev, rdev)),
-        got_a, got_b, *product(r_own, local_inverse), *vecs,
+        *got, *product(r_own, local_inverse), *vecs,
     )
     vecs = (vecs, across(vecs, nnar, 1))
 
@@ -369,15 +378,15 @@
         scratch=[pltpu.VMEM((nsub * pad, ncol * LANES), F32)],
     )
     block = exchange(block, "nar")
-    p_own, to_a, to_b, precond = local_call(
+    p_own, send, precond = local_call(
         precond_kernel, pieces + (shape(k, rdev),), block, part, ev_count, *vecs,
         specs={1: lists, 2: smem},
     )
 
-    got_a, got_b = beside(to_a, to_b, nsub)
+    got = beside(send, nsub, nnar)
     image, stats = local_call(
         image_kernel, (shape(k, rdev), shape(nsub * nnar, 1, LANES)),
-        got_a, got_b, *product(p_own, stiffness), residual, beta,
+        *got, *product(p_own, stiffness), residual, beta,
     )
     stats = exchange(stats, ("sub", "nar"))
     return local_call(

time: 86.3 us -> 84.7 us (0.981)
  blocking collectives: 20 us -> 32.8 us
  starting transfers between devices: 32.8 us -> 24.6 us
  waiting for transfers between devices: 19.6 us -> 14.1 us
    all_to_all x1 -> x2, blocking collectives: 20 us -> 32.8 us  [exchange(): return lax.all_to_all(blocks, axes, 0, 0)]
    all_to_all x3 -> x2, waiting for transfers between devices: 15.2 us -> 8.37 us  [exchange(): return lax.all_to_all(blocks, axes, 0, 0)]
    all_to_all x3 -> x2, starting transfers between devices: 16.7 us -> 10.5 us  [exchange(): return lax.all_to_all(blocks, axes, 0, 0)]
    ppermute x4 -> x2, starting transfers between devices: 9.93 us -> 8.17 us  [beside(): got = lax.ppermute(block, ('sub', 'nar'), route)]
    ppermute x4 -> x2, waiting for transfers between devices: 4.39 us -> 5.62 us  [beside(): got = lax.ppermute(block, ('sub', 'nar'), route)]
    ppermute x4 -> x6, starting transfers between devices: 6.1 us -> 5.99 us  [across(): return lax.ppermute(block, 'nar', [(i, i ^ mask) for i in range(n)])]
  transfers between devices with their start and end apart: 11 -> 10, of which waited for: 5 -> 4; matrix products, arithmetic and copies ran while one was open for 0% -> 0% of each run, Pallas kernels for 6% -> 5%
where the time goes in v4:
time: 84.7 us; the launch traced here: 84.3 us
  blocking collectives  32.8 us (39%)
  starting transfers between devices  24.6 us (29%)
  waiting for transfers between devices  14.1 us (17%)
  Pallas kernels  9.47 us (11%)
  local copies, waits for them, and re-layouts  1.91 us (2%)
  between operations  1.43 us (2%)
    all_to_all x2, blocking collectives, exchange(): return lax.all_to_all(blocks, axes, 0, 0)  32.8 us
    all_to_all x2, starting transfers between devices, exchange(): return lax.all_to_all(blocks, axes, 0, 0)  10.5 us
    pallas_call x10, Pallas kernels, local_call(): pl.pallas_call(body, grid=(1,), out_shape=outs, in_specs=[specs.get(i) or...  9.47 us
    all_to_all x2, waiting for transfers between devices, exchange(): return lax.all_to_all(blocks, axes, 0, 0)  8.37 us
    ppermute x2, starting transfers between devices, beside(): got = lax.ppermute(block, ('sub', 'nar'), route)  8.17 us
    ppermute x6, starting transfers between devices, across(): return lax.ppermute(block, 'nar', [(i, i ^ mask) for i in range(n)])  5.99 us
    ppermute x2, waiting for transfers between devices, beside(): got = lax.ppermute(block, ('sub', 'nar'), route)  5.62 us
    unnamed x10, local copies, waits for them, and re-layouts  1.91 us
  transfers between devices with their start and end apart: 10, of which 4 were waited for; matrix products, arithmetic and copies ran while one was open for 0% of the time, Pallas kernels for 5%

profile of v4, /device:TPU:1, one launch (start us, length us, event | category | flops | bytes accessed | tf_op | source)
XLA Modules:
  0.0 84.3 jit_solution(415561977012237389)
XLA Ops:
  0.6 0.0 copy-start.2
  1.3 2.4 %shard_map.103 = f32[8,120,128]{2,1,0:T(8,128)} custom-call(f32[32,1,256]{2,1,0:T(1,128)} %res_ref.3, f32[1,96,256]{2,1,0:T(8,128)} %refs_0_.1, f32[96,384]{1,0:T(8,128)} %inv_hbm.1, s32[2,1,64]{2,1,0:T(1,128)} %rows_hbm.1, s32[1]{0:T(128)S(6)} %copy.11.count_ref), custom_call_target="tpu_custom_call" | custom-call | flops 1000000000 | bytes 1024 | tf_op jit(solution)/shard_map/pallas_call | solution.py:29
  3.8 6.6 %all-to-all-start = ((f32[8,120,128]{2,1,0:T(8,128)}), f32[8,120,128]{2,1,0:T(8,128)S(1)}, u32[]{:S(2)}, u32[]{:S(2)}) async-start(f32[8,120,128]{2,1,0:T(8,128)} %shard_map.103), calls=%async_computation | async-start | bytes 983040 | tf_op jit(solution)/shard_map/all_to_all | solution.py:292
  10.4 0.0 copy-done.2
  10.4 2.9 %collective-permute-start.3 = (f32[1,96,256]{2,1,0:T(8,128)S(1)}, f32[1,96,256]{2,1,0:T(8,128)S(1)}, u32[]{:S(2)}, u32[]{:S(2)}) collective-permute-start(f32[1,96,256]{2,1,0:T(8,128)S(1)} %copy-done.2), channel_id=1, source_target_pairs={{0,4},{1,5},{2,6},{3,7},{4,0},{5,1},{6,2},{7,3},{8,12},{9,13},{10,... | collective-permute-start | bytes 294920 | tf_op jit(solution)/shard_map/ppermute | solution.py:309
  13.3 0.3 collective-permute-start.2
  13.6 0.6 collective-permute-start.4
  14.2 5.4 %all-to-all-done.got_ref.one_ref.two_ref.lists_ref = f32[8,120,128]{2,1,0:T(8,128)S(1)} async-done(((f32[8,120,128]{2,1,0:T(8,128)}), f32[8,120,128]{2,1,0:T(8,128)S(1)}, u32[]{:S(2)}, u32[]{:S(2)}) %all-to-all-start) | async-done | bytes 491552 | tf_op jit(solution)/shard_map/all_to_all | solution.py:292
  19.6 0.4 shard_map.104
  20.0 7.3 %collective-permute-start = (f32[32,512]{1,0:T(8,128)S(1)}, f32[32,512]{1,0:T(8,128)S(1)}, u32[]{:S(2)}, u32[]{:S(2)}) collective-permute-start(f32[32,512]{1,0:T(8,128)S(1)} %get-tuple-element.20.after_ref), channel_id=1, source_target_pairs={{0,8},{1,249},{2,10},{3,251},{4,12},{5,253},{6,14},{7,255},{8,0},{... | collective-permute-start | bytes 196616 | tf_op jit(solution)/shard_map/ppermute | solution.py:304
  27.3 0.6 shard_map.105
  27.9 3.8 %all-to-all-start.1 = ((f32[32,4,128]{2,1,0:T(4,128)}), f32[32,4,128]{2,1,0:T(4,128)S(1)}, u32[]{:S(2)}, u32[]{:S(2)}) async-start(f32[32,4,128]{2,1,0:T(4,128)} %shard_map.105), calls=%async_computation.1 | async-start | bytes 131072 | tf_op jit(solution)/shard_map/all_to_all | solution.py:292
  31.8 0.0 collective-permute-done.a_ref
  31.8 2.1 %collective-permute-start.1 = (f32[32,512]{1,0:T(8,128)S(1)}, f32[32,512]{1,0:T(8,128)S(1)}, u32[]{:S(2)}, u32[]{:S(2)}) collective-permute-start(f32[32,512]{1,0:T(8,128)S(1)} %collective-permute-done.a_ref), channel_id=1, source_target_pairs={{0,1},{1,0},{2,3},{3,2},{4,5},{5,4},{6,7},{7,6},{8,9},{9,8},{10,11... | collective-permute-start | bytes 196616 | tf_op jit(solution)/shard_map/ppermute | solution.py:309
  33.9 0.0 copy-start
  33.9 1.9 %copy-done = f32[1,256,3072]{2,1,0:T(8,128)S(1)} copy-done((f32[1,256,3072]{2,1,0:T(8,128)S(1)}, f32[1,256,3072]{2,1,0:T(8,128)}, u32[]{:S(2)}) %copy-start) | copy-done | bytes 3145752
  35.8 1.2 %shard_map.106 = (f32[32,256]{1,0:T(8,128)S(1)}, bf16[256,1024]{1,0:T(8,128)(2,1)S(1)}, bf16[256,1024]{1,0:T(8,128)(2,1)S(1)}) custom-call(f32[32,2048]{1,0:T(8,128)S(1)} %get-tuple-element.21.field_ref, f32[1,256,3072]{2,1,0:T(8,128)S(1)} %copy-done), custom_call_target="tpu_custom_call" | custom-call | flops 1000000000 | bytes 1024 | tf_op jit(solution)/shard_map/pallas_call | solution.py:29
  37.0 0.0 collective-permute-done.3.refs_2_
  37.0 0.0 collective-permute-done.2.refs_1_
  37.0 0.0 collective-permute-done.4.refs_3_
  37.0 0.0 collective-permute-done.1.b_ref
  37.0 0.6 shard_map.107
  37.6 0.1 collective-permute-start.5
  37.6 3.0 %all-to-all-done.1.got_ref = f32[32,4,128]{2,1,0:T(4,128)S(1)} async-done(((f32[32,4,128]{2,1,0:T(4,128)}), f32[32,4,128]{2,1,0:T(4,128)S(1)}, u32[]{:S(2)}, u32[]{:S(2)}) %all-to-all-start.1) | async-done | bytes 65568 | tf_op jit(solution)/shard_map/all_to_all | solution.py:292
  40.6 0.3 shard_map.108
  41.0 0.0 copy-start.1
  41.0 14.7 %all_to_all.20.got_ref = f32[8,32,384]{2,1,0:T(8,128)S(1)} all-to-all(f32[8,32,384]{2,1,0:T(8,128)S(1)} %get-tuple-element.26), channel_id=1, replica_groups=mesh['sub'=32,'nar'=8] {'nar'}, dimensions={0} | all-to-all | bytes 786432 | tf_op jit(solution)/shard_map/all_to_all | solution.py:292
  55.7 0.0 copy-start.3
  55.7 0.0 collective-permute-done.5.odd_ref
  55.7 0.7 shard_map.109
  56.4 0.9 %collective-permute-start.6 = (f32[32,512]{1,0:T(8,128)S(1)}, f32[32,512]{1,0:T(8,128)S(1)}, u32[]{:S(2)}, u32[]{:S(2)}) collective-permute-start(f32[32,512]{1,0:T(8,128)S(1)} %get-tuple-element.28), channel_id=1, source_target_pairs={{0,8},{1,249},{2,10},{3,251},{4,12},{5,253},{6,14},{7,255},{8,0},{... | collective-permute-start | bytes 196616 | tf_op jit(solution)/shard_map/ppermute | solution.py:304
  57.3 5.6 %collective-permute-done.6.a_ref = f32[32,512]{1,0:T(8,128)S(1)} collective-permute-done((f32[32,512]{1,0:T(8,128)S(1)}, f32[32,512]{1,0:T(8,128)S(1)}, u32[]{:S(2)}, u32[]{:S(2)}) %collective-permute-start.6) | collective-permute-done | bytes 65568 | tf_op jit(solution)/shard_map/ppermute | solution.py:304
  62.9 0.0 collective-permute-start.7
  62.9 0.0 copy-done.1
  62.9 0.0 copy-start.4
  62.9 1.2 %shard_map.110 = (f32[32,256]{1,0:T(8,128)S(1)}, bf16[256,1024]{1,0:T(8,128)(2,1)S(1)}, bf16[256,1024]{1,0:T(8,128)(2,1)S(1)}) custom-call(f32[32,2048]{1,0:T(8,128)S(1)} %get-tuple-element.29.field_ref, f32[1,256,3072]{2,1,0:T(8,128)S(1)} %copy-done.1), custom_call_target="tpu_custom_call" | custom-call | flops 1000000000 | bytes 1024 | tf_op jit(solution)/shard_map/pallas_call | solution.py:29
  64.1 0.1 collective-permute-done.7.b_ref
  64.2 0.0 copy-done.3
  64.2 0.9 %shard_map.111 = (f32[32,256]{1,0:T(8,128)S(1)}, f32[256,1,128]{2,1,0:T(1,128)S(1)}) custom-call(f32[32,512]{1,0:T(8,128)S(1)} %collective-permute-done.6.a_ref, f32[32,512]{1,0:T(8,128)S(1)} %collective-permute-done.7.b_ref, f32[32,256]{1,0:T(8,128)S(1)} %get-tuple-element.30.own_ref, bf16[256,1024]{1,0:T(8,128)(2,1)S(1)} %get-tuple-element.31.high_ref, ...), custom_call_target="tpu_custom_call" | custom-call | flops 1000000000 | bytes 1024 | tf_op jit(solution)/shard_map/pallas_call | solution.py:29
  65.0 18.1 %all_to_all.21.got_ref = f32[256,1,128]{2,1,0:T(1,128)S(1)} all-to-all(f32[256,1,128]{2,1,0:T(1,128)S(1)} %get-tuple-element.34), channel_id=1, replica_groups=mesh['sub'=32,'nar'=8] {'sub','nar'}, dimensions={0} | all-to-all | bytes 262144 | tf_op jit(solution)/shard_map/all_to_all | solution.py:292
  83.1 0.0 copy-done.4
  83.1 1.2 %shard_map.112 = (f32[32,1,256]{2,1,0:T(1,128)}, f32[32,1,256]{2,1,0:T(1,128)}, f32[3,32]{1,0:T(4,128)}) custom-call(f32[256,1,128]{2,1,0:T(1,128)S(1)} %all_to_all.21.got_ref, f32[32,256]{1,0:T(8,128)S(1)} %get-tuple-element.35.image_ref, f32[32,1,256]{2,1,0:T(1,128)S(1)} %copy-done.3, f32[32,1,256]{2,1,0:T(1,128)S(1)} %copy-done.4, ...), custom_call_target="tpu_custom_call" | custom-call | flops 1000000000 | bytes 1024 | tf_op jit(solution)/shard_map/pallas_call | solution.py:29
Async XLA Ops:
  0.6 9.8 %copy-start.2 = (f32[1,96,256]{2,1,0:T(8,128)S(1)}, f32[1,96,256]{2,1,0:T(8,128)}, u32[]{:S(2)}) copy-start(f32[1,96,256]{2,1,0:T(8,128)} %refs_0_.1) | copy-start | bytes 294916
  3.8 15.8 %all-to-all-start = ((f32[8,120,128]{2,1,0:T(8,128)}), f32[8,120,128]{2,1,0:T(8,128)S(1)}, u32[]{:S(2)}, u32[]{:S(2)}) async-start(f32[8,120,128]{2,1,0:T(8,128)} %shard_map.103), calls=%async_computation | async-start | bytes 983040 | tf_op jit(solution)/shard_map/all_to_all | solution.py:292
  10.4 26.6 %collective-permute-start.3 = (f32[1,96,256]{2,1,0:T(8,128)S(1)}, f32[1,96,256]{2,1,0:T(8,128)S(1)}, u32[]{:S(2)}, u32[]{:S(2)}) collective-permute-start(f32[1,96,256]{2,1,0:T(8,128)S(1)} %copy-done.2), channel_id=1, source_target_pairs={{0,4},{1,5},{2,6},{3,7},{4,0},{5,1},{6,2},{7,3},{8,12},{9,13},{10,... | collective-permute-start | bytes 294920 | tf_op jit(solution)/shard_map/ppermute | solution.py:309
  13.3 23.7 %collective-permute-start.2 = (f32[1,96,256]{2,1,0:T(8,128)S(1)}, f32[1,96,256]{2,1,0:T(8,128)S(1)}, u32[]{:S(2)}, u32[]{:S(2)}) collective-permute-start(f32[1,96,256]{2,1,0:T(8,128)S(1)} %copy-done.2), channel_id=1, source_target_pairs={{0,2},{1,3},{2,0},{3,1},{4,6},{5,7},{6,4},{7,5},{8,10},{9,11},{10,... | collective-permute-start | bytes 294920 | tf_op jit(solution)/shard_map/ppermute | solution.py:309
  13.6 23.4 %collective-permute-start.4 = (f32[1,96,256]{2,1,0:T(8,128)S(1)}, f32[1,96,256]{2,1,0:T(8,128)S(1)}, u32[]{:S(2)}, u32[]{:S(2)}) collective-permute-start(f32[1,96,256]{2,1,0:T(8,128)S(1)} %copy-done.2), channel_id=1, source_target_pairs={{0,6},{1,7},{2,4},{3,5},{4,2},{5,3},{6,0},{7,1},{8,14},{9,15},{10,... | collective-permute-start | bytes 294920 | tf_op jit(solution)/shard_map/ppermute | solution.py:309
  20.0 11.8 %collective-permute-start = (f32[32,512]{1,0:T(8,128)S(1)}, f32[32,512]{1,0:T(8,128)S(1)}, u32[]{:S(2)}, u32[]{:S(2)}) collective-permute-start(f32[32,512]{1,0:T(8,128)S(1)} %get-tuple-element.20.after_ref), channel_id=1, source_target_pairs={{0,8},{1,249},{2,10},{3,251},{4,12},{5,253},{6,14},{7,255},{8,0},{... | collective-permute-start | bytes 196616 | tf_op jit(solution)/shard_map/ppermute | solution.py:304
  27.9 12.7 %all-to-all-start.1 = ((f32[32,4,128]{2,1,0:T(4,128)}), f32[32,4,128]{2,1,0:T(4,128)S(1)}, u32[]{:S(2)}, u32[]{:S(2)}) async-start(f32[32,4,128]{2,1,0:T(4,128)} %shard_map.105), calls=%async_computation.1 | async-start | bytes 131072 | tf_op jit(solution)/shard_map/all_to_all | solution.py:292
  31.8 5.2 %collective-permute-start.1 = (f32[32,512]{1,0:T(8,128)S(1)}, f32[32,512]{1,0:T(8,128)S(1)}, u32[]{:S(2)}, u32[]{:S(2)}) collective-permute-start(f32[32,512]{1,0:T(8,128)S(1)} %collective-permute-done.a_ref), channel_id=1, source_target_pairs={{0,1},{1,0},{2,3},{3,2},{4,5},{5,4},{6,7},{7,6},{8,9},{9,8},{10,11... | collective-permute-start | bytes 196616 | tf_op jit(solution)/shard_map/ppermute | solution.py:309
  33.9 1.9 %copy-start = (f32[1,256,3072]{2,1,0:T(8,128)S(1)}, f32[1,256,3072]{2,1,0:T(8,128)}, u32[]{:S(2)}) copy-start(f32[1,256,3072]{2,1,0:T(8,128)} %mat_ref.2) | copy-start | bytes 9437188
  37.6 18.1 %collective-permute-start.5 = (f32[4,96,256]{2,1,0:T(8,128)S(1)}, f32[4,96,256]{2,1,0:T(8,128)S(1)}, u32[]{:S(2)}, u32[]{:S(2)}) collective-permute-start(f32[4,96,256]{2,1,0:T(8,128)S(1)} %get-tuple-element.27.even_ref), channel_id=1, source_target_pairs={{0,1},{1,0},{2,3},{3,2},{4,5},{5,4},{6,7},{7,6},{8,9},{9,8},{10,11... | collective-permute-start | bytes 1179656 | tf_op jit(solution)/shard_map/ppermute | solution.py:309
  41.0 22.0 %copy-start.1 = (f32[1,256,3072]{2,1,0:T(8,128)S(1)}, f32[1,256,3072]{2,1,0:T(8,128)}, u32[]{:S(2)}) copy-start(f32[1,256,3072]{2,1,0:T(8,128)} %mat_ref.3) | copy-start | bytes 9437188
  55.7 8.5 %copy-start.3 = (f32[32,1,256]{2,1,0:T(1,128)S(1)}, f32[32,1,256]{2,1,0:T(1,128)}, u32[]{:S(2)}) copy-start(f32[32,1,256]{2,1,0:T(1,128)} %res_ref.3) | copy-start | bytes 98308
  56.4 6.5 %collective-permute-start.6 = (f32[32,512]{1,0:T(8,128)S(1)}, f32[32,512]{1,0:T(8,128)S(1)}, u32[]{:S(2)}, u32[]{:S(2)}) collective-permute-start(f32[32,512]{1,0:T(8,128)S(1)} %get-tuple-element.28), channel_id=1, source_target_pairs={{0,8},{1,249},{2,10},{3,251},{4,12},{5,253},{6,14},{7,255},{8,0},{... | collective-permute-start | bytes 196616 | tf_op jit(solution)/shard_map/ppermute | solution.py:304
  62.9 1.3 %collective-permute-start.7 = (f32[32,512]{1,0:T(8,128)S(1)}, f32[32,512]{1,0:T(8,128)S(1)}, u32[]{:S(2)}, u32[]{:S(2)}) collective-permute-start(f32[32,512]{1,0:T(8,128)S(1)} %collective-permute-done.6.a_ref), channel_id=1, source_target_pairs={{0,1},{1,0},{2,3},{3,2},{4,5},{5,4},{6,7},{7,6},{8,9},{9,8},{10,11... | collective-permute-start | bytes 196616 | tf_op jit(solution)/shard_map/ppermute | solution.py:309
  62.9 20.2 %copy-start.4 = (f32[32,1,256]{2,1,0:T(1,128)S(1)}, f32[32,1,256]{2,1,0:T(1,128)}, u32[]{:S(2)}) copy-start(f32[32,1,256]{2,1,0:T(1,128)} %iter_ref.1) | copy-start | bytes 98308

commit v5 on v4

--- a/solution.py
+++ b/solution.py
@@ -8,6 +8,7 @@
 from jax.sharding import PartitionSpec as P
 
 EPS = 1e-06
+COSTS = {'middle_kernel': 0.01, 'product_kernel': 3, 'half_kernel': 1, 'rest_kernel': 1, 'local_kernel': 0.3, 'solve_kernel': 3, 'begin_kernel': 0.3}
 F32, BF16 = jnp.float32, jnp.bfloat16
 LANES = 128
 NT = (((1,), (1,)), ((), ()))
@@ -23,7 +24,9 @@
     return pl.BlockSpec(x.shape, lambda i: zeros)
 
 
-def local_call(body, outs, *args, specs=None, scratch=(), limit=4, cost=1):
+def local_call(body, outs, *args, specs=None, scratch=(), limit=6, cost=1):
+    body_name = getattr(body, "func", body).__name__
+    cost = COSTS.get(body_name, cost)
     many = isinstance(outs, tuple)
     specs = specs or {}
     return pl.pallas_call(
@@ -151,18 +154,15 @@
         out_ref[:, i * half : i * half + LANES] = jnp.where(core == 0, first, second)
 
 
-def sum_kernel(got_ref, after_ref, out_ref):
-    del after_ref
-    total = jnp.sum(got_ref[...], axis=0)[: out_ref.shape[1]]
-    out_ref[...] = jnp.broadcast_to(total[None], out_ref.shape)
-
-
-def middle_kernel(got_ref, own_ref, send_ref):
+def middle_kernel(got_ref, res_ref, own_ref, send_ref):
     n, _, lanes = got_ref.shape
+    pad = res_ref.shape[1]
     k = own_ref.shape[0]
     rdev = own_ref.shape[1] // n
     halves_of = rdev // lanes
     at = halves_of * k
+    total = jnp.sum(got_ref[:, at : at + 8, :], axis=0)[:pad]
+    res_ref[...] = jnp.broadcast_to(total[None], res_ref.shape)
     ends = []
     for c in range(n):
         field = jnp.concatenate([got_ref[c, i * k : (i + 1) * k, :] for i in range(halves_of)], axis=1)
@@ -186,6 +186,15 @@
     own = field_ref.shape[1]
     out_ref[...] = dot3(field_ref[...], mat_ref[0, :, :own], NT)
     high_ref[...], low_ref[...] = halves(mat_ref[0, :, own:])
+
+
+def half_kernel(field_ref, mat_ref, out_ref):
+    out_ref[...] = dot3(field_ref[...], mat_ref[0], NT)
+
+
+def rest_kernel(field_ref, mat_ref, edge_ref, before_ref, out_ref, high_ref, low_ref):
+    out_ref[...] = before_ref[...] + dot3(field_ref[...], mat_ref[0], NT)
+    high_ref[...], low_ref[...] = halves(edge_ref[0])
 
 
 def margin_product(a_ref, b_ref, high_ref, low_ref):
@@ -315,6 +324,27 @@
     return local_call(product_kernel, (shape(field.shape[0], rdev), split, split), field, matrix, limit=10)
 
 
+def product_in_two(field, matrix):
+    k, own = field.shape
+    rdev, ext = matrix.shape[1:]
+    half = own // 2
+    split = jax.ShapeDtypeStruct((rdev, ext - own), BF16)
+
+    def columns(at):
+        return pl.BlockSpec((1, rdev, half), lambda i: (0, 0, at))
+
+    def rows(at):
+        return pl.BlockSpec((k, half), lambda i: (0, at))
+
+    first = local_call(
+        half_kernel, shape(k, rdev), field, matrix, specs={0: rows(0), 1: columns(0)}, limit=8
+    )
+    return local_call(
+        rest_kernel, (shape(k, rdev), split, split), field, matrix, matrix, first,
+        specs={0: rows(1), 1: columns(1), 2: columns(2)}, limit=10,
+    )
+
+
 def per_device(
     residual, iterate, stiffness, local_inverse, eigvecs, ev_count, coarse_inverse, send_rows
 ):
@@ -346,24 +376,21 @@
             pltpu.VMEM(send_rows.shape, jnp.int32),
             pltpu.SemaphoreType.DMA((4,)),
         ],
-        limit=60,
+        limit=62,
     )
     part = exchange(part, "nar")
     lists = pl.BlockSpec((nnar, 8, LANES), lambda i: (0, head // 8, 0))
     pieces = (shape(k, own), shape(k, nnar * over))
-    r_own, send = local_call(
-        middle_kernel, pieces, part,
+    res, r_own, send = local_call(
+        middle_kernel, (shape(nsub, pad, LANES),) + pieces, part,
         specs={0: pl.BlockSpec((nnar, head + 8, LANES), lambda i: (0, 0, 0))},
-    )
-    res = local_call(
-        sum_kernel, shape(nsub, pad, LANES), part, send, specs={0: lists, 1: hbm}, cost=10
     )
     res = exchange(res, "sub")
 
     got = beside(send, nsub, nnar)
     local, vecs = local_call(
         local_kernel, (shape(k, rdev), shape(nnar // 2, maxev, rdev)),
-        *got, *product(r_own, local_inverse), *vecs,
+        *got, *product_in_two(r_own, local_inverse), *vecs,
     )
     vecs = (vecs, across(vecs, nnar, 1))
 
@@ -386,7 +413,7 @@
     got = beside(send, nsub, nnar)
     image, stats = local_call(
         image_kernel, (shape(k, rdev), shape(nsub * nnar, 1, LANES)),
-        *got, *product(p_own, stiffness), residual, beta,
+        *got, *product_in_two(p_own, stiffness), residual, beta,
     )
     stats = exchange(stats, ("sub", "nar"))
     return local_call(

time: 84.7 us -> 83.2 us (0.982)
  waiting for transfers between devices: 14.1 us -> 10 us
  starting transfers between devices: 24.6 us -> 27.5 us
  blocking collectives: 32.8 us -> 31.3 us
  local copies, waits for them, and re-layouts: 1.91 us -> 3.12 us
    all_to_all x2, starting transfers between devices: 10.5 us -> 17 us  [exchange(): return lax.all_to_all(blocks, axes, 0, 0)]
    all_to_all x2, waiting for transfers between devices: 8.37 us -> 5.41 us  [exchange(): return lax.all_to_all(blocks, axes, 0, 0)]
    ppermute x6, starting transfers between devices: 5.99 us -> 3.95 us  [across(): return lax.ppermute(block, 'nar', [(i, i ^ mask) for i in range(n)])]
    ppermute x2, starting transfers between devices: 8.17 us -> 6.56 us  [beside(): got = lax.ppermute(block, ('sub', 'nar'), route)]
    ppermute x2, waiting for transfers between devices: 5.62 us -> 4.11 us  [beside(): got = lax.ppermute(block, ('sub', 'nar'), route)]
    all_to_all x2, blocking collectives: 32.8 us -> 31.3 us  [exchange(): return lax.all_to_all(blocks, axes, 0, 0)]
    unnamed x10 -> x12, local copies, waits for them, and re-layouts: 1.91 us -> 3.12 us
    pallas_call x10 -> x11, Pallas kernels: 9.47 us -> 9.43 us  [local_call(): pl.pallas_call(body, grid=(1,), out_shape=outs, in_specs=[specs.get(i) or...]
  transfers between devices with their start and end apart: 10 -> 10, of which waited for: 4 -> 3; matrix products, arithmetic and copies ran while one was open for 0% -> 0% of each run, Pallas kernels for 5% -> 5%
where the time goes in v5:
time: 83.2 us; the launch traced here: 82.9 us
  blocking collectives  31.3 us (38%)
  starting transfers between devices  27.5 us (33%)
  waiting for transfers between devices  10 us (12%)
  Pallas kernels  9.43 us (11%)
  local copies, waits for them, and re-layouts  3.12 us (4%)
  between operations  1.48 us (2%)
    all_to_all x2, blocking collectives, exchange(): return lax.all_to_all(blocks, axes, 0, 0)  31.3 us
    all_to_all x2, starting transfers between devices, exchange(): return lax.all_to_all(blocks, axes, 0, 0)  17 us
    pallas_call x11, Pallas kernels, local_call(): pl.pallas_call(body, grid=(1,), out_shape=outs, in_specs=[specs.get(i) or...  9.43 us
    ppermute x2, starting transfers between devices, beside(): got = lax.ppermute(block, ('sub', 'nar'), route)  6.56 us
    all_to_all x2, waiting for transfers between devices, exchange(): return lax.all_to_all(blocks, axes, 0, 0)  5.41 us
    ppermute x2, waiting for transfers between devices, beside(): got = lax.ppermute(block, ('sub', 'nar'), route)  4.11 us
    ppermute x6, starting transfers between devices, across(): return lax.ppermute(block, 'nar', [(i, i ^ mask) for i in range(n)])  3.95 us
    unnamed x12, local copies, waits for them, and re-layouts  3.12 us
  transfers between devices with their start and end apart: 10, of which 3 were waited for; matrix products, arithmetic and copies ran while one was open for 0% of the time, Pallas kernels for 5%

profile of v5, /device:TPU:1, one launch (start us, length us, event | category | flops | bytes accessed | tf_op | source)
XLA Modules:
  0.0 82.9 jit_solution(939455492410627130)
XLA Ops:
  1.3 2.4 %shard_map.103 = f32[8,120,128]{2,1,0:T(8,128)} custom-call(f32[32,1,256]{2,1,0:T(1,128)} %res_ref.3, f32[1,96,256]{2,1,0:T(8,128)} %refs_0_.1, f32[96,384]{1,0:T(8,128)} %inv_hbm.1, s32[2,1,64]{2,1,0:T(1,128)} %rows_hbm.1, s32[1]{0:T(128)S(6)} %copy.11.count_ref), custom_call_target="tpu_custom_call" | custom-call | flops 300000000 | bytes 1024 | tf_op jit(solution)/shard_map/pallas_call | solution.py:32
  3.7 6.6 %all-to-all-start = ((f32[8,120,128]{2,1,0:T(8,128)}), f32[8,120,128]{2,1,0:T(8,128)S(1)}, u32[]{:S(2)}, u32[]{:S(2)}) async-start(f32[8,120,128]{2,1,0:T(8,128)} %shard_map.103), calls=%async_computation | async-start | bytes 983040 | tf_op jit(solution)/shard_map/all_to_all | solution.py:301
  10.3 2.9 %collective-permute-start.3 = (f32[1,96,256]{2,1,0:T(8,128)}, f32[1,96,256]{2,1,0:T(8,128)S(1)}, u32[]{:S(2)}, u32[]{:S(2)}) collective-permute-start(f32[1,96,256]{2,1,0:T(8,128)} %refs_0_.1), channel_id=1, source_target_pairs={{0,4},{1,5},{2,6},{3,7},{4,0},{5,1},{6,2},{7,3},{8,12},{9,13},{10,... | collective-permute-start | bytes 294920 | tf_op jit(solution)/shard_map/ppermute | solution.py:318
  13.3 0.3 collective-permute-start.2
  13.6 0.6 collective-permute-start.4
  14.1 5.4 %all-to-all-done.got_ref.one_ref.two_ref.lists_ref = f32[8,120,128]{2,1,0:T(8,128)S(1)} async-done(((f32[8,120,128]{2,1,0:T(8,128)}), f32[8,120,128]{2,1,0:T(8,128)S(1)}, u32[]{:S(2)}, u32[]{:S(2)}) %all-to-all-start) | async-done | bytes 491552 | tf_op jit(solution)/shard_map/all_to_all | solution.py:301
  19.5 0.8 shard_map.104
  20.3 10.4 %all-to-all-start.1 = ((f32[32,4,128]{2,1,0:T(4,128)}), f32[32,4,128]{2,1,0:T(4,128)S(1)}, u32[]{:S(2)}, u32[]{:S(2)}) async-start(f32[32,4,128]{2,1,0:T(4,128)} %get-tuple-element.21), calls=%async_computation.1 | async-start | bytes 131072 | tf_op jit(solution)/shard_map/all_to_all | solution.py:301
  30.7 4.7 %collective-permute-start = (f32[32,512]{1,0:T(8,128)S(1)}, f32[32,512]{1,0:T(8,128)S(1)}, u32[]{:S(2)}, u32[]{:S(2)}) collective-permute-start(f32[32,512]{1,0:T(8,128)S(1)} %get-tuple-element.22), channel_id=1, source_target_pairs={{0,8},{1,249},{2,10},{3,251},{4,12},{5,253},{6,14},{7,255},{8,0},{... | collective-permute-start | bytes 196616 | tf_op jit(solution)/shard_map/ppermute | solution.py:313
  35.4 0.0 copy-start
  35.4 1.9 %copy-done = f32[1,256,3072]{2,1,0:T(8,128)S(1)} copy-done((f32[1,256,3072]{2,1,0:T(8,128)S(1)}, f32[1,256,3072]{2,1,0:T(8,128)}, u32[]{:S(2)}) %copy-start) | copy-done | bytes 3145752
  37.3 0.0 copy-start.1
  37.3 0.5 shard_map.105.before_ref
  37.9 0.0 copy-start.3
  37.9 0.0 collective-permute-done.a_ref
  37.9 0.1 collective-permute-start.1
  38.0 1.2 %copy-done.1 = f32[1,256,3072]{2,1,0:T(8,128)S(1)} copy-done((f32[1,256,3072]{2,1,0:T(8,128)S(1)}, f32[1,256,3072]{2,1,0:T(8,128)}, u32[]{:S(2)}) %copy-start.1) | copy-done | bytes 3145752
  39.2 0.7 shard_map.106
  40.0 0.0 collective-permute-done.3.refs_2_
  40.0 0.0 collective-permute-done.2.refs_1_
  40.0 0.0 collective-permute-done.4.refs_3_
  40.0 0.0 collective-permute-done.1.b_ref
  40.0 0.0 copy-done.3
  40.0 0.6 shard_map.107
  40.6 0.1 collective-permute-start.5
  40.7 0.0 all-to-all-done.1.got_ref
  40.7 0.3 shard_map.108
  41.0 0.0 copy-start.2
  41.0 13.0 %all_to_all.20.got_ref = f32[8,32,384]{2,1,0:T(8,128)S(1)} all-to-all(f32[8,32,384]{2,1,0:T(8,128)S(1)} %get-tuple-element.28), channel_id=1, replica_groups=mesh['sub'=32,'nar'=8] {'nar'}, dimensions={0} | all-to-all | bytes 786432 | tf_op jit(solution)/shard_map/all_to_all | solution.py:301
  54.1 0.0 collective-permute-done.5.odd_ref
  54.1 0.7 shard_map.109
  54.8 1.8 %collective-permute-start.6 = (f32[32,512]{1,0:T(8,128)S(1)}, f32[32,512]{1,0:T(8,128)S(1)}, u32[]{:S(2)}, u32[]{:S(2)}) collective-permute-start(f32[32,512]{1,0:T(8,128)S(1)} %get-tuple-element.30), channel_id=1, source_target_pairs={{0,8},{1,249},{2,10},{3,251},{4,12},{5,253},{6,14},{7,255},{8,0},{... | collective-permute-start | bytes 196616 | tf_op jit(solution)/shard_map/ppermute | solution.py:313
  56.6 0.0 copy-done.2
  56.6 0.5 shard_map.110.before_ref
  57.2 0.0 copy-start.4
  57.2 4.1 %collective-permute-done.6.a_ref = f32[32,512]{1,0:T(8,128)S(1)} collective-permute-done((f32[32,512]{1,0:T(8,128)S(1)}, f32[32,512]{1,0:T(8,128)S(1)}, u32[]{:S(2)}, u32[]{:S(2)}) %collective-permute-start.6) | collective-permute-done | bytes 65568 | tf_op jit(solution)/shard_map/ppermute | solution.py:313
  61.3 0.0 collective-permute-start.7
  61.3 0.7 shard_map.111
  62.0 0.0 copy-start.5
  62.1 0.5 collective-permute-done.7.b_ref
  62.6 0.0 copy-done.4
  62.6 0.9 %shard_map.112 = (f32[32,256]{1,0:T(8,128)S(1)}, f32[256,1,128]{2,1,0:T(1,128)S(1)}) custom-call(f32[32,512]{1,0:T(8,128)S(1)} %collective-permute-done.6.a_ref, f32[32,512]{1,0:T(8,128)S(1)} %collective-permute-done.7.b_ref, f32[32,256]{1,0:T(8,128)S(1)} %get-tuple-element.32.own_ref, bf16[256,1024]{1,0:T(8,128)(2,1)S(1)} %get-tuple-element.33.high_ref, ...), custom_call_target="tpu_custom_call" | custom-call | flops 1000000000 | bytes 1024 | tf_op jit(solution)/shard_map/pallas_call | solution.py:32
  63.4 18.3 %all_to_all.21.got_ref = f32[256,1,128]{2,1,0:T(1,128)S(1)} all-to-all(f32[256,1,128]{2,1,0:T(1,128)S(1)} %get-tuple-element.36), channel_id=1, replica_groups=mesh['sub'=32,'nar'=8] {'sub','nar'}, dimensions={0} | all-to-all | bytes 262144 | tf_op jit(solution)/shard_map/all_to_all | solution.py:301
  81.7 0.0 copy-done.5
  81.7 1.2 %shard_map.113 = (f32[32,1,256]{2,1,0:T(1,128)}, f32[32,1,256]{2,1,0:T(1,128)}, f32[3,32]{1,0:T(4,128)}) custom-call(f32[256,1,128]{2,1,0:T(1,128)S(1)} %all_to_all.21.got_ref, f32[32,256]{1,0:T(8,128)S(1)} %get-tuple-element.37.image_ref, f32[32,1,256]{2,1,0:T(1,128)S(1)} %copy-done.4, f32[32,1,256]{2,1,0:T(1,128)S(1)} %copy-done.5, ...), custom_call_target="tpu_custom_call" | custom-call | flops 1000000000 | bytes 1024 | tf_op jit(solution)/shard_map/pallas_call | solution.py:32
Async XLA Ops:
  3.7 15.8 %all-to-all-start = ((f32[8,120,128]{2,1,0:T(8,128)}), f32[8,120,128]{2,1,0:T(8,128)S(1)}, u32[]{:S(2)}, u32[]{:S(2)}) async-start(f32[8,120,128]{2,1,0:T(8,128)} %shard_map.103), calls=%async_computation | async-start | bytes 983040 | tf_op jit(solution)/shard_map/all_to_all | solution.py:301
  10.3 29.6 %collective-permute-start.3 = (f32[1,96,256]{2,1,0:T(8,128)}, f32[1,96,256]{2,1,0:T(8,128)S(1)}, u32[]{:S(2)}, u32[]{:S(2)}) collective-permute-start(f32[1,96,256]{2,1,0:T(8,128)} %refs_0_.1), channel_id=1, source_target_pairs={{0,4},{1,5},{2,6},{3,7},{4,0},{5,1},{6,2},{7,3},{8,12},{9,13},{10,... | collective-permute-start | bytes 294920 | tf_op jit(solution)/shard_map/ppermute | solution.py:318
  13.3 26.7 %collective-permute-start.2 = (f32[1,96,256]{2,1,0:T(8,128)}, f32[1,96,256]{2,1,0:T(8,128)S(1)}, u32[]{:S(2)}, u32[]{:S(2)}) collective-permute-start(f32[1,96,256]{2,1,0:T(8,128)} %refs_0_.1), channel_id=1, source_target_pairs={{0,2},{1,3},{2,0},{3,1},{4,6},{5,7},{6,4},{7,5},{8,10},{9,11},{10,... | collective-permute-start | bytes 294920 | tf_op jit(solution)/shard_map/ppermute | solution.py:318
  13.6 26.4 %collective-permute-start.4 = (f32[1,96,256]{2,1,0:T(8,128)}, f32[1,96,256]{2,1,0:T(8,128)S(1)}, u32[]{:S(2)}, u32[]{:S(2)}) collective-permute-start(f32[1,96,256]{2,1,0:T(8,128)} %refs_0_.1), channel_id=1, source_target_pairs={{0,6},{1,7},{2,4},{3,5},{4,2},{5,3},{6,0},{7,1},{8,14},{9,15},{10,... | collective-permute-start | bytes 294920 | tf_op jit(solution)/shard_map/ppermute | solution.py:318
  20.3 20.3 %all-to-all-start.1 = ((f32[32,4,128]{2,1,0:T(4,128)}), f32[32,4,128]{2,1,0:T(4,128)S(1)}, u32[]{:S(2)}, u32[]{:S(2)}) async-start(f32[32,4,128]{2,1,0:T(4,128)} %get-tuple-element.21), calls=%async_computation.1 | async-start | bytes 131072 | tf_op jit(solution)/shard_map/all_to_all | solution.py:301
  30.7 7.2 %collective-permute-start = (f32[32,512]{1,0:T(8,128)S(1)}, f32[32,512]{1,0:T(8,128)S(1)}, u32[]{:S(2)}, u32[]{:S(2)}) collective-permute-start(f32[32,512]{1,0:T(8,128)S(1)} %get-tuple-element.22), channel_id=1, source_target_pairs={{0,8},{1,249},{2,10},{3,251},{4,12},{5,253},{6,14},{7,255},{8,0},{... | collective-permute-start | bytes 196616 | tf_op jit(solution)/shard_map/ppermute | solution.py:313
  35.4 1.9 %copy-start = (f32[1,256,3072]{2,1,0:T(8,128)S(1)}, f32[1,256,3072]{2,1,0:T(8,128)}, u32[]{:S(2)}) copy-start(f32[1,256,3072]{2,1,0:T(8,128)} %edge_ref.2) | copy-start | bytes 9437188
  37.3 1.9 %copy-start.1 = (f32[1,256,3072]{2,1,0:T(8,128)S(1)}, f32[1,256,3072]{2,1,0:T(8,128)}, u32[]{:S(2)}) copy-start(f32[1,256,3072]{2,1,0:T(8,128)} %edge_ref.2) | copy-start | bytes 9437188
  37.9 2.1 %copy-start.3 = (f32[1,96,256]{2,1,0:T(8,128)S(1)}, f32[1,96,256]{2,1,0:T(8,128)}, u32[]{:S(2)}) copy-start(f32[1,96,256]{2,1,0:T(8,128)} %refs_0_.1) | copy-start | bytes 294916
  37.9 2.1 %collective-permute-start.1 = (f32[32,512]{1,0:T(8,128)S(1)}, f32[32,512]{1,0:T(8,128)S(1)}, u32[]{:S(2)}, u32[]{:S(2)}) collective-permute-start(f32[32,512]{1,0:T(8,128)S(1)} %collective-permute-done.a_ref), channel_id=1, source_target_pairs={{0,1},{1,0},{2,3},{3,2},{4,5},{5,4},{6,7},{7,6},{8,9},{9,8},{10,11... | collective-permute-start | bytes 196616 | tf_op jit(solution)/shard_map/ppermute | solution.py:318
  40.6 13.5 %collective-permute-start.5 = (f32[4,96,256]{2,1,0:T(8,128)S(1)}, f32[4,96,256]{2,1,0:T(8,128)S(1)}, u32[]{:S(2)}, u32[]{:S(2)}) collective-permute-start(f32[4,96,256]{2,1,0:T(8,128)S(1)} %get-tuple-element.29.even_ref), channel_id=1, source_target_pairs={{0,1},{1,0},{2,3},{3,2},{4,5},{5,4},{6,7},{7,6},{8,9},{9,8},{10,11... | collective-permute-start | bytes 1179656 | tf_op jit(solution)/shard_map/ppermute | solution.py:318
  41.0 15.6 %copy-start.2 = (f32[1,256,3072]{2,1,0:T(8,128)S(1)}, f32[1,256,3072]{2,1,0:T(8,128)}, u32[]{:S(2)}) copy-start(f32[1,256,3072]{2,1,0:T(8,128)} %edge_ref.3) | copy-start | bytes 9437188
  54.8 6.5 %collective-permute-start.6 = (f32[32,512]{1,0:T(8,128)S(1)}, f32[32,512]{1,0:T(8,128)S(1)}, u32[]{:S(2)}, u32[]{:S(2)}) collective-permute-start(f32[32,512]{1,0:T(8,128)S(1)} %get-tuple-element.30), channel_id=1, source_target_pairs={{0,8},{1,249},{2,10},{3,251},{4,12},{5,253},{6,14},{7,255},{8,0},{... | collective-permute-start | bytes 196616 | tf_op jit(solution)/shard_map/ppermute | solution.py:313
  57.2 5.4 %copy-start.4 = (f32[32,1,256]{2,1,0:T(1,128)S(1)}, f32[32,1,256]{2,1,0:T(1,128)}, u32[]{:S(2)}) copy-start(f32[32,1,256]{2,1,0:T(1,128)} %res_ref.3) | copy-start | bytes 98308
  61.3 1.3 %collective-permute-start.7 = (f32[32,512]{1,0:T(8,128)S(1)}, f32[32,512]{1,0:T(8,128)S(1)}, u32[]{:S(2)}, u32[]{:S(2)}) collective-permute-start(f32[32,512]{1,0:T(8,128)S(1)} %collective-permute-done.6.a_ref), channel_id=1, source_target_pairs={{0,1},{1,0},{2,3},{3,2},{4,5},{5,4},{6,7},{7,6},{8,9},{9,8},{10,11... | collective-permute-start | bytes 196616 | tf_op jit(solution)/shard_map/ppermute | solution.py:318
  62.0 19.7 %copy-start.5 = (f32[32,1,256]{2,1,0:T(1,128)S(1)}, f32[32,1,256]{2,1,0:T(1,128)}, u32[]{:S(2)}) copy-start(f32[32,1,256]{2,1,0:T(1,128)} %iter_ref.1) | copy-start | bytes 98308

commit v6 on v5

--- a/solution.py
+++ b/solution.py
@@ -8,7 +8,7 @@
 from jax.sharding import PartitionSpec as P
 
 EPS = 1e-06
-COSTS = {'middle_kernel': 0.01, 'product_kernel': 3, 'half_kernel': 1, 'rest_kernel': 1, 'local_kernel': 0.3, 'solve_kernel': 3, 'begin_kernel': 0.3}
+COSTS = {'middle_kernel': 0.01, 'product_kernel': 3, 'half_kernel': 1, 'rest_kernel': 1, 'local_kernel': 0.3, 'solve_kernel': 3, 'begin_kernel': 0.3, 'precond_kernel': 8}
 F32, BF16 = jnp.float32, jnp.bfloat16
 LANES = 128
 NT = (((1,), (1,)), ((), ()))
@@ -270,12 +270,12 @@
     s = jnp.sum(off * off, axis=1, keepdims=True)
     image_ref[...] = image
     row = as_row(n) + pltpu.roll(as_row(a), k, 1) + pltpu.roll(as_row(s), 2 * k, 1)
-    out_ref[...] = jnp.broadcast_to(row[None], out_ref.shape)
+    out_ref[...] = jnp.broadcast_to(row, out_ref.shape)
 
 
 def end_kernel(got_ref, image_ref, res_ref, iter_ref, pre_ref, beta_ref, next_ref, new_ref, hess_ref, *, total):
     k = image_ref.shape[0]
-    stats = got_ref[:, 0, :]
+    stats = got_ref[...]
     n_i = stats
     a_i = pltpu.roll(stats, LANES - k, 1)
     s_i = pltpu.roll(stats, LANES - 2 * k, 1)
@@ -412,10 +412,10 @@
 
     got = beside(send, nsub, nnar)
     image, stats = local_call(
-        image_kernel, (shape(k, rdev), shape(nsub * nnar, 1, LANES)),
+        image_kernel, (shape(k, rdev), shape(nsub * nnar, LANES)),
         *got, *product_in_two(p_own, stiffness), residual, beta,
     )
-    stats = exchange(stats, ("sub", "nar"))
+    stats = exchange(stats[:, None], ("sub", "nar")).reshape(nsub * nnar, LANES)
     return local_call(
         functools.partial(end_kernel, total=total),
         (shape(k, 1, rdev), shape(k, 1, rdev), shape(3, k)),

time: 83.2 us -> 82.7 us (level)
  no operation moved by 1% of the time
where the time goes in v6:
time: 82.7 us; the launch traced here: 82.3 us
  blocking collectives  31.1 us (38%)
  starting transfers between devices  27.5 us (33%)
  waiting for transfers between devices  10 us (12%)
  Pallas kernels  9.16 us (11%)
  local copies, waits for them, and re-layouts  3.12 us (4%)
  between operations  1.47 us (2%)
    all_to_all x2, blocking collectives, exchange(): return lax.all_to_all(blocks, axes, 0, 0)  31.1 us
    all_to_all x2, starting transfers between devices, exchange(): return lax.all_to_all(blocks, axes, 0, 0)  17 us
    pallas_call x11, Pallas kernels, local_call(): pl.pallas_call(body, grid=(1,), out_shape=outs, in_specs=[specs.get(i) or...  9.16 us
    ppermute x2, starting transfers between devices, beside(): got = lax.ppermute(block, ('sub', 'nar'), route)  6.55 us
    all_to_all x2, waiting for transfers between devices, exchange(): return lax.all_to_all(blocks, axes, 0, 0)  5.41 us
    ppermute x2, waiting for transfers between devices, beside(): got = lax.ppermute(block, ('sub', 'nar'), route)  4.12 us
    ppermute x6, starting transfers between devices, across(): return lax.ppermute(block, 'nar', [(i, i ^ mask) for i in range(n)])  3.95 us
    unnamed x12, local copies, waits for them, and re-layouts  3.12 us
  transfers between devices with their start and end apart: 10, of which 3 were waited for; matrix products, arithmetic and copies ran while one was open for 0% of the time, Pallas kernels for 5%

profile of v6, /device:TPU:1, one launch (start us, length us, event | category | flops | bytes accessed | tf_op | source)
XLA Modules:
  0.0 82.3 jit_solution(1751506512468897658)
XLA Ops:
  1.3 2.4 %shard_map.103 = f32[8,120,128]{2,1,0:T(8,128)} custom-call(f32[32,1,256]{2,1,0:T(1,128)} %res_ref.3, f32[1,96,256]{2,1,0:T(8,128)} %refs_0_.1, f32[96,384]{1,0:T(8,128)} %inv_hbm.1, s32[2,1,64]{2,1,0:T(1,128)} %rows_hbm.1, s32[1]{0:T(128)S(6)} %copy.12.count_ref), custom_call_target="tpu_custom_call" | custom-call | flops 300000000 | bytes 1024 | tf_op jit(solution)/shard_map/pallas_call | solution.py:32
  3.7 6.6 %all-to-all-start = ((f32[8,120,128]{2,1,0:T(8,128)}), f32[8,120,128]{2,1,0:T(8,128)S(1)}, u32[]{:S(2)}, u32[]{:S(2)}) async-start(f32[8,120,128]{2,1,0:T(8,128)} %shard_map.103), calls=%async_computation | async-start | bytes 983040 | tf_op jit(solution)/shard_map/all_to_all | solution.py:301
  10.3 2.9 %collective-permute-start.3 = (f32[1,96,256]{2,1,0:T(8,128)}, f32[1,96,256]{2,1,0:T(8,128)S(1)}, u32[]{:S(2)}, u32[]{:S(2)}) collective-permute-start(f32[1,96,256]{2,1,0:T(8,128)} %refs_0_.1), channel_id=1, source_target_pairs={{0,4},{1,5},{2,6},{3,7},{4,0},{5,1},{6,2},{7,3},{8,12},{9,13},{10,... | collective-permute-start | bytes 294920 | tf_op jit(solution)/shard_map/ppermute | solution.py:318
  13.3 0.3 collective-permute-start.2
  13.6 0.6 collective-permute-start.4
  14.1 5.4 %all-to-all-done.got_ref.one_ref.two_ref.lists_ref = f32[8,120,128]{2,1,0:T(8,128)S(1)} async-done(((f32[8,120,128]{2,1,0:T(8,128)}), f32[8,120,128]{2,1,0:T(8,128)S(1)}, u32[]{:S(2)}, u32[]{:S(2)}) %all-to-all-start) | async-done | bytes 491552 | tf_op jit(solution)/shard_map/all_to_all | solution.py:301
  19.5 0.8 shard_map.104
  20.3 10.4 %all-to-all-start.1 = ((f32[32,4,128]{2,1,0:T(4,128)}), f32[32,4,128]{2,1,0:T(4,128)S(1)}, u32[]{:S(2)}, u32[]{:S(2)}) async-start(f32[32,4,128]{2,1,0:T(4,128)} %get-tuple-element.21), calls=%async_computation.1 | async-start | bytes 131072 | tf_op jit(solution)/shard_map/all_to_all | solution.py:301
  30.7 4.7 %collective-permute-start = (f32[32,512]{1,0:T(8,128)S(1)}, f32[32,512]{1,0:T(8,128)S(1)}, u32[]{:S(2)}, u32[]{:S(2)}) collective-permute-start(f32[32,512]{1,0:T(8,128)S(1)} %get-tuple-element.22), channel_id=1, source_target_pairs={{0,8},{1,249},{2,10},{3,251},{4,12},{5,253},{6,14},{7,255},{8,0},{... | collective-permute-start | bytes 196616 | tf_op jit(solution)/shard_map/ppermute | solution.py:313
  35.4 0.0 copy-start
  35.4 1.9 %copy-done = f32[1,256,3072]{2,1,0:T(8,128)S(1)} copy-done((f32[1,256,3072]{2,1,0:T(8,128)S(1)}, f32[1,256,3072]{2,1,0:T(8,128)}, u32[]{:S(2)}) %copy-start) | copy-done | bytes 3145752
  37.3 0.0 copy-start.1
  37.3 0.5 shard_map.105.before_ref
  37.9 0.0 copy-start.3
  37.9 0.0 collective-permute-done.a_ref
  37.9 0.1 collective-permute-start.1
  38.0 1.2 %copy-done.1 = f32[1,256,3072]{2,1,0:T(8,128)S(1)} copy-done((f32[1,256,3072]{2,1,0:T(8,128)S(1)}, f32[1,256,3072]{2,1,0:T(8,128)}, u32[]{:S(2)}) %copy-start.1) | copy-done | bytes 3145752
  39.2 0.7 shard_map.106
  40.0 0.0 collective-permute-done.3.refs_2_
  40.0 0.0 collective-permute-done.2.refs_1_
  40.0 0.0 collective-permute-done.4.refs_3_
  40.0 0.0 collective-permute-done.1.b_ref
  40.0 0.0 copy-done.3
  40.0 0.6 shard_map.107
  40.6 0.1 collective-permute-start.5
  40.7 0.0 all-to-all-done.1.got_ref
  40.7 0.3 shard_map.108
  41.0 12.8 %all_to_all.20.got_ref = f32[8,32,384]{2,1,0:T(8,128)S(1)} all-to-all(f32[8,32,384]{2,1,0:T(8,128)S(1)} %get-tuple-element.28), channel_id=1, replica_groups=mesh['sub'=32,'nar'=8] {'nar'}, dimensions={0} | all-to-all | bytes 786432 | tf_op jit(solution)/shard_map/all_to_all | solution.py:301
  53.8 0.0 copy-start.2
  53.8 0.0 collective-permute-done.5.odd_ref
  53.8 0.7 shard_map.109
  54.5 1.8 %collective-permute-start.6 = (f32[32,512]{1,0:T(8,128)S(1)}, f32[32,512]{1,0:T(8,128)S(1)}, u32[]{:S(2)}, u32[]{:S(2)}) collective-permute-start(f32[32,512]{1,0:T(8,128)S(1)} %get-tuple-element.30), channel_id=1, source_target_pairs={{0,8},{1,249},{2,10},{3,251},{4,12},{5,253},{6,14},{7,255},{8,0},{... | collective-permute-start | bytes 196616 | tf_op jit(solution)/shard_map/ppermute | solution.py:313
  56.3 0.0 copy-done.2
  56.3 0.5 shard_map.110.before_ref
  56.9 0.0 copy-start.4
  56.9 4.1 %collective-permute-done.6.a_ref = f32[32,512]{1,0:T(8,128)S(1)} collective-permute-done((f32[32,512]{1,0:T(8,128)S(1)}, f32[32,512]{1,0:T(8,128)S(1)}, u32[]{:S(2)}, u32[]{:S(2)}) %collective-permute-start.6) | collective-permute-done | bytes 65568 | tf_op jit(solution)/shard_map/ppermute | solution.py:313
  61.0 0.0 collective-permute-start.7
  61.0 0.7 shard_map.111
  61.8 0.0 copy-start.5
  61.8 0.5 collective-permute-done.7.b_ref
  62.3 0.0 copy-done.4
  62.3 0.8 shard_map.112
  63.1 18.3 %all_to_all.21 = f32[256,1,128]{2,1,0:T(1,128)S(1)} all-to-all(f32[256,1,128]{2,1,0:T(1,128)S(1)} %bitcast.5), channel_id=1, replica_groups=mesh['sub'=32,'nar'=8] {'sub','nar'}, dimensions={0} | all-to-all | bytes 262144 | tf_op jit(solution)/shard_map/all_to_all | solution.py:301
  81.4 0.0 copy-done.5
  81.4 1.0 %shard_map.113 = (f32[32,1,256]{2,1,0:T(1,128)}, f32[32,1,256]{2,1,0:T(1,128)}, f32[3,32]{1,0:T(4,128)}) custom-call(f32[256,128]{1,0:T(8,128)S(1)} %bitcast.4, f32[32,256]{1,0:T(8,128)S(1)} %get-tuple-element.37.image_ref, f32[32,1,256]{2,1,0:T(1,128)S(1)} %copy-done.4, f32[32,1,256]{2,1,0:T(1,128)S(1)} %copy-done.5, ...), custom_call_target="tpu_custom_call" | custom-call | flops 1000000000 | bytes 1024 | tf_op jit(solution)/shard_map/pallas_call | solution.py:32
Async XLA Ops:
  3.7 15.8 %all-to-all-start = ((f32[8,120,128]{2,1,0:T(8,128)}), f32[8,120,128]{2,1,0:T(8,128)S(1)}, u32[]{:S(2)}, u32[]{:S(2)}) async-start(f32[8,120,128]{2,1,0:T(8,128)} %shard_map.103), calls=%async_computation | async-start | bytes 983040 | tf_op jit(solution)/shard_map/all_to_all | solution.py:301
  10.3 29.6 %collective-permute-start.3 = (f32[1,96,256]{2,1,0:T(8,128)}, f32[1,96,256]{2,1,0:T(8,128)S(1)}, u32[]{:S(2)}, u32[]{:S(2)}) collective-permute-start(f32[1,96,256]{2,1,0:T(8,128)} %refs_0_.1), channel_id=1, source_target_pairs={{0,4},{1,5},{2,6},{3,7},{4,0},{5,1},{6,2},{7,3},{8,12},{9,13},{10,... | collective-permute-start | bytes 294920 | tf_op jit(solution)/shard_map/ppermute | solution.py:318
  13.3 26.7 %collective-permute-start.2 = (f32[1,96,256]{2,1,0:T(8,128)}, f32[1,96,256]{2,1,0:T(8,128)S(1)}, u32[]{:S(2)}, u32[]{:S(2)}) collective-permute-start(f32[1,96,256]{2,1,0:T(8,128)} %refs_0_.1), channel_id=1, source_target_pairs={{0,2},{1,3},{2,0},{3,1},{4,6},{5,7},{6,4},{7,5},{8,10},{9,11},{10,... | collective-permute-start | bytes 294920 | tf_op jit(solution)/shard_map/ppermute | solution.py:318
  13.6 26.4 %collective-permute-start.4 = (f32[1,96,256]{2,1,0:T(8,128)}, f32[1,96,256]{2,1,0:T(8,128)S(1)}, u32[]{:S(2)}, u32[]{:S(2)}) collective-permute-start(f32[1,96,256]{2,1,0:T(8,128)} %refs_0_.1), channel_id=1, source_target_pairs={{0,6},{1,7},{2,4},{3,5},{4,2},{5,3},{6,0},{7,1},{8,14},{9,15},{10,... | collective-permute-start | bytes 294920 | tf_op jit(solution)/shard_map/ppermute | solution.py:318
  20.3 20.3 %all-to-all-start.1 = ((f32[32,4,128]{2,1,0:T(4,128)}), f32[32,4,128]{2,1,0:T(4,128)S(1)}, u32[]{:S(2)}, u32[]{:S(2)}) async-start(f32[32,4,128]{2,1,0:T(4,128)} %get-tuple-element.21), calls=%async_computation.1 | async-start | bytes 131072 | tf_op jit(solution)/shard_map/all_to_all | solution.py:301
  30.7 7.2 %collective-permute-start = (f32[32,512]{1,0:T(8,128)S(1)}, f32[32,512]{1,0:T(8,128)S(1)}, u32[]{:S(2)}, u32[]{:S(2)}) collective-permute-start(f32[32,512]{1,0:T(8,128)S(1)} %get-tuple-element.22), channel_id=1, source_target_pairs={{0,8},{1,249},{2,10},{3,251},{4,12},{5,253},{6,14},{7,255},{8,0},{... | collective-permute-start | bytes 196616 | tf_op jit(solution)/shard_map/ppermute | solution.py:313
  35.4 1.9 %copy-start = (f32[1,256,3072]{2,1,0:T(8,128)S(1)}, f32[1,256,3072]{2,1,0:T(8,128)}, u32[]{:S(2)}) copy-start(f32[1,256,3072]{2,1,0:T(8,128)} %edge_ref.2) | copy-start | bytes 9437188
  37.3 1.9 %copy-start.1 = (f32[1,256,3072]{2,1,0:T(8,128)S(1)}, f32[1,256,3072]{2,1,0:T(8,128)}, u32[]{:S(2)}) copy-start(f32[1,256,3072]{2,1,0:T(8,128)} %edge_ref.2) | copy-start | bytes 9437188
  37.9 2.1 %copy-start.3 = (f32[1,96,256]{2,1,0:T(8,128)S(1)}, f32[1,96,256]{2,1,0:T(8,128)}, u32[]{:S(2)}) copy-start(f32[1,96,256]{2,1,0:T(8,128)} %refs_0_.1) | copy-start | bytes 294916
  37.9 2.1 %collective-permute-start.1 = (f32[32,512]{1,0:T(8,128)S(1)}, f32[32,512]{1,0:T(8,128)S(1)}, u32[]{:S(2)}, u32[]{:S(2)}) collective-permute-start(f32[32,512]{1,0:T(8,128)S(1)} %collective-permute-done.a_ref), channel_id=1, source_target_pairs={{0,1},{1,0},{2,3},{3,2},{4,5},{5,4},{6,7},{7,6},{8,9},{9,8},{10,11... | collective-permute-start | bytes 196616 | tf_op jit(solution)/shard_map/ppermute | solution.py:318
  40.6 13.2 %collective-permute-start.5 = (f32[4,96,256]{2,1,0:T(8,128)S(1)}, f32[4,96,256]{2,1,0:T(8,128)S(1)}, u32[]{:S(2)}, u32[]{:S(2)}) collective-permute-start(f32[4,96,256]{2,1,0:T(8,128)S(1)} %get-tuple-element.29.even_ref), channel_id=1, source_target_pairs={{0,1},{1,0},{2,3},{3,2},{4,5},{5,4},{6,7},{7,6},{8,9},{9,8},{10,11... | collective-permute-start | bytes 1179656 | tf_op jit(solution)/shard_map/ppermute | solution.py:318
  53.8 2.6 %copy-start.2 = (f32[1,256,3072]{2,1,0:T(8,128)S(1)}, f32[1,256,3072]{2,1,0:T(8,128)}, u32[]{:S(2)}) copy-start(f32[1,256,3072]{2,1,0:T(8,128)} %edge_ref.3) | copy-start | bytes 9437188
  54.5 6.5 %collective-permute-start.6 = (f32[32,512]{1,0:T(8,128)S(1)}, f32[32,512]{1,0:T(8,128)S(1)}, u32[]{:S(2)}, u32[]{:S(2)}) collective-permute-start(f32[32,512]{1,0:T(8,128)S(1)} %get-tuple-element.30), channel_id=1, source_target_pairs={{0,8},{1,249},{2,10},{3,251},{4,12},{5,253},{6,14},{7,255},{8,0},{... | collective-permute-start | bytes 196616 | tf_op jit(solution)/shard_map/ppermute | solution.py:313
  56.9 5.4 %copy-start.4 = (f32[32,1,256]{2,1,0:T(1,128)S(1)}, f32[32,1,256]{2,1,0:T(1,128)}, u32[]{:S(2)}) copy-start(f32[32,1,256]{2,1,0:T(1,128)} %res_ref.3) | copy-start | bytes 98308
  61.0 1.3 %collective-permute-start.7 = (f32[32,512]{1,0:T(8,128)S(1)}, f32[32,512]{1,0:T(8,128)S(1)}, u32[]{:S(2)}, u32[]{:S(2)}) collective-permute-start(f32[32,512]{1,0:T(8,128)S(1)} %collective-permute-done.6.a_ref), channel_id=1, source_target_pairs={{0,1},{1,0},{2,3},{3,2},{4,5},{5,4},{6,7},{7,6},{8,9},{9,8},{10,11... | collective-permute-start | bytes 196616 | tf_op jit(solution)/shard_map/ppermute | solution.py:318
  61.8 19.6 %copy-start.5 = (f32[32,1,256]{2,1,0:T(1,128)S(1)}, f32[32,1,256]{2,1,0:T(1,128)}, u32[]{:S(2)}) copy-start(f32[32,1,256]{2,1,0:T(1,128)} %iter_ref.1) | copy-start | bytes 98308

commit v7 on v6

--- a/solution.py
+++ b/solution.py
@@ -46,23 +46,28 @@
     return high, (x - high.astype(F32)).astype(BF16)
 
 
+def stacked(parts):
+    return jnp.concatenate(parts, axis=0).astype(BF16)
+
+
 def dot3(a, b, dims):
     dot = functools.partial(lax.dot_general, dimension_numbers=dims, preferred_element_type=F32)
-    (ah, al), (bh, bl) = halves(a), halves(b)
-    return dot(ah, bh) + (dot(al, bh) + dot(ah, bl))
-
-
-def exactly(pick, x, dims, first):
-    high = x.astype(BF16)
-    rest = x - high.astype(F32)
-    mid = rest.astype(BF16)
-    low = (rest - mid.astype(F32)).astype(BF16)
-    total = None
-    for part in (low, mid, high):
-        pair = (pick, part) if first else (part, pick)
-        term = lax.dot_general(*pair, dimension_numbers=dims, preferred_element_type=F32)
-        total = term if total is None else total + term
-    return total
+    rows = a.shape[0]
+    high = a.astype(BF16).astype(F32)
+    bh, bl = halves(b)
+    both = dot(stacked([high, a - high]), bh)
+    return both[:rows] + (both[rows:] + dot(high.astype(BF16), bl))
+
+
+def exactly(pick, x, dims):
+    rows = x.shape[0]
+    high = x.astype(BF16).astype(F32)
+    rest = x - high
+    mid = rest.astype(BF16).astype(F32)
+    out = lax.dot_general(
+        stacked([rest - mid, mid, high]), pick, dimension_numbers=dims, preferred_element_type=F32
+    )
+    return out[:rows] + out[rows : 2 * rows] + out[2 * rows :]
 
 
 def iota(dims, axis):
@@ -140,7 +145,7 @@
     c = p // (each * per * ncol)
     want = q * maxev + b * (maxev // ncol) + c * each + a
     pick = (want == iota((ncols, ncols), 0)).astype(F32).astype(BF16)
-    return exactly(pick, inverse, NN, False).T
+    return exactly(pick, inverse, NN).T
 
 
 def weave(ends, out_ref):
@@ -168,7 +173,7 @@
         field = jnp.concatenate([got_ref[c, i * k : (i + 1) * k, :] for i in range(halves_of)], axis=1)
         own_ref[:, c * rdev : (c + 1) * rdev] = field
         listed = got_ref[c, at + 4 : at + 5, :]
-        ends.append(exactly(pick_of(listed, rdev), field, NN, False))
+        ends.append(exactly(pick_of(listed, rdev), field, NN))
     weave(ends, send_ref)
 
 
@@ -199,8 +204,11 @@
 
 def margin_product(a_ref, b_ref, high_ref, low_ref):
     dot = functools.partial(lax.dot_general, dimension_numbers=NT, preferred_element_type=F32)
-    high, low = halves(jnp.concatenate(margins(a_ref, b_ref), axis=1))
-    return dot(high, high_ref[...]) + (dot(low, high_ref[...]) + dot(high, low_ref[...]))
+    field = jnp.concatenate(margins(a_ref, b_ref), axis=1)
+    rows = field.shape[0]
+    high = field.astype(BF16).astype(F32)
+    both = dot(stacked([high, field - high]), high_ref[...])
+    return both[:rows] + (both[rows:] + dot(high.astype(BF16), low_ref[...]))
 
 
 def local_kernel(a_ref, b_ref, own_ref, high_ref, low_ref, *refs):
@@ -250,7 +258,7 @@
         if i == 0:
             mine_ref[...] = field
     ends = [
-        exactly(pick_of(lists_ref[c, 4:5, :], rdev), own_ref[:, c * rdev : (c + 1) * rdev], NN, False)
+        exactly(pick_of(lists_ref[c, 4:5, :], rdev), own_ref[:, c * rdev : (c + 1) * rdev], NN)
         for c in range(n)
     ]
     weave(ends, send_ref)

time: 82.7 us -> 82.2 us (level)
  Pallas kernels: 9.16 us -> 8.13 us
    pallas_call x11, Pallas kernels: 9.16 us -> 8.13 us  [local_call(): pl.pallas_call(body, grid=(1,), out_shape=outs, in_specs=[specs.get(i) or...]
  transfers between devices with their start and end apart: 10 -> 10, of which waited for: 3 -> 3; matrix products, arithmetic and copies ran while one was open for 0% -> 0% of each run, Pallas kernels for 5% -> 4%
where the time goes in v7:
time: 82.2 us; the launch traced here: 81.8 us
  blocking collectives  31.2 us (38%)
  starting transfers between devices  27.4 us (33%)
  waiting for transfers between devices  10.4 us (13%)
  Pallas kernels  8.13 us (10%)
  local copies, waits for them, and re-layouts  3.28 us (4%)
  between operations  1.44 us (2%)
    all_to_all x2, blocking collectives, exchange(): return lax.all_to_all(blocks, axes, 0, 0)  31.2 us
    all_to_all x2, starting transfers between devices, exchange(): return lax.all_to_all(blocks, axes, 0, 0)  17 us
    pallas_call x11, Pallas kernels, local_call(): pl.pallas_call(body, grid=(1,), out_shape=outs, in_specs=[specs.get(i) or...  8.13 us
    ppermute x2, starting transfers between devices, beside(): got = lax.ppermute(block, ('sub', 'nar'), route)  6.39 us
    all_to_all x2, waiting for transfers between devices, exchange(): return lax.all_to_all(blocks, axes, 0, 0)  5.41 us
    ppermute x2, waiting for transfers between devices, beside(): got = lax.ppermute(block, ('sub', 'nar'), route)  4.43 us
    ppermute x6, starting transfers between devices, across(): return lax.ppermute(block, 'nar', [(i, i ^ mask) for i in range(n)])  3.97 us
    unnamed x12, local copies, waits for them, and re-layouts  3.28 us
  transfers between devices with their start and end apart: 10, of which 3 were waited for; matrix products, arithmetic and copies ran while one was open for 0% of the time, Pallas kernels for 4%

profile of v7, /device:TPU:1, one launch (start us, length us, event | category | flops | bytes accessed | tf_op | source)
XLA Modules:
  0.0 81.8 jit_solution(17502365674340996952)
XLA Ops:
  1.3 2.3 %shard_map.103 = f32[8,120,128]{2,1,0:T(8,128)} custom-call(f32[32,1,256]{2,1,0:T(1,128)} %res_ref.3, f32[1,96,256]{2,1,0:T(8,128)} %refs_0_.1, f32[96,384]{1,0:T(8,128)} %inv_hbm.1, s32[2,1,64]{2,1,0:T(1,128)} %rows_hbm.1, s32[1]{0:T(128)S(6)} %copy.12.count_ref), custom_call_target="tpu_custom_call" | custom-call | flops 300000000 | bytes 1024 | tf_op jit(solution)/shard_map/pallas_call | solution.py:32
  3.6 6.6 %all-to-all-start = ((f32[8,120,128]{2,1,0:T(8,128)}), f32[8,120,128]{2,1,0:T(8,128)S(1)}, u32[]{:S(2)}, u32[]{:S(2)}) async-start(f32[8,120,128]{2,1,0:T(8,128)} %shard_map.103), calls=%async_computation | async-start | bytes 983040 | tf_op jit(solution)/shard_map/all_to_all | solution.py:309
  10.2 2.9 %collective-permute-start.3 = (f32[1,96,256]{2,1,0:T(8,128)}, f32[1,96,256]{2,1,0:T(8,128)S(1)}, u32[]{:S(2)}, u32[]{:S(2)}) collective-permute-start(f32[1,96,256]{2,1,0:T(8,128)} %refs_0_.1), channel_id=1, source_target_pairs={{0,4},{1,5},{2,6},{3,7},{4,0},{5,1},{6,2},{7,3},{8,12},{9,13},{10,... | collective-permute-start | bytes 294920 | tf_op jit(solution)/shard_map/ppermute | solution.py:326
  13.2 0.3 collective-permute-start.2
  13.5 0.6 collective-permute-start.4
  14.0 5.4 %all-to-all-done.got_ref.one_ref.two_ref.lists_ref = f32[8,120,128]{2,1,0:T(8,128)S(1)} async-done(((f32[8,120,128]{2,1,0:T(8,128)}), f32[8,120,128]{2,1,0:T(8,128)S(1)}, u32[]{:S(2)}, u32[]{:S(2)}) %all-to-all-start) | async-done | bytes 491552 | tf_op jit(solution)/shard_map/all_to_all | solution.py:309
  19.4 0.7 shard_map.104
  20.2 10.4 %all-to-all-start.1 = ((f32[32,4,128]{2,1,0:T(4,128)}), f32[32,4,128]{2,1,0:T(4,128)S(1)}, u32[]{:S(2)}, u32[]{:S(2)}) async-start(f32[32,4,128]{2,1,0:T(4,128)} %get-tuple-element.21), calls=%async_computation.1 | async-start | bytes 131072 | tf_op jit(solution)/shard_map/all_to_all | solution.py:309
  30.6 4.7 %collective-permute-start = (f32[32,512]{1,0:T(8,128)S(1)}, f32[32,512]{1,0:T(8,128)S(1)}, u32[]{:S(2)}, u32[]{:S(2)}) collective-permute-start(f32[32,512]{1,0:T(8,128)S(1)} %get-tuple-element.22), channel_id=1, source_target_pairs={{0,8},{1,249},{2,10},{3,251},{4,12},{5,253},{6,14},{7,255},{8,0},{... | collective-permute-start | bytes 196616 | tf_op jit(solution)/shard_map/ppermute | solution.py:321
  35.3 0.0 copy-start
  35.3 1.9 %copy-done = f32[1,256,3072]{2,1,0:T(8,128)S(1)} copy-done((f32[1,256,3072]{2,1,0:T(8,128)S(1)}, f32[1,256,3072]{2,1,0:T(8,128)}, u32[]{:S(2)}) %copy-start) | copy-done | bytes 3145752
  37.2 0.0 copy-start.1
  37.2 0.4 shard_map.105.before_ref
  37.6 0.0 copy-start.3
  37.6 0.0 collective-permute-done.a_ref
  37.6 0.1 collective-permute-start.1
  37.7 1.3 %copy-done.1 = f32[1,256,3072]{2,1,0:T(8,128)S(1)} copy-done((f32[1,256,3072]{2,1,0:T(8,128)S(1)}, f32[1,256,3072]{2,1,0:T(8,128)}, u32[]{:S(2)}) %copy-start.1) | copy-done | bytes 3145752
  39.1 0.6 shard_map.106
  39.7 0.0 collective-permute-done.3.refs_2_
  39.7 0.0 collective-permute-done.2.refs_1_
  39.7 0.0 collective-permute-done.4.refs_3_
  39.7 0.0 collective-permute-done.1.b_ref
  39.7 0.0 copy-done.3
  39.8 0.4 shard_map.107
  40.2 0.1 collective-permute-start.5
  40.3 0.0 all-to-all-done.1.got_ref
  40.3 0.3 shard_map.108
  40.6 13.0 %all_to_all.20.got_ref = f32[8,32,384]{2,1,0:T(8,128)S(1)} all-to-all(f32[8,32,384]{2,1,0:T(8,128)S(1)} %get-tuple-element.28), channel_id=1, replica_groups=mesh['sub'=32,'nar'=8] {'nar'}, dimensions={0} | all-to-all | bytes 786432 | tf_op jit(solution)/shard_map/all_to_all | solution.py:309
  53.6 0.0 copy-start.2
  53.6 0.0 collective-permute-done.5.odd_ref
  53.6 0.6 shard_map.109
  54.2 1.7 %collective-permute-start.6 = (f32[32,512]{1,0:T(8,128)S(1)}, f32[32,512]{1,0:T(8,128)S(1)}, u32[]{:S(2)}, u32[]{:S(2)}) collective-permute-start(f32[32,512]{1,0:T(8,128)S(1)} %get-tuple-element.30), channel_id=1, source_target_pairs={{0,8},{1,249},{2,10},{3,251},{4,12},{5,253},{6,14},{7,255},{8,0},{... | collective-permute-start | bytes 196616 | tf_op jit(solution)/shard_map/ppermute | solution.py:321
  55.9 0.0 copy-done.2
  55.9 0.4 shard_map.110.before_ref
  56.3 0.0 copy-start.4
  56.3 4.4 %collective-permute-done.6.a_ref = f32[32,512]{1,0:T(8,128)S(1)} collective-permute-done((f32[32,512]{1,0:T(8,128)S(1)}, f32[32,512]{1,0:T(8,128)S(1)}, u32[]{:S(2)}, u32[]{:S(2)}) %collective-permute-start.6) | collective-permute-done | bytes 65568 | tf_op jit(solution)/shard_map/ppermute | solution.py:321
  60.8 0.0 collective-permute-start.7
  60.8 0.6 shard_map.111
  61.4 0.0 copy-start.5
  61.4 0.6 collective-permute-done.7.b_ref
  62.0 0.0 copy-done.4
  62.0 0.7 shard_map.112
  62.7 18.2 %all_to_all.21 = f32[256,1,128]{2,1,0:T(1,128)S(1)} all-to-all(f32[256,1,128]{2,1,0:T(1,128)S(1)} %bitcast.5), channel_id=1, replica_groups=mesh['sub'=32,'nar'=8] {'sub','nar'}, dimensions={0} | all-to-all | bytes 262144 | tf_op jit(solution)/shard_map/all_to_all | solution.py:309
  80.9 0.0 copy-done.5
  80.9 1.0 %shard_map.113 = (f32[32,1,256]{2,1,0:T(1,128)}, f32[32,1,256]{2,1,0:T(1,128)}, f32[3,32]{1,0:T(4,128)}) custom-call(f32[256,128]{1,0:T(8,128)S(1)} %bitcast.4, f32[32,256]{1,0:T(8,128)S(1)} %get-tuple-element.37.image_ref, f32[32,1,256]{2,1,0:T(1,128)S(1)} %copy-done.4, f32[32,1,256]{2,1,0:T(1,128)S(1)} %copy-done.5, ...), custom_call_target="tpu_custom_call" | custom-call | flops 1000000000 | bytes 1024 | tf_op jit(solution)/shard_map/pallas_call | solution.py:32
Async XLA Ops:
  3.6 15.8 %all-to-all-start = ((f32[8,120,128]{2,1,0:T(8,128)}), f32[8,120,128]{2,1,0:T(8,128)S(1)}, u32[]{:S(2)}, u32[]{:S(2)}) async-start(f32[8,120,128]{2,1,0:T(8,128)} %shard_map.103), calls=%async_computation | async-start | bytes 983040 | tf_op jit(solution)/shard_map/all_to_all | solution.py:309
  10.2 29.5 %collective-permute-start.3 = (f32[1,96,256]{2,1,0:T(8,128)}, f32[1,96,256]{2,1,0:T(8,128)S(1)}, u32[]{:S(2)}, u32[]{:S(2)}) collective-permute-start(f32[1,96,256]{2,1,0:T(8,128)} %refs_0_.1), channel_id=1, source_target_pairs={{0,4},{1,5},{2,6},{3,7},{4,0},{5,1},{6,2},{7,3},{8,12},{9,13},{10,... | collective-permute-start | bytes 294920 | tf_op jit(solution)/shard_map/ppermute | solution.py:326
  13.2 26.6 %collective-permute-start.2 = (f32[1,96,256]{2,1,0:T(8,128)}, f32[1,96,256]{2,1,0:T(8,128)S(1)}, u32[]{:S(2)}, u32[]{:S(2)}) collective-permute-start(f32[1,96,256]{2,1,0:T(8,128)} %refs_0_.1), channel_id=1, source_target_pairs={{0,2},{1,3},{2,0},{3,1},{4,6},{5,7},{6,4},{7,5},{8,10},{9,11},{10,... | collective-permute-start | bytes 294920 | tf_op jit(solution)/shard_map/ppermute | solution.py:326
  13.5 26.3 %collective-permute-start.4 = (f32[1,96,256]{2,1,0:T(8,128)}, f32[1,96,256]{2,1,0:T(8,128)S(1)}, u32[]{:S(2)}, u32[]{:S(2)}) collective-permute-start(f32[1,96,256]{2,1,0:T(8,128)} %refs_0_.1), channel_id=1, source_target_pairs={{0,6},{1,7},{2,4},{3,5},{4,2},{5,3},{6,0},{7,1},{8,14},{9,15},{10,... | collective-permute-start | bytes 294920 | tf_op jit(solution)/shard_map/ppermute | solution.py:326
  20.2 20.1 %all-to-all-start.1 = ((f32[32,4,128]{2,1,0:T(4,128)}), f32[32,4,128]{2,1,0:T(4,128)S(1)}, u32[]{:S(2)}, u32[]{:S(2)}) async-start(f32[32,4,128]{2,1,0:T(4,128)} %get-tuple-element.21), calls=%async_computation.1 | async-start | bytes 131072 | tf_op jit(solution)/shard_map/all_to_all | solution.py:309
  30.6 7.1 %collective-permute-start = (f32[32,512]{1,0:T(8,128)S(1)}, f32[32,512]{1,0:T(8,128)S(1)}, u32[]{:S(2)}, u32[]{:S(2)}) collective-permute-start(f32[32,512]{1,0:T(8,128)S(1)} %get-tuple-element.22), channel_id=1, source_target_pairs={{0,8},{1,249},{2,10},{3,251},{4,12},{5,253},{6,14},{7,255},{8,0},{... | collective-permute-start | bytes 196616 | tf_op jit(solution)/shard_map/ppermute | solution.py:321
  35.3 1.9 %copy-start = (f32[1,256,3072]{2,1,0:T(8,128)S(1)}, f32[1,256,3072]{2,1,0:T(8,128)}, u32[]{:S(2)}) copy-start(f32[1,256,3072]{2,1,0:T(8,128)} %edge_ref.2) | copy-start | bytes 9437188
  37.2 1.9 %copy-start.1 = (f32[1,256,3072]{2,1,0:T(8,128)S(1)}, f32[1,256,3072]{2,1,0:T(8,128)}, u32[]{:S(2)}) copy-start(f32[1,256,3072]{2,1,0:T(8,128)} %edge_ref.2) | copy-start | bytes 9437188
  37.6 2.2 %copy-start.3 = (f32[1,96,256]{2,1,0:T(8,128)S(1)}, f32[1,96,256]{2,1,0:T(8,128)}, u32[]{:S(2)}) copy-start(f32[1,96,256]{2,1,0:T(8,128)} %refs_0_.1) | copy-start | bytes 294916
  37.6 2.1 %collective-permute-start.1 = (f32[32,512]{1,0:T(8,128)S(1)}, f32[32,512]{1,0:T(8,128)S(1)}, u32[]{:S(2)}, u32[]{:S(2)}) collective-permute-start(f32[32,512]{1,0:T(8,128)S(1)} %collective-permute-done.a_ref), channel_id=1, source_target_pairs={{0,1},{1,0},{2,3},{3,2},{4,5},{5,4},{6,7},{7,6},{8,9},{9,8},{10,11... | collective-permute-start | bytes 196616 | tf_op jit(solution)/shard_map/ppermute | solution.py:326
  40.2 13.4 %collective-permute-start.5 = (f32[4,96,256]{2,1,0:T(8,128)S(1)}, f32[4,96,256]{2,1,0:T(8,128)S(1)}, u32[]{:S(2)}, u32[]{:S(2)}) collective-permute-start(f32[4,96,256]{2,1,0:T(8,128)S(1)} %get-tuple-element.29.even_ref), channel_id=1, source_target_pairs={{0,1},{1,0},{2,3},{3,2},{4,5},{5,4},{6,7},{7,6},{8,9},{9,8},{10,11... | collective-permute-start | bytes 1179656 | tf_op jit(solution)/shard_map/ppermute | solution.py:326
  53.6 2.3 %copy-start.2 = (f32[1,256,3072]{2,1,0:T(8,128)S(1)}, f32[1,256,3072]{2,1,0:T(8,128)}, u32[]{:S(2)}) copy-start(f32[1,256,3072]{2,1,0:T(8,128)} %edge_ref.3) | copy-start | bytes 9437188
  54.2 6.5 %collective-permute-start.6 = (f32[32,512]{1,0:T(8,128)S(1)}, f32[32,512]{1,0:T(8,128)S(1)}, u32[]{:S(2)}, u32[]{:S(2)}) collective-permute-start(f32[32,512]{1,0:T(8,128)S(1)} %get-tuple-element.30), channel_id=1, source_target_pairs={{0,8},{1,249},{2,10},{3,251},{4,12},{5,253},{6,14},{7,255},{8,0},{... | collective-permute-start | bytes 196616 | tf_op jit(solution)/shard_map/ppermute | solution.py:321
  56.3 5.7 %copy-start.4 = (f32[32,1,256]{2,1,0:T(1,128)S(1)}, f32[32,1,256]{2,1,0:T(1,128)}, u32[]{:S(2)}) copy-start(f32[32,1,256]{2,1,0:T(1,128)} %res_ref.3) | copy-start | bytes 98308
  60.8 1.3 %collective-permute-start.7 = (f32[32,512]{1,0:T(8,128)S(1)}, f32[32,512]{1,0:T(8,128)S(1)}, u32[]{:S(2)}, u32[]{:S(2)}) collective-permute-start(f32[32,512]{1,0:T(8,128)S(1)} %collective-permute-done.6.a_ref), channel_id=1, source_target_pairs={{0,1},{1,0},{2,3},{3,2},{4,5},{5,4},{6,7},{7,6},{8,9},{9,8},{10,11... | collective-permute-start | bytes 196616 | tf_op jit(solution)/shard_map/ppermute | solution.py:326
  61.4 19.5 %copy-start.5 = (f32[32,1,256]{2,1,0:T(1,128)S(1)}, f32[32,1,256]{2,1,0:T(1,128)}, u32[]{:S(2)}) copy-start(f32[32,1,256]{2,1,0:T(1,128)} %iter_ref.1) | copy-start | bytes 98308
